TPU v7x, 256 devices: a whole 4x4x8 slice. The times are simulated.
256 devices in a mesh: region: 32 (over x, y, core), local: 8 (over z).
Axes of the slice: x: 4, y: 4, z: 8, core: 2. Of those that a mesh axis runs over, the one named last changes fastest.
Arguments:
- tokens: bfloat16 [4096, 7168], P('region', 'local'), may hold values from -44 to 44
- norm_gain: float32 [7168], P('local'), may hold values from 0.1 to 1.9
- w_gate: bfloat16 [32, 7168, 2048], P('region', None, 'local'), may hold values from -0.0625 to 0.0625
- w_up: bfloat16 [32, 7168, 2048], P('region', None, 'local'), may hold values from -0.0625 to 0.0625
- w_down: bfloat16 [32, 2048, 7168], P('region', 'local'), may hold values from -0.125 to 0.125
- regions: int32 [4096, 2], P('region'), may hold values from 0 to 31, all different within a row; in each aligned block of 128 rows (0 to 127, 128 to 255, ...) at most 10 rows name the same one
- combine: float32 [4096, 2], P('region'), may hold values from 0.1 to 1
- grad_out: bfloat16 [4096, 7168], P('region', 'local'), may hold values from -3 to 3
Outputs:
- moe_out: bfloat16 [4096, 7168], P('region', 'local')
- grad_tokens: bfloat16 [4096, 7168], P('region', 'local')
- grad_combine: float32 [4096, 2], P('region')
Inputs may be any that keep to these rules, and one draw needn't show every extreme that they name: `regions`: each row names 2 different experts; among the rows of one device (aligned blocks of 128 rows) no expert is named by more than 10 rows, a bound that some block reaches.
All inputs are finite; a program needn't handle non-finite values.
Results may differ from a plain program's by a relative error of at most 0.02.
Values may be sent and summed in bfloat16 or wider, within the bound.
No kernel may reach another device: no remote copies, remote signals or barrier semaphores. Data moves between devices by JAX's collectives and lax.ppermute only.
A program may use at most 128 MiB of HBM per device.

v0:
```python
import jax
import jax.numpy as jnp
from jax import lax
from jax.sharding import PartitionSpec as P

D = 7168


def on_device(tokens, norm_gain, w_gate, w_up, w_down, regions, combine, grad_out):
    inputs_f32 = tokens.astype(jnp.float32)
    token_count, width_local = inputs_f32.shape
    region_count = lax.axis_size("region")
    route_count = regions.shape[1]
    capacity = max(2, token_count * route_count * 5 // (4 * region_count))
    slot_total = region_count * capacity
    sum_squares = lax.psum(jnp.sum(inputs_f32 * inputs_f32, axis=1), "local")
    inv_rms = lax.rsqrt(sum_squares / D + 1e-06)[:, None]
    normed = (inputs_f32 * inv_rms * norm_gain).astype(jnp.bfloat16)
    flat_routes = regions.reshape(-1)
    one_hot = (flat_routes[:, None] == jnp.arange(region_count, dtype=jnp.int32)[None, :]).astype(
        jnp.int32
    )
    running = jnp.cumsum(one_hot, axis=0) - one_hot
    slot_index = jnp.sum(running * one_hot, axis=1)
    placement = flat_routes * capacity + slot_index
    owner = jnp.arange(token_count * route_count, dtype=jnp.int32) // route_count
    source = jnp.full((slot_total,), token_count, jnp.int32).at[placement].set(owner)

    def pack_rows(matrix):
        picked = jnp.take(matrix, source, axis=0, mode="fill", fill_value=0)
        return picked.reshape(region_count, capacity, matrix.shape[1])

    gate_w = w_gate[0]
    up_w = w_up[0]
    down_w = w_down[0]
    contract_last = (((1,), (1,)), ((), ()))
    normed_full, grad_full = (
        lax.all_gather(normed, "local", axis=1, tiled=True),
        lax.all_gather(grad_out, "local", axis=1, tiled=True),
    )
    sent_in, sent_grad = (
        lax.all_to_all(pack_rows(normed_full), "region", split_axis=0, concat_axis=0, tiled=True),
        lax.all_to_all(pack_rows(grad_full), "region", split_axis=0, concat_axis=0, tiled=True),
    )
    rows_in = sent_in.reshape(slot_total, D)
    rows_grad = sent_grad.reshape(slot_total, D)
    gate_pre = jnp.dot(rows_in, gate_w, preferred_element_type=jnp.float32)
    up_pre = jnp.dot(rows_in, up_w, preferred_element_type=jnp.float32)
    grad_hidden = lax.dot_general(
        rows_grad, down_w, contract_last, preferred_element_type=jnp.float32
    )
    sig_gate = jax.nn.sigmoid(gate_pre)
    act_gate = gate_pre * sig_gate
    hidden = (act_gate * up_pre).astype(jnp.bfloat16)
    grad_gate = (grad_hidden * up_pre * sig_gate * (1.0 + gate_pre * (1.0 - sig_gate))).astype(
        jnp.bfloat16
    )
    grad_up = (grad_hidden * act_gate).astype(jnp.bfloat16)
    expert_out = jnp.dot(hidden, down_w, preferred_element_type=jnp.float32)
    stacked_grads = jnp.concatenate((grad_gate, grad_up), axis=1)
    stacked_weights = jnp.concatenate((gate_w, up_w), axis=1)
    branch_grad = lax.dot_general(
        stacked_grads, stacked_weights, contract_last, preferred_element_type=jnp.float32
    )
    out_share, grad_share = (
        lax.psum_scatter(
            expert_out.astype(jnp.bfloat16), "local", scatter_dimension=1, tiled=True
        ).astype(jnp.float32),
        lax.psum_scatter(
            branch_grad.astype(jnp.bfloat16), "local", scatter_dimension=1, tiled=True
        ).astype(jnp.float32),
    )
    back_out, back_grad = (
        lax.all_to_all(
            out_share.reshape(region_count, capacity, width_local).astype(jnp.bfloat16),
            "region",
            split_axis=0,
            concat_axis=0,
            tiled=True,
        ).astype(jnp.float32),
        lax.all_to_all(
            grad_share.reshape(region_count, capacity, width_local).astype(jnp.bfloat16),
            "region",
            split_axis=0,
            concat_axis=0,
            tiled=True,
        ).astype(jnp.float32),
    )
    pick_index = placement.reshape(token_count, route_count)
    out_picked = back_out.reshape(slot_total, width_local)[pick_index]
    grad_picked = back_grad.reshape(slot_total, width_local)[pick_index]
    weights = combine[:, :, None]
    moe_out = jnp.sum(weights * out_picked, axis=1).astype(jnp.bfloat16)
    grad_normed = jnp.sum(weights * grad_picked, axis=1)
    scaled = norm_gain * grad_normed
    inner_part = jnp.sum(inputs_f32 * scaled, axis=1)
    comb_part = jnp.sum(grad_out.astype(jnp.float32)[:, None, :] * out_picked, axis=2)
    inner, grad_combine = lax.psum((inner_part, comb_part), "local")
    grad_tokens = (
        inv_rms * scaled - inputs_f32 * inv_rms * inv_rms * inv_rms * inner[:, None] / D
    ).astype(jnp.bfloat16)
    return (moe_out, grad_tokens, grad_combine)


def solution(mesh):
    placed = (
        P("region", "local"),
        P("local"),
        P("region", None, "local"),
        P("region", None, "local"),
        P("region", "local", None),
        P("region", None),
        P("region", None),
        P("region", "local"),
    )
    return jax.shard_map(
        on_device,
        mesh=mesh,
        in_specs=placed,
        out_specs=(P("region", "local"), P("region", "local"), P("region", None)),
        check_vma=False,
    )
```

profile of v0, /device:TPU:2, one launch (start us, length us, event | category | flops | bytes accessed | tf_op | source)
XLA Modules:
  0.0 603.6 jit_solution(289672054082005427)
XLA Ops:
  7.2 1.1 fusion.14
  8.3 20.0 %psum.21 = f32[128]{0:T(128)S(1)} all-reduce(f32[128]{0:T(128)S(1)} %fusion.14), channel_id=1, replica_groups=mesh['region'=32,'local'=8] {'local'}, use_global_device_ids=true, to_apply=%region_1.0 | all-reduce | flops 128 | bytes 1024 | tf_op jit(solution)/shard_map/psum | solution.py:16
  28.3 1.8 fusion.8
  30.1 0.7 all-gather.5.cloned.1.call-update
  30.8 0.8 copy.18
  31.9 0.6 reduce-window.6
  32.5 0.2 slice_reduce_fusion
  33.2 1.4 scatter_custom_fusion
  34.6 34.6 %all-gather.3.cloned.1.call-done = bf16[128,7168]{1,0:T(8,128)(2,1)} async-done(((bf16[128,896]{1,0:T(8,128)(2,1)}), bf16[128,7168]{1,0:T(8,128)(2,1)}) %all-gather.3.cloned.1.call-update) | async-done | bytes 1835024 | tf_op jit(solution)/shard_map/all_gather | solution.py:38
  69.2 14.7 %gather_fusion.2 = bf16[320,7168]{1,0:T(8,128)(2,1)} fusion(bf16[128,7168]{1,0:T(8,128)(2,1)} %all-gather.3.cloned.1.call-done, s32[1024]{0:T(1024)S(1)} %pad_clamp_fusion.1), kind=kCustom, calls=%fused_computation.clone | custom fusion | bytes 9176320 | tf_op jit(solution)/shard_map/jit(_take)/gather | solution.py:30
  83.9 26.3 %all-gather.5.cloned.1.call-done = bf16[128,7168]{1,0:T(8,128)(2,1)} async-done(((bf16[128,896]{1,0:T(8,128)(2,1)}), bf16[128,7168]{1,0:T(8,128)(2,1)}) %all-gather.5.cloned.1.call-update) | async-done | bytes 1835024 | tf_op jit(solution)/shard_map/all_gather | solution.py:39
  110.2 14.8 %gather_fusion.3 = bf16[320,7168]{1,0:T(8,128)(2,1)} fusion(bf16[128,7168]{1,0:T(8,128)(2,1)} %all-gather.5.cloned.1.call-done, s32[1024]{0:T(1024)S(1)} %pad_clamp_fusion.1), kind=kCustom, calls=%fused_computation.1.clone | custom fusion | bytes 9176320 | tf_op jit(solution)/shard_map/jit(_take)/gather | solution.py:30
  125.0 7.8 %broadcast_select_fusion = (bf16[320,7168]{1,0:T(8,128)(2,1)}, bf16[320,7168]{1,0:T(8,128)(2,1)}) fusion(bf16[320,7168]{1,0:T(8,128)(2,1)} %gather_fusion.3, pred[320]{0:T(512)(128)(4,1)S(1)} %compare_and_fusion, bf16[320,7168]{1,0:T(8,128)(2,1)} %gather_fusion.2), kind=kLoop, calls=%fused_computation.10 | loop fusion | flops 4587520 | bytes 18350400 | tf_op jit(solution)/shard_map/jit(_take)/select_n | solution.py:30
  132.8 7.8 %reshape.93 = bf16[32,10,7168]{2,1,0:T(8,128)(2,1)} reshape(bf16[320,7168]{1,0:T(8,128)(2,1)} %get-tuple-element.17) | data formatting | bytes 9175040 | tf_op jit(solution)/shard_map/reshape | solution.py:31
  140.6 7.5 %all-to-all-start = ((bf16[32,10,7168]{2,1,0:T(8,128)(2,1)}), bf16[32,10,7168]{2,1,0:T(8,128)(2,1)}, u32[]{:S(2)}, u32[]{:S(2)}) async-start(bf16[32,10,7168]{2,1,0:T(8,128)(2,1)} %reshape.93), calls=%async_computation | async-start | bytes 14680064 | tf_op jit(solution)/shard_map/all_to_all | solution.py:42
  148.1 7.8 %reshape.97 = bf16[32,10,7168]{2,1,0:T(8,128)(2,1)} reshape(bf16[320,7168]{1,0:T(8,128)(2,1)} %get-tuple-element.16) | data formatting | bytes 9175040 | tf_op jit(solution)/shard_map/reshape | solution.py:31
  155.9 82.8 %all-to-all-done = bf16[32,10,7168]{2,1,0:T(8,128)(2,1)} async-done(((bf16[32,10,7168]{2,1,0:T(8,128)(2,1)}), bf16[32,10,7168]{2,1,0:T(8,128)(2,1)}, u32[]{:S(2)}, u32[]{:S(2)}) %all-to-all-start) | async-done | bytes 4587552 | tf_op jit(solution)/shard_map/all_to_all | solution.py:42
  238.7 25.1 %all-to-all-start.2 = ((bf16[32,10,7168]{2,1,0:T(8,128)(2,1)}), bf16[32,10,7168]{2,1,0:T(8,128)(2,1)}, u32[]{:S(2)}, u32[]{:S(2)}) async-start(bf16[32,10,7168]{2,1,0:T(8,128)(2,1)} %reshape.97), calls=%async_computation.2 | async-start | bytes 14680064 | tf_op jit(solution)/shard_map/all_to_all | solution.py:43
  263.9 8.2 %reshape.94 = bf16[320,7168]{1,0:T(8,128)(2,1)} reshape(bf16[32,10,7168]{2,1,0:T(8,128)(2,1)} %all-to-all-done) | data formatting | bytes 9175040 | tf_op jit(solution)/shard_map/reshape | solution.py:45
  272.1 4.8 fusion.28
  276.9 77.5 %all-to-all-done.2 = bf16[32,10,7168]{2,1,0:T(8,128)(2,1)} async-done(((bf16[32,10,7168]{2,1,0:T(8,128)(2,1)}), bf16[32,10,7168]{2,1,0:T(8,128)(2,1)}, u32[]{:S(2)}, u32[]{:S(2)}) %all-to-all-start.2) | async-done | bytes 4587552 | tf_op jit(solution)/shard_map/all_to_all | solution.py:43
  354.4 8.1 %reshape.98 = bf16[320,7168]{1,0:T(8,128)(2,1)} reshape(bf16[32,10,7168]{2,1,0:T(8,128)(2,1)} %all-to-all-done.2) | data formatting | bytes 9175040 | tf_op jit(solution)/shard_map/reshape | solution.py:46
  362.4 5.0 fusion.3
  367.4 0.9 copy-done.6
  368.3 1.5 multiply_convert_fusion.1
  369.8 0.6 copy-done.5
  370.3 4.3 convolution_convert_fusion
  374.6 7.6 %copy.25 = bf16[320,7168]{0,1:T(8,128)(2,1)} copy(bf16[320,7168]{1,0:T(8,128)(2,1)} %convolution_convert_fusion) | data formatting | bytes 9175040
  382.2 5.6 convolution_convert_fusion.1
  387.8 7.5 %copy.23 = bf16[320,7168]{0,1:T(8,128)(2,1)} copy(bf16[320,7168]{1,0:T(8,128)(2,1)} %convolution_convert_fusion.1) | data formatting | bytes 9175040
  395.4 70.5 %reduce-scatter.9.cloned.1.call-done = bf16[896,320]{1,0:T(8,128)(2,1)} async-done(((bf16[7168,320]{1,0:T(8,128)(2,1)}), bf16[896,320]{1,0:T(8,128)(2,1)}) %reduce-scatter.9.cloned.1.call-update) | async-done | bytes 573456
  465.9 1.4 copy.26
  467.4 1.2 convert_element_type.60
  468.5 7.4 %all-to-all-start.3 = ((bf16[32,10,896]{2,1,0:T(8,128)(2,1)}), bf16[32,10,896]{2,1,0:T(8,128)(2,1)S(1)}, u32[]{:S(2)}, u32[]{:S(2)}) async-start(bf16[32,10,896]{2,1,0:T(8,128)(2,1)} %convert_element_type.60), calls=%async_computation.3 | async-start | bytes 1835008 | tf_op jit(solution)/shard_map/all_to_all | solution.py:81
  475.9 58.7 %reduce-scatter.7.cloned.1.call-done = bf16[896,320]{1,0:T(8,128)(2,1)} async-done(((bf16[7168,320]{1,0:T(8,128)(2,1)}), bf16[896,320]{1,0:T(8,128)(2,1)}) %reduce-scatter.7.cloned.1.call-update) | async-done | bytes 573456
  534.7 1.4 copy.24
  536.1 1.1 convert_element_type.55
  537.2 7.4 %all-to-all-start.1 = ((bf16[32,10,896]{2,1,0:T(8,128)(2,1)}), bf16[32,10,896]{2,1,0:T(8,128)(2,1)S(1)}, u32[]{:S(2)}, u32[]{:S(2)}) async-start(bf16[32,10,896]{2,1,0:T(8,128)(2,1)} %convert_element_type.55), calls=%async_computation.1 | async-start | bytes 1835008 | tf_op jit(solution)/shard_map/all_to_all | solution.py:74
  544.6 0.8 convert_element_type.62
  545.9 2.1 gather_fusion.1
  548.0 1.7 reshape.130
  549.7 8.1 %all-to-all-done.1 = bf16[32,10,896]{2,1,0:T(8,128)(2,1)S(1)} async-done(((bf16[32,10,896]{2,1,0:T(8,128)(2,1)}), bf16[32,10,896]{2,1,0:T(8,128)(2,1)S(1)}, u32[]{:S(2)}, u32[]{:S(2)}) %all-to-all-start.1) | async-done | bytes 573472 | tf_op jit(solution)/shard_map/all_to_all | solution.py:74
  558.0 2.0 gather_fusion
  560.0 1.7 reshape.122
  561.7 4.5 multiply_reduce_fusion
  566.4 29.2 %all-reduce = (f32[128]{0:T(128)S(1)}, f32[128,2]{1,0:T(8,128)S(1)}) all-reduce(f32[128]{0:T(128)S(1)} %fusion.15, f32[128,2]{1,0:T(8,128)S(1)} %get-tuple-element.7), channel_id=1, replica_groups=mesh['region'=32,'local'=8] {'local'}, use_global_device_ids=true, to_apply=%region_11.13 | all-reduce | flops 384 | bytes 3072 | tf_op jit(solution)/shard_map/psum | solution.py:98
  595.6 0.9 fusion.13
  596.5 0.6 copy.22
  (41 shorter events, 1.8 us)
Async XLA Ops:
  7.2 62.1 %all-gather.3.cloned.1.call-start = ((), (), s32[]{:S(2)}) async-start(), calls=%async_computation.6 | async-start | bytes 2064384 | tf_op jit(solution)/shard_map/all_gather | solution.py:38
  30.1 80.1 %all-gather.5.cloned.1.call-start = ((), (), s32[]{:S(2)}) async-start(), calls=%async_computation.7 | async-start | bytes 2064384 | tf_op jit(solution)/shard_map/all_gather | solution.py:39
  140.6 98.0 %all-to-all-start = ((bf16[32,10,7168]{2,1,0:T(8,128)(2,1)}), bf16[32,10,7168]{2,1,0:T(8,128)(2,1)}, u32[]{:S(2)}, u32[]{:S(2)}) async-start(bf16[32,10,7168]{2,1,0:T(8,128)(2,1)} %reshape.93), calls=%async_computation | async-start | bytes 14680064 | tf_op jit(solution)/shard_map/all_to_all | solution.py:42
  238.7 115.7 %all-to-all-start.2 = ((bf16[32,10,7168]{2,1,0:T(8,128)(2,1)}), bf16[32,10,7168]{2,1,0:T(8,128)(2,1)}, u32[]{:S(2)}, u32[]{:S(2)}) async-start(bf16[32,10,7168]{2,1,0:T(8,128)(2,1)} %reshape.97), calls=%async_computation.2 | async-start | bytes 14680064 | tf_op jit(solution)/shard_map/all_to_all | solution.py:43
  263.8 202.1 %reduce-scatter.9.cloned.1.call-start = ((), (), s32[]{:S(2)}) async-start(), calls=%async_computation.9 | async-start | bytes 6193152
  362.4 5.0 copy-start
  362.4 5.9 copy-start.6
  368.3 2.0 copy-start.5
  382.2 152.5 %reduce-scatter.7.cloned.1.call-start = ((), (), s32[]{:S(2)}) async-start(), calls=%async_computation.8 | async-start | bytes 6193152
  465.9 78.7 %copy-start.2 = (bf16[128,896]{1,0:T(8,128)(2,1)S(1)}, bf16[128,896]{1,0:T(8,128)(2,1)}, u32[]{:S(2)}) copy-start(bf16[128,896]{1,0:T(8,128)(2,1)} %param.17) | copy-start | bytes 688132
  467.3 78.2 %copy-start.4 = (f32[128,2]{0,1:T(2,128)S(1)}, f32[128,2]{0,1:T(2,128)}, u32[]{:S(2)}) copy-start(f32[128,2]{0,1:T(2,128)} %param.16) | copy-start | bytes 3076
  468.5 68.7 %all-to-all-start.3 = ((bf16[32,10,896]{2,1,0:T(8,128)(2,1)}), bf16[32,10,896]{2,1,0:T(8,128)(2,1)S(1)}, u32[]{:S(2)}, u32[]{:S(2)}) async-start(bf16[32,10,896]{2,1,0:T(8,128)(2,1)} %convert_element_type.60), calls=%async_computation.3 | async-start | bytes 1835008 | tf_op jit(solution)/shard_map/all_to_all | solution.py:81
  537.2 20.6 %all-to-all-start.1 = ((bf16[32,10,896]{2,1,0:T(8,128)(2,1)}), bf16[32,10,896]{2,1,0:T(8,128)(2,1)S(1)}, u32[]{:S(2)}, u32[]{:S(2)}) async-start(bf16[32,10,896]{2,1,0:T(8,128)(2,1)} %convert_element_type.55), calls=%async_computation.1 | async-start | bytes 1835008 | tf_op jit(solution)/shard_map/all_to_all | solution.py:74
  557.9 8.3 %copy-start.1 = (bf16[128,896]{1,0:T(8,128)(2,1)S(1)}, bf16[128,896]{1,0:T(8,128)(2,1)}, u32[]{:S(2)}) copy-start(bf16[128,896]{1,0:T(8,128)(2,1)} %param.10) | copy-start | bytes 688132
  558.0 8.3 %copy-start.3 = (f32[896]{0:T(1024)S(1)}, f32[896]{0:T(1024)}, u32[]{:S(2)}) copy-start(f32[896]{0:T(1024)} %param.11) | copy-start | bytes 10756
Sparse Core Ops, SparseCore 0:
  30.2 39.0 all-gather.2
  71.0 39.1 all-gather.4
  382.3 83.5 reduce-scatter.8
  468.3 66.2 reduce-scatter.6
where the time goes:
time: 606 us; the launch traced here: 604 us
  waiting for transfers between devices  359 us (59%)
  local copies, waits for them, and re-layouts  94.7 us (16%)
  blocking collectives  49.2 us (8%)
  starting transfers between devices  47.6 us (8%)
  matrix products  21 us (3%)
  other arithmetic  17.8 us (3%)
  between operations  14 us (2%)
    unnamed x6, waiting for transfers between devices  130 us
    all_to_all x1, waiting for transfers between devices, on_device(): lax.all_to_all(pack_rows(normed_full), 'region', split_axis=0, concat_axi...  82.8 us
    all_to_all x1, waiting for transfers between devices, on_device(): lax.all_to_all(pack_rows(grad_full), 'region', split_axis=0, concat_axis=...  77.5 us
    all_gather x1, waiting for transfers between devices, on_device(): lax.all_gather(normed, 'local', axis=1, tiled=True)  34.6 us
    gather x2, local copies, waits for them, and re-layouts, pack_rows(): picked = jnp.take(matrix, source, axis=0, mode='fill', fill_value=0)  29.5 us
    psum x1, blocking collectives, on_device(): inner, grad_combine = lax.psum((inner_part, comb_part), 'local')  29.2 us
    all_gather x1, waiting for transfers between devices, on_device(): lax.all_gather(grad_out, 'local', axis=1, tiled=True)  26.3 us
    all_to_all x1, starting transfers between devices, on_device(): lax.all_to_all(pack_rows(grad_full), 'region', split_axis=0, concat_axis=...  25.1 us
  transfers between devices with their start and end apart: 8, of which 7 were waited for; matrix products, arithmetic and copies ran while one was open for 10% of the time, Pallas kernels for 0%

commit v1 on v0

v1 whole, which is shorter than its diff:
```python
import functools

import jax
import jax.numpy as jnp
from jax import lax
from jax.experimental import pallas as pl
from jax.experimental.pallas import tpu as pltpu
from jax.sharding import PartitionSpec as P

BF = jnp.bfloat16
F32 = jnp.float32
NT = (((1,), (1,)), ((), ()))
TN = (((0,), (0,)), ((), ()))
VMEM_LIMIT = 48 * 1024 * 1024


def fold_lanes(width):
    return 128 * -(-width // 256)


def packed_lanes(width):
    return 2 * width + fold_lanes(width)


def dot(a, b, dims=(((1,), (0,)), ((), ())), precision=None):
    return lax.dot_general(a, b, dims, precision=precision, preferred_element_type=F32)


def params(**kw):
    return pltpu.CompilerParams(vmem_limit_bytes=VMEM_LIMIT, **kw)


def fold_matrix(regions):
    rows = 8 * regions
    i = lax.broadcasted_iota(jnp.int32, (rows, rows), 0)
    j = lax.broadcasted_iota(jnp.int32, (rows, rows), 1)
    return (j == 4 * (i % (2 * regions)) + i // (2 * regions)).astype(BF)


def encode(main, rest, fold):
    width = main.shape[1] // 2
    lanes = fold_lanes(width)
    pad = 2 * lanes - width
    parts = []
    for side in range(2):
        parts.append(rest[:, side * width : side * width + lanes])
        tail = rest[:, side * width + lanes : (side + 1) * width]
        if pad:
            tail = jnp.concatenate([tail, jnp.zeros((rest.shape[0], pad), rest.dtype)], axis=1)
        parts.append(tail)
    stacked = jnp.concatenate(parts, axis=0)
    return jnp.concatenate([main, dot(fold, stacked, TN).astype(BF)], axis=1)


def decode(block, width, fold):
    lanes = fold_lanes(width)
    rows = block.shape[0]
    rest = dot(fold, block[:, 2 * width :]).astype(BF)
    few = rows // 4
    sides = []
    for side in range(2):
        head = rest[(2 * side) * few : (2 * side + 1) * few]
        tail = rest[(2 * side + 1) * few : (2 * side + 2) * few, : width - lanes]
        low = jnp.concatenate([head, tail], axis=1)
        sides.append(jnp.concatenate([block[:, side * width : (side + 1) * width], low], axis=0))
    return sides


def slot_ids(regions, tokens):
    s = lax.broadcasted_iota(jnp.int32, (10 * regions, tokens), 0)
    late = s - 8 * regions
    expert = jnp.where(late < 0, s // 8, late // 2)
    slot = jnp.where(late < 0, s % 8, 8 + late % 2)
    return expert, slot


def ranks(named):
    count = named.shape[1]
    before = lax.broadcasted_iota(jnp.int32, (count, count), 0)
    after = lax.broadcasted_iota(jnp.int32, (count, count), 1)
    return dot(named.astype(F32).astype(BF), (before < after).astype(F32).astype(BF))


def placed(routes, regions):
    expert, slot = slot_ids(regions, routes.shape[1])
    named = [routes[k : k + 1, :] == expert for k in range(2)]
    at = ranks(named[0] | named[1]) == slot.astype(F32)
    return [n & at for n in named]


def placed_packed(routes, regions):
    s = lax.broadcasted_iota(jnp.int32, (8 * regions, routes.shape[1]), 0)
    expert = s // 8
    named = [routes[k : k + 1, :] == expert for k in range(2)]
    rank = ranks(named[0] | named[1])
    main = rank == (s % 8).astype(F32)
    late = (rank == (8 + (s % 8) // 4).astype(F32)) & (s % 4 == 0)
    return [n & main for n in named], [n & late for n in named]


def pack_kernel(regions, tok, gain, grad, routes, out):
    at = placed(routes[...], regions)
    pick = (at[0] | at[1]).astype(F32).astype(BF)
    scaled = (tok[...].astype(F32) * gain[...]).astype(BF)
    rows = dot(pick, jnp.concatenate([scaled, grad[...]], axis=1)).astype(BF)
    cut = 8 * regions
    out[...] = encode(rows[:cut], rows[cut:], fold_matrix(regions))


def pack(tok, gain, grad, routes, regions):
    width = tok.shape[1]
    return pl.pallas_call(
        functools.partial(pack_kernel, regions),
        out_shape=jax.ShapeDtypeStruct((8 * regions, packed_lanes(width)), BF),
        compiler_params=params(),
    )(tok, gain, grad, routes)


def inverse(squares, full):
    return lax.rsqrt(jnp.sum(squares, axis=0, keepdims=True) / full + 1e-06)


def spread_kernel(regions, full, squares, routes, out):
    inv = inverse(squares[...], full)
    main, late = placed_packed(routes[...], regions)
    lane = lax.broadcasted_iota(jnp.int32, out.shape, 1)
    first = jnp.sum(jnp.where(main[0] | main[1], inv, 0.0), axis=1, keepdims=True)
    second = jnp.sum(jnp.where(late[0] | late[1], inv, 0.0), axis=1, keepdims=True)
    out[...] = jnp.where(lane == 0, first, jnp.where(lane == 1, second, 0.0))


def spread(squares, routes, regions, full):
    return pl.pallas_call(
        functools.partial(spread_kernel, regions, full),
        out_shape=jax.ShapeDtypeStruct((8 * regions, 128), F32),
        compiler_params=params(),
    )(squares, routes)


def hidden_kernel(regions, width, scales, block, gate_w, up_w, down_w, hid_out, gate_out, up_out, scal_out, acc_g, acc_u, acc_h):
    step = pl.program_id(0)
    fold = fold_matrix(regions)

    @pl.when(step == 0)
    def _():
        acc_g[...] = jnp.zeros_like(acc_g)
        acc_u[...] = jnp.zeros_like(acc_u)
        acc_h[...] = jnp.zeros_like(acc_h)

    rows_in, rows_grad = decode(block[0], width, fold)
    acc_g[...] += dot(rows_in, gate_w[0])
    acc_u[...] += dot(rows_in, up_w[0])
    acc_h[...] += dot(rows_grad, down_w[0], NT)

    @pl.when(step == pl.num_programs(0) - 1)
    def _():
        cut = 8 * regions
        i = lax.broadcasted_iota(jnp.int32, (2 * regions, cut), 0)
        j = lax.broadcasted_iota(jnp.int32, (2 * regions, cut), 1)
        low = dot((j == 4 * i).astype(F32), scales[...], precision=lax.Precision.HIGHEST)
        inv = jnp.concatenate([scales[:, 0:1], low[:, 1:2]], axis=0)
        gate_raw, up_raw, grad_hidden = acc_g[...], acc_u[...], acc_h[...]
        gate_pre, up_pre = gate_raw * inv, up_raw * inv
        sig = jax.nn.sigmoid(gate_pre)
        act = gate_pre * sig
        hidden = (act * up_pre).astype(BF)
        grad_gate = (grad_hidden * up_pre * sig * (1.0 + gate_pre * (1.0 - sig))).astype(BF)
        grad_up = (grad_hidden * act).astype(BF)
        hid_out[...] = hidden
        gate_out[...] = grad_gate
        up_out[...] = grad_up
        comb = jnp.sum(hidden.astype(F32) * grad_hidden, axis=1, keepdims=True)
        inner = jnp.sum(grad_gate.astype(F32) * gate_raw + grad_up.astype(F32) * up_raw, axis=1, keepdims=True)
        lane = lax.broadcasted_iota(jnp.int32, (cut, 128), 1)
        lane_low = lax.broadcasted_iota(jnp.int32, (2 * regions, 128), 1)
        main = jnp.where(lane == 0, comb[:cut], jnp.where(lane == 1, inner[:cut], 0.0))
        rest = jnp.where(lane_low == 2, comb[cut:], jnp.where(lane_low == 3, inner[cut:], 0.0))
        a = lax.broadcasted_iota(jnp.int32, (cut, 2 * regions), 0)
        b = lax.broadcasted_iota(jnp.int32, (cut, 2 * regions), 1)
        scal_out[...] = main + dot((a == 4 * b).astype(F32), rest, precision=lax.Precision.HIGHEST)


def hidden_part(scales, blocks, gate_w, up_w, down_w, regions):
    count, rows, lanes = blocks.shape
    width = gate_w.shape[1] // count
    units = gate_w.shape[2]
    total = 10 * regions
    whole = lambda shape: pl.BlockSpec(shape, lambda z: (0,) * len(shape))
    return pl.pallas_call(
        functools.partial(hidden_kernel, regions, width),
        grid=(count,),
        in_specs=[
            whole((rows, 128)),
            pl.BlockSpec((1, rows, lanes), lambda z: (z, 0, 0)),
            pl.BlockSpec((1, width, units), lambda z: (0, z, 0)),
            pl.BlockSpec((1, width, units), lambda z: (0, z, 0)),
            pl.BlockSpec((1, units, width), lambda z: (0, 0, z)),
        ],
        out_specs=[whole((total, units))] * 3 + [whole((rows, 128))],
        out_shape=[jax.ShapeDtypeStruct((total, units), BF)] * 3 + [jax.ShapeDtypeStruct((rows, 128), F32)],
        scratch_shapes=[pltpu.VMEM((total, units), F32)] * 3,
        compiler_params=params(),
    )(scales, blocks, gate_w, up_w, down_w)


def back_kernel(regions, hid, gate_g, up_g, gate_w, up_w, down_w, out):
    moe = dot(hid[...], down_w[0]).astype(BF)
    grad = (dot(gate_g[...], gate_w[0], NT) + dot(up_g[...], up_w[0], NT)).astype(BF)
    both = jnp.concatenate([moe, grad], axis=1)
    cut = 8 * regions
    out[0] = encode(both[:cut], both[cut:], fold_matrix(regions))


def back_part(hid, gate_g, up_g, gate_w, up_w, down_w, regions, count):
    width = gate_w.shape[1] // count
    units = gate_w.shape[2]
    total = 10 * regions
    lanes = packed_lanes(width)
    rows = 8 * regions
    whole = lambda shape: pl.BlockSpec(shape, lambda z: (0,) * len(shape))
    return pl.pallas_call(
        functools.partial(back_kernel, regions),
        grid=(count,),
        in_specs=[whole((total, units))] * 3
        + [
            pl.BlockSpec((1, width, units), lambda z: (0, z, 0)),
            pl.BlockSpec((1, width, units), lambda z: (0, z, 0)),
            pl.BlockSpec((1, units, width), lambda z: (0, 0, z)),
        ],
        out_specs=pl.BlockSpec((1, rows, lanes), lambda z: (z, 0, 0)),
        out_shape=jax.ShapeDtypeStruct((count, rows, lanes), BF),
        compiler_params=params(),
    )(hid, gate_g, up_g, gate_w, up_w, down_w)


def scalars_kernel(regions, scal, routes, weights, out):
    main, late = placed_packed(routes[...], regions)
    here = scal[...]
    parts = []
    inner = 0.0
    for k in range(2):
        comb = jnp.where(main[k], here[:, 0:1], 0.0) + jnp.where(late[k], here[:, 2:3], 0.0)
        part = jnp.where(main[k], here[:, 1:2], 0.0) + jnp.where(late[k], here[:, 3:4], 0.0)
        parts.append(jnp.sum(comb, axis=0, keepdims=True))
        inner = inner + weights[k : k + 1, :] * jnp.sum(part, axis=0, keepdims=True)
    row = lax.broadcasted_iota(jnp.int32, out.shape, 0)
    out[...] = jnp.where(row == 0, parts[0], jnp.where(row == 1, parts[1], jnp.where(row == 2, inner, 0.0)))


def scalars(scal, routes, weights, regions):
    return pl.pallas_call(
        functools.partial(scalars_kernel, regions),
        out_shape=jax.ShapeDtypeStruct((8, routes.shape[1]), F32),
        compiler_params=params(),
    )(scal, routes, weights)


def combine_rows(block, width, routes, weights, regions):
    at = placed(routes, regions)
    weight = jnp.where(at[0], weights[0:1, :], 0.0) + jnp.where(at[1], weights[1:2, :], 0.0)
    high = weight.astype(BF)
    low = (weight - high.astype(F32)).astype(BF)
    return [dot(high, rows, TN) + dot(low, rows, TN) for rows in decode(block, width, fold_matrix(regions))]


def final_kernel(regions, full, back, tok, gain, squares, sums, routes, weights, moe_out, grad_out, comb_out):
    width = tok.shape[1]
    moe, grad = combine_rows(back[...], width, routes[...], weights[...], regions)
    moe_out[...] = moe.astype(BF)
    total = jnp.sum(sums[...], axis=0)
    comb_out[...] = total[0:2]
    inv_row = inverse(squares[...], full)
    row = lax.broadcasted_iota(jnp.int32, total.shape, 0)
    columns = jnp.transpose(jnp.where(row == 3, inv_row, total))
    inner, inv = columns[:, 2:3], columns[:, 3:4]
    scaled = gain[...] * grad
    grad_out[...] = (inv * scaled - tok[...].astype(F32) * (inv * inv * inv * inner / full)).astype(BF)


def final(back, tok, gain, squares, sums, routes, weights, regions, full):
    count, width = tok.shape
    return pl.pallas_call(
        functools.partial(final_kernel, regions, full),
        out_shape=[
            jax.ShapeDtypeStruct((count, width), BF),
            jax.ShapeDtypeStruct((count, width), BF),
            jax.ShapeDtypeStruct((2, count), F32),
        ],
        compiler_params=params(),
    )(back, tok, gain, squares, sums, routes, weights)


def swap(array, regions):
    split = array.reshape(regions, 8, array.shape[1])
    moved = lax.all_to_all(split, "region", split_axis=0, concat_axis=0, tiled=True)
    return moved.reshape(array.shape)


def on_device(tokens, norm_gain, w_gate, w_up, w_down, routes, combine, grad_out):
    regions = lax.axis_size("region")
    depth = lax.axis_size("local")
    full = depth * tokens.shape[1]
    gain = norm_gain.reshape(1, -1)
    routes, weights = routes.T, combine.T
    wide = tokens.astype(F32)
    packed = pack(tokens, gain, grad_out, routes, regions)
    squares = lax.all_gather(jnp.sum(wide * wide, axis=1), "local")
    rows = swap(packed, regions)
    scales = swap(spread(squares, routes, regions, full), regions)
    blocks = lax.all_gather(rows, "local")
    hid, gate_g, up_g, scal = hidden_part(scales, blocks, w_gate, w_up, w_down, regions)
    sums = lax.all_gather(scalars(swap(scal, regions), routes, weights, regions), "local")
    partial = back_part(hid, gate_g, up_g, w_gate, w_up, w_down, regions, depth)
    summed = lax.psum_scatter(partial, "local", scatter_dimension=0)
    back = swap(summed, regions)
    moe, grad, comb = final(back, tokens, gain, squares, sums, routes, weights, regions, full)
    return moe, grad, comb.T


def solution(mesh):
    specs = (
        P("region", "local"),
        P("local"),
        P("region", None, "local"),
        P("region", None, "local"),
        P("region", "local", None),
        P("region", None),
        P("region", None),
        P("region", "local"),
    )
    return jax.shard_map(
        on_device,
        mesh=mesh,
        in_specs=specs,
        out_specs=(P("region", "local"), P("region", "local"), P("region", None)),
        check_vma=False,
    )
```

time: 606 us -> 311 us (0.51)
  waiting for transfers between devices: 359 us -> 163 us
  local copies, waits for them, and re-layouts: 94.7 us -> 5.3 us
  blocking collectives: 49.2 us -> 94 us
  starting transfers between devices: 47.6 us -> 7.49 us
  Pallas kernels: 0 us -> 26.4 us
  matrix products: 21 us -> 0 us
  other arithmetic: 17.8 us -> 0.13 us
    all_to_all x4 -> x1, waiting for transfers between devices: 168 us -> 0.01 us  [swap(): lax.all_to_all(split, 'region', split_axis=0, concat_axis=0, tiled=True)]
    unnamed x6 -> x2, waiting for transfers between devices: 130 us -> 0.03 us
    reduce_scatter x0 -> x1, waiting for transfers between devices: none -> 89.7 us  [on_device(): summed = lax.psum_scatter(partial, 'local', scatter_dimension=0)]
    all_to_all x0 -> x3, blocking collectives: none -> 50.5 us  [swap(): lax.all_to_all(split, 'region', split_axis=0, concat_axis=0, tiled=True)]
    psum x2 -> x0, blocking collectives: 49.2 us -> none  [the longest x1 29.2 us: on_device(): inner, grad_combine = lax.psum((inner_part, comb_part), 'local')]
    all_gather x0 -> x2, blocking collectives: none -> 43.5 us  [the longest x1 24.5 us: on_device(): lax.all_gather(scalars(swap(scal, regions), routes, weights, regions), 'l...]
    all_to_all x4 -> x1, starting transfers between devices: 47.5 us -> 7.41 us  [swap(): lax.all_to_all(split, 'region', split_axis=0, concat_axis=0, tiled=True)]
    gather x6 -> x0, local copies, waits for them, and re-layouts: 37 us -> none  [the longest x2 29.5 us: pack_rows(): picked = jnp.take(matrix, source, axis=0, mode='fill', fill_value=0)]
  transfers between devices with their start and end apart: 8 -> 3, of which waited for: 7 -> 2; matrix products, arithmetic and copies ran while one was open for 10% -> 0% of each run, Pallas kernels for 0% -> 0%
where the time goes in v1:
time: 311 us
  waiting for transfers between devices  163 us (52%)
  blocking collectives  94 us (30%)
  Pallas kernels  26.4 us (8%)
  between operations  14.1 us (5%)
  starting transfers between devices  7.49 us (2%)
  local copies, waits for them, and re-layouts  5.3 us (2%)
    reduce_scatter x1, waiting for transfers between devices, on_device(): summed = lax.psum_scatter(partial, 'local', scatter_dimension=0)  89.7 us
    all_gather x1, waiting for transfers between devices, on_device(): blocks = lax.all_gather(rows, 'local')  73.4 us
    all_to_all x3, blocking collectives, swap(): lax.all_to_all(split, 'region', split_axis=0, concat_axis=0, tiled=True)  50.5 us
    all_gather x1, blocking collectives, on_device(): lax.all_gather(scalars(swap(scal, regions), routes, weights, regions), 'l...  24.5 us
    all_gather x1, blocking collectives, on_device(): squares = lax.all_gather(jnp.sum(wide * wide, axis=1), 'local')  19 us
    pallas_call x1, Pallas kernels, back_part(): pl.pallas_call(functools.partial(back_kernel, regions), grid=(count,), in...  11.7 us
    pallas_call x1, Pallas kernels, hidden_part(): pl.pallas_call(functools.partial(hidden_kernel, regions, width), grid=(co...  11.6 us
    all_to_all x1, starting transfers between devices, swap(): lax.all_to_all(split, 'region', split_axis=0, concat_axis=0, tiled=True)  7.41 us
  transfers between devices with their start and end apart: 3, of which 2 were waited for; matrix products, arithmetic and copies ran while one was open for 0% of the time, Pallas kernels for 0%

profile of v1, /device:TPU:2, one launch (start us, length us, event | category | flops | bytes accessed | tf_op | source)
XLA Modules:
  0.0 310.6 jit_solution(11331499676352660138)
XLA Ops:
  7.2 0.0 copy-start.6
  7.2 0.0 all-gather.5.cloned.1.call-start
  7.2 0.7 reshape.29.gain
  7.9 0.0 copy-start.2
  7.9 0.9 copy-done.2
  8.9 0.0 copy-start.4
  8.9 0.9 copy-done.4
  9.8 0.0 copy-start.5
  9.8 0.7 copy-done.5
  10.5 0.0 copy-start.3
  10.5 0.8 shard_map.104
  11.3 25.4 %all_to_all.20 = bf16[32,8,2304]{2,1,0:T(8,128)(2,1)} all-to-all(bf16[32,8,2304]{2,1,0:T(8,128)(2,1)S(1)} %bitcast.15), channel_id=1, replica_groups=mesh['region'=32,'local'=8] {'region'}, dimensions={0} | all-to-all | bytes 2359296 | tf_op jit(solution)/shard_map/all_to_all | solution.py:295
  36.7 0.0 all-gather.5.cloned.1.call-update
  36.7 0.0 reduce-scatter.2.cloned.1.call-start
  36.8 0.0 copy-done.3
  36.8 0.1 multiply_reduce_fusion
  36.9 19.0 %all-gather.2 = f32[8,1,128]{2,1,0:T(1,128)S(1)} all-gather(f32[1,1,128]{2,1,0:T(1,128)S(1)} %bitcast.31), channel_id=2, replica_groups=mesh['region'=32,'local'=8] {'local'}, dimensions={0}, use_global_device_ids=true | all-gather | bytes 4608 | tf_op jit(solution)/shard_map/all_gather | solution.py:307
  55.9 0.0 copy-done.6
  55.9 0.3 shard_map.103
  56.3 11.3 %all_to_all.21 = f32[32,8,128]{2,1,0:T(8,128)S(1)} all-to-all(f32[32,8,128]{2,1,0:T(8,128)S(1)} %bitcast.18), channel_id=1, replica_groups=mesh['region'=32,'local'=8] {'region'}, dimensions={0} | all-to-all | bytes 262144 | tf_op jit(solution)/shard_map/all_to_all | solution.py:295
  67.6 73.4 %all-gather.5.cloned.1.call-done.block = bf16[8,256,2304]{2,1,0:T(8,128)(2,1)} async-done(((bf16[1,256,2304]{2,1,0:T(8,128)(2,1)}), bf16[8,256,2304]{2,1,0:T(8,128)(2,1)}) %all-gather.5.cloned.1.call-update) | async-done | bytes 9437200 | tf_op jit(solution)/shard_map/all_gather | solution.py:310
  141.0 0.0 copy-start
  141.0 2.0 copy-done
  143.1 0.0 copy-start.1
  143.1 11.6 %shard_map.105 = (bf16[320,256]{1,0:T(8,128)(2,1)S(1)}, bf16[320,256]{1,0:T(8,128)(2,1)S(1)}, bf16[320,256]{1,0:T(8,128)(2,1)S(1)}, f32[256,128]{1,0:T(8,128)S(1)}) custom-call(f32[256,128]{1,0:T(8,128)S(1)} %bitcast.16, bf16[8,256,2304]{2,1,0:T(8,128)(2,1)} %all-gather.5.cloned.1.call-done.block, bf16[1,7168,256]{2,1,0:T(8,128)(2,1)S(1)} %copy-done, ...), custom_call_target="tpu_custom_call" | custom-call | tf_op jit(solution)/shard_map/pallas_call | solution.py:189
  154.7 0.0 copy-done.1
  154.7 11.7 %shard_map.106 = bf16[8,256,2304]{2,1,0:T(8,128)(2,1)} custom-call(bf16[320,256]{1,0:T(8,128)(2,1)S(1)} %get-tuple-element.10.hid, bf16[320,256]{1,0:T(8,128)(2,1)S(1)} %get-tuple-element.11.gate_g, bf16[320,256]{1,0:T(8,128)(2,1)S(1)} %get-tuple-element.12.up_g, bf16[1,7168,256]{2,1,0:T(8,128)(2,1)S(1)} %copy-done.1, bf16[1,7168,256]{2,1,0:T(8,128)(2,1)} %up_w.3, ...), custom_call_target="tpu_custom_call" | custom-call | tf_op jit(solution)/shard_map/pallas_call | solution.py:221
  166.3 0.0 copy-start.7
  166.3 0.0 reduce-scatter.2.cloned.1.call-update
  166.4 13.9 %all_to_all.22 = f32[32,8,128]{2,1,0:T(8,128)S(1)} all-to-all(f32[32,8,128]{2,1,0:T(8,128)S(1)} %bitcast.20), channel_id=1, replica_groups=mesh['region'=32,'local'=8] {'region'}, dimensions={0} | all-to-all | bytes 262144 | tf_op jit(solution)/shard_map/all_to_all | solution.py:295
  180.2 89.7 %reduce-scatter.2.cloned.1.call-done = bf16[1,256,2304]{2,1,0:T(8,128)(2,1)} async-done(((bf16[8,256,2304]{2,1,0:T(8,128)(2,1)}), bf16[1,256,2304]{2,1,0:T(8,128)(2,1)}) %reduce-scatter.2.cloned.1.call-update) | async-done | bytes 1179664 | tf_op jit(solution)/shard_map/reduce_scatter | solution.py:314
  269.9 7.4 %all-to-all-start.2 = ((bf16[32,8,2304]{2,1,0:T(8,128)(2,1)}), bf16[32,8,2304]{2,1,0:T(8,128)(2,1)S(1)}, u32[]{:S(2)}, u32[]{:S(2)}) async-start(bf16[32,8,2304]{2,1,0:T(8,128)(2,1)} %bitcast.30), calls=%async_computation.3 | async-start | bytes 2359296 | tf_op jit(solution)/shard_map/all_to_all | solution.py:295
  277.4 0.0 copy-done.7
  277.4 0.3 shard_map.107
  277.7 24.5 %all-gather.1 = f32[64,128]{1,0:T(8,128)S(1)} all-gather(f32[8,128]{1,0:T(8,128)S(1)} %shard_map.107), channel_id=3, replica_groups=mesh['region'=32,'local'=8] {'local'}, dimensions={0}, use_global_device_ids=true | all-gather | bytes 36864 | tf_op jit(solution)/shard_map/all_gather | solution.py:312
  302.2 0.0 all-to-all-done.2
  302.2 1.6 shard_map.108
Async XLA Ops:
  7.2 48.8 %copy-start.6 = (s32[128,2]{0,1:T(2,128)S(1)}, s32[128,2]{0,1:T(2,128)}, u32[]{:S(2)}) copy-start(s32[128,2]{0,1:T(2,128)} %param.13) | copy-start | bytes 3076
  7.2 133.8 %all-gather.5.cloned.1.call-start = ((), (), s32[]{:S(2)}) async-start(), calls=%async_computation.5 | async-start | bytes 10616832 | tf_op jit(solution)/shard_map/all_gather | solution.py:310
  7.9 0.9 copy-start.2
  8.9 0.9 copy-start.4
  9.8 0.7 copy-start.5
  10.5 26.3 %copy-start.3 = (bf16[128,896]{1,0:T(8,128)(2,1)S(1)}, bf16[128,896]{1,0:T(8,128)(2,1)}, u32[]{:S(2)}) copy-start(bf16[128,896]{1,0:T(8,128)(2,1)} %tok.3) | copy-start | bytes 688132
  36.7 233.2 %reduce-scatter.2.cloned.1.call-start = ((), (), s32[]{:S(2)}) async-start(), calls=%async_computation.6 | async-start | bytes 10616832 | tf_op jit(solution)/shard_map/reduce_scatter | solution.py:314
  141.0 2.0 copy-start
  143.1 11.6 %copy-start.1 = (bf16[1,7168,256]{2,1,0:T(8,128)(2,1)S(1)}, bf16[1,7168,256]{2,1,0:T(8,128)(2,1)}, u32[]{:S(2)}) copy-start(bf16[1,7168,256]{2,1,0:T(8,128)(2,1)} %gate_w.3) | copy-start | bytes 11010052
  166.3 111.0 %copy-start.7 = (f32[128,2]{0,1:T(2,128)S(1)}, f32[128,2]{0,1:T(2,128)}, u32[]{:S(2)}) copy-start(f32[128,2]{0,1:T(2,128)} %param.14) | copy-start | bytes 3076
  269.9 32.2 %all-to-all-start.2 = ((bf16[32,8,2304]{2,1,0:T(8,128)(2,1)}), bf16[32,8,2304]{2,1,0:T(8,128)(2,1)S(1)}, u32[]{:S(2)}, u32[]{:S(2)}) async-start(bf16[32,8,2304]{2,1,0:T(8,128)(2,1)} %bitcast.30), calls=%async_computation.3 | async-start | bytes 2359296 | tf_op jit(solution)/shard_map/all_to_all | solution.py:295
Sparse Core Ops, SparseCore 0:
  36.8 104.1 all-gather.4
  166.5 103.3 reduce-scatter.1

commit v2 on v1

--- a/solution.py
+++ b/solution.py
@@ -12,6 +12,7 @@
 NT = (((1,), (1,)), ((), ()))
 TN = (((0,), (0,)), ((), ()))
 VMEM_LIMIT = 48 * 1024 * 1024
+EARLY = 384
 
 
 def fold_lanes(width):
@@ -98,26 +99,62 @@
     return [n & main for n in named], [n & late for n in named]
 
 
-def pack_kernel(regions, tok, gain, grad, routes, out):
+def fold_part(regions, part):
+    i = lax.broadcasted_iota(jnp.int32, (2 * regions, 8 * regions), 0)
+    j = lax.broadcasted_iota(jnp.int32, (2 * regions, 8 * regions), 1)
+    return (j == 4 * i + part).astype(F32).astype(BF)
+
+
+def pack_kernel(regions, tok, gain, grad, routes, out, early):
     at = placed(routes[...], regions)
     pick = (at[0] | at[1]).astype(F32).astype(BF)
+    late = out.shape[1] * 2 // 5
     scaled = (tok[...].astype(F32) * gain[...]).astype(BF)
-    rows = dot(pick, jnp.concatenate([scaled, grad[...]], axis=1)).astype(BF)
+    rows = dot(pick, jnp.concatenate([scaled[:, :late], grad[:, :late]], axis=1)).astype(BF)
     cut = 8 * regions
     out[...] = encode(rows[:cut], rows[cut:], fold_matrix(regions))
+    early[...] = jnp.concatenate([scaled[:, late:], grad[:, late:]], axis=1)
 
 
 def pack(tok, gain, grad, routes, regions):
-    width = tok.shape[1]
+    count, width = tok.shape
     return pl.pallas_call(
         functools.partial(pack_kernel, regions),
-        out_shape=jax.ShapeDtypeStruct((8 * regions, packed_lanes(width)), BF),
+        out_shape=[
+            jax.ShapeDtypeStruct((8 * regions, packed_lanes(width - EARLY)), BF),
+            jax.ShapeDtypeStruct((count, 2 * EARLY), BF),
+        ],
         compiler_params=params(),
     )(tok, gain, grad, routes)
 
 
+def pack_early_kernel(regions, early, routes, out):
+    depth, _, lanes = early.shape
+    at = placed(routes[...], regions)
+    pick = (at[0] | at[1]).astype(F32).astype(BF)
+    cut = 8 * regions
+    rests = []
+    for z in range(depth):
+        rows = dot(pick, early[z]).astype(BF)
+        out[:, z * lanes : (z + 1) * lanes] = rows[:cut]
+        rests.append(rows[cut:])
+    for half in range(depth // 4):
+        stacked = jnp.concatenate([rests[part * (depth // 4) + half] for part in range(4)], axis=0)
+        at_lane = (depth + half) * lanes
+        out[:, at_lane : at_lane + lanes] = dot(fold_matrix(regions), stacked, TN).astype(BF)
+
+
+def pack_early(early, routes, regions):
+    depth, _, lanes = early.shape
+    return pl.pallas_call(
+        functools.partial(pack_early_kernel, regions),
+        out_shape=jax.ShapeDtypeStruct((8 * regions, lanes * depth * 5 // 4), BF),
+        compiler_params=params(),
+    )(early, routes)
+
+
 def inverse(squares, full):
-    return lax.rsqrt(jnp.sum(squares, axis=0, keepdims=True) / full + 1e-06)
+    return lax.rsqrt(squares / full + 1e-06)
 
 
 def spread_kernel(regions, full, squares, routes, out):
@@ -137,9 +174,11 @@
     )(squares, routes)
 
 
-def hidden_kernel(regions, width, scales, block, gate_w, up_w, down_w, hid_out, gate_out, up_out, scal_out, acc_g, acc_u, acc_h):
+def early_kernel(regions, main, rest, gate_w, up_w, down_w, acc_g, acc_u, acc_h):
     step = pl.program_id(0)
-    fold = fold_matrix(regions)
+    lanes = main.shape[1]
+    width = lanes // 2
+    skip = gate_w.shape[1] - width
 
     @pl.when(step == 0)
     def _():
@@ -147,10 +186,61 @@
         acc_u[...] = jnp.zeros_like(acc_u)
         acc_h[...] = jnp.zeros_like(acc_h)
 
+    part = step // (pl.num_programs(0) // 4)
+    low = dot(fold_part(regions, part), rest[...]).astype(BF)
+    rows = jnp.concatenate([main[...], low], axis=0)
+    acc_g[...] += dot(rows[:, :width], gate_w[0, skip:, :])
+    acc_u[...] += dot(rows[:, :width], up_w[0, skip:, :])
+    acc_h[...] += dot(rows[:, width:], down_w[0, :, skip:], NT)
+
+
+def whole(shape):
+    return pl.BlockSpec(shape, lambda z: (0,) * len(shape))
+
+
+def weight_specs(width, units):
+    return [
+        pl.BlockSpec((1, width, units), lambda z: (0, z, 0)),
+        pl.BlockSpec((1, width, units), lambda z: (0, z, 0)),
+        pl.BlockSpec((1, units, width), lambda z: (0, 0, z)),
+    ]
+
+
+def early_part(rows, gate_w, up_w, down_w, regions, depth):
+    cut = rows.shape[0]
+    width, units = gate_w.shape[1] // depth, gate_w.shape[2]
+    lanes = 2 * EARLY
+    total = 10 * regions
+    return pl.pallas_call(
+        functools.partial(early_kernel, regions),
+        grid=(depth,),
+        in_specs=[
+            pl.BlockSpec((cut, lanes), lambda z: (0, z)),
+            pl.BlockSpec((cut, lanes), lambda z: (0, depth + z % (depth // 4))),
+        ]
+        + weight_specs(width, units),
+        out_specs=[whole((total, units))] * 3,
+        out_shape=[jax.ShapeDtypeStruct((total, units), F32)] * 3,
+        compiler_params=params(),
+    )(rows, rows, gate_w, up_w, down_w)
+
+
+def hidden_kernel(
+    regions, width, scales, block, gate_w, up_w, down_w, pre_g, pre_u, pre_h, hid_out, gate_out, up_out, scal_out, acc_g, acc_u, acc_h
+):
+    step = pl.program_id(0)
+    fold = fold_matrix(regions)
+
+    @pl.when(step == 0)
+    def _():
+        acc_g[...] = pre_g[...]
+        acc_u[...] = pre_u[...]
+        acc_h[...] = pre_h[...]
+
     rows_in, rows_grad = decode(block[0], width, fold)
-    acc_g[...] += dot(rows_in, gate_w[0])
-    acc_u[...] += dot(rows_in, up_w[0])
-    acc_h[...] += dot(rows_grad, down_w[0], NT)
+    acc_g[...] += dot(rows_in, gate_w[0, :width, :])
+    acc_u[...] += dot(rows_in, up_w[0, :width, :])
+    acc_h[...] += dot(rows_grad, down_w[0, :, :width], NT)
 
     @pl.when(step == pl.num_programs(0) - 1)
     def _():
@@ -180,55 +270,80 @@
         scal_out[...] = main + dot((a == 4 * b).astype(F32), rest, precision=lax.Precision.HIGHEST)
 
 
-def hidden_part(scales, blocks, gate_w, up_w, down_w, regions):
-    count, rows, lanes = blocks.shape
-    width = gate_w.shape[1] // count
-    units = gate_w.shape[2]
+def hidden_part(scales, blocks, gate_w, up_w, down_w, sums, regions):
+    depth, rows, lanes = blocks.shape
+    width, units = gate_w.shape[1] // depth, gate_w.shape[2]
     total = 10 * regions
-    whole = lambda shape: pl.BlockSpec(shape, lambda z: (0,) * len(shape))
-    return pl.pallas_call(
-        functools.partial(hidden_kernel, regions, width),
-        grid=(count,),
-        in_specs=[
-            whole((rows, 128)),
-            pl.BlockSpec((1, rows, lanes), lambda z: (z, 0, 0)),
-            pl.BlockSpec((1, width, units), lambda z: (0, z, 0)),
-            pl.BlockSpec((1, width, units), lambda z: (0, z, 0)),
-            pl.BlockSpec((1, units, width), lambda z: (0, 0, z)),
-        ],
+    return pl.pallas_call(
+        functools.partial(hidden_kernel, regions, width - EARLY),
+        grid=(depth,),
+        in_specs=[whole((rows, 128)), pl.BlockSpec((1, rows, lanes), lambda z: (z, 0, 0))]
+        + weight_specs(width, units)
+        + [whole((total, units))] * 3,
         out_specs=[whole((total, units))] * 3 + [whole((rows, 128))],
         out_shape=[jax.ShapeDtypeStruct((total, units), BF)] * 3 + [jax.ShapeDtypeStruct((rows, 128), F32)],
         scratch_shapes=[pltpu.VMEM((total, units), F32)] * 3,
         compiler_params=params(),
-    )(scales, blocks, gate_w, up_w, down_w)
+    )(scales, blocks, gate_w, up_w, down_w, *sums)
+
+
+def back_early_kernel(regions, hid, gate_g, up_g, gate_w, up_w, down_w, out):
+    depth = pl.num_programs(0)
+    step = pl.program_id(0)
+    skip = gate_w.shape[1] - EARLY
+    lanes = 2 * EARLY
+    moe = dot(hid[...], down_w[0, :, skip:]).astype(BF)
+    grad = (dot(gate_g[...], gate_w[0, skip:, :], NT) + dot(up_g[...], up_w[0, skip:, :], NT)).astype(BF)
+    both = jnp.concatenate([moe, grad], axis=1)
+    cut = 8 * regions
+    quarter = depth // 4
+    out[:, pl.ds(pl.multiple_of(step * lanes, 128), lanes)] = both[:cut]
+    spot = pl.ds(pl.multiple_of((depth + step % quarter) * lanes, 128), lanes)
+    low = dot(fold_part(regions, step // quarter), both[cut:], TN).astype(BF)
+
+    @pl.when(step < quarter)
+    def _():
+        out[:, spot] = low
+
+    @pl.when(step >= quarter)
+    def _():
+        out[:, spot] = out[:, spot] + low
+
+
+def back_early(hid, gate_g, up_g, gate_w, up_w, down_w, regions, depth):
+    width, units = gate_w.shape[1] // depth, gate_w.shape[2]
+    total = 10 * regions
+    shape = (8 * regions, 2 * EARLY * depth * 5 // 4)
+    return pl.pallas_call(
+        functools.partial(back_early_kernel, regions),
+        grid=(depth,),
+        in_specs=[whole((total, units))] * 3 + weight_specs(width, units),
+        out_specs=whole(shape),
+        out_shape=jax.ShapeDtypeStruct(shape, BF),
+        compiler_params=params(),
+    )(hid, gate_g, up_g, gate_w, up_w, down_w)
 
 
 def back_kernel(regions, hid, gate_g, up_g, gate_w, up_w, down_w, out):
-    moe = dot(hid[...], down_w[0]).astype(BF)
-    grad = (dot(gate_g[...], gate_w[0], NT) + dot(up_g[...], up_w[0], NT)).astype(BF)
+    late = gate_w.shape[1] - EARLY
+    moe = dot(hid[...], down_w[0, :, :late]).astype(BF)
+    grad = (dot(gate_g[...], gate_w[0, :late, :], NT) + dot(up_g[...], up_w[0, :late, :], NT)).astype(BF)
     both = jnp.concatenate([moe, grad], axis=1)
     cut = 8 * regions
     out[0] = encode(both[:cut], both[cut:], fold_matrix(regions))
 
 
-def back_part(hid, gate_g, up_g, gate_w, up_w, down_w, regions, count):
-    width = gate_w.shape[1] // count
-    units = gate_w.shape[2]
+def back_part(hid, gate_g, up_g, gate_w, up_w, down_w, regions, depth):
+    width, units = gate_w.shape[1] // depth, gate_w.shape[2]
     total = 10 * regions
-    lanes = packed_lanes(width)
+    lanes = packed_lanes(width - EARLY)
     rows = 8 * regions
-    whole = lambda shape: pl.BlockSpec(shape, lambda z: (0,) * len(shape))
     return pl.pallas_call(
         functools.partial(back_kernel, regions),
-        grid=(count,),
-        in_specs=[whole((total, units))] * 3
-        + [
-            pl.BlockSpec((1, width, units), lambda z: (0, z, 0)),
-            pl.BlockSpec((1, width, units), lambda z: (0, z, 0)),
-            pl.BlockSpec((1, units, width), lambda z: (0, 0, z)),
-        ],
+        grid=(depth,),
+        in_specs=[whole((total, units))] * 3 + weight_specs(width, units),
         out_specs=pl.BlockSpec((1, rows, lanes), lambda z: (z, 0, 0)),
-        out_shape=jax.ShapeDtypeStruct((count, rows, lanes), BF),
+        out_shape=jax.ShapeDtypeStruct((depth, rows, lanes), BF),
         compiler_params=params(),
     )(hid, gate_g, up_g, gate_w, up_w, down_w)
 
@@ -255,29 +370,50 @@
     )(scal, routes, weights)
 
 
-def combine_rows(block, width, routes, weights, regions):
+def combining(routes, weights, regions):
     at = placed(routes, regions)
     weight = jnp.where(at[0], weights[0:1, :], 0.0) + jnp.where(at[1], weights[1:2, :], 0.0)
     high = weight.astype(BF)
-    low = (weight - high.astype(F32)).astype(BF)
-    return [dot(high, rows, TN) + dot(low, rows, TN) for rows in decode(block, width, fold_matrix(regions))]
-
-
-def final_kernel(regions, full, back, tok, gain, squares, sums, routes, weights, moe_out, grad_out, comb_out):
-    width = tok.shape[1]
-    moe, grad = combine_rows(back[...], width, routes[...], weights[...], regions)
-    moe_out[...] = moe.astype(BF)
-    total = jnp.sum(sums[...], axis=0)
+    return high, (weight - high.astype(F32)).astype(BF)
+
+
+def combine_early_kernel(regions, back, routes, weights, out):
+    depth, _, lanes = out.shape
+    high, low = combining(routes[...], weights[...], regions)
+    quarter = depth // 4
+    rests = [dot(fold_matrix(regions), back[:, (depth + half) * lanes : (depth + half + 1) * lanes]).astype(BF) for half in range(quarter)]
+    few = 2 * regions
+    for z in range(depth):
+        part = z // quarter
+        rest = rests[z % quarter][part * few : (part + 1) * few]
+        rows = jnp.concatenate([back[:, z * lanes : (z + 1) * lanes], rest], axis=0)
+        out[z] = (dot(high, rows, TN) + dot(low, rows, TN)).astype(BF)
+
+
+def combine_early(back, routes, weights, regions, depth):
+    return pl.pallas_call(
+        functools.partial(combine_early_kernel, regions),
+        out_shape=jax.ShapeDtypeStruct((depth, routes.shape[1], 2 * EARLY), BF),
+        compiler_params=params(),
+    )(back, routes, weights)
+
+
+def final_kernel(regions, full, back, early, tok, gain, squares, sums, routes, weights, moe_out, grad_out, comb_out):
+    late = tok.shape[1] - EARLY
+    high, low = combining(routes[...], weights[...], regions)
+    moe, grad = [dot(high, rows, TN) + dot(low, rows, TN) for rows in decode(back[...], late, fold_matrix(regions))]
+    moe_out[:, :late] = moe.astype(BF)
+    moe_out[:, late:] = early[:, :EARLY]
+    total = sums[...]
     comb_out[...] = total[0:2]
-    inv_row = inverse(squares[...], full)
     row = lax.broadcasted_iota(jnp.int32, total.shape, 0)
-    columns = jnp.transpose(jnp.where(row == 3, inv_row, total))
+    columns = jnp.transpose(jnp.where(row == 3, inverse(squares[...], full), total))
     inner, inv = columns[:, 2:3], columns[:, 3:4]
-    scaled = gain[...] * grad
+    scaled = gain[...] * jnp.concatenate([grad, early[:, EARLY:].astype(F32)], axis=1)
     grad_out[...] = (inv * scaled - tok[...].astype(F32) * (inv * inv * inv * inner / full)).astype(BF)
 
 
-def final(back, tok, gain, squares, sums, routes, weights, regions, full):
+def final(back, early, tok, gain, squares, sums, routes, weights, regions, full):
     count, width = tok.shape
     return pl.pallas_call(
         functools.partial(final_kernel, regions, full),
@@ -287,13 +423,22 @@
             jax.ShapeDtypeStruct((2, count), F32),
         ],
         compiler_params=params(),
-    )(back, tok, gain, squares, sums, routes, weights)
+    )(back, early, tok, gain, squares, sums, routes, weights)
 
 
 def swap(array, regions):
     split = array.reshape(regions, 8, array.shape[1])
     moved = lax.all_to_all(split, "region", split_axis=0, concat_axis=0, tiled=True)
     return moved.reshape(array.shape)
+
+
+def add_over_local(array):
+    depth = lax.axis_size("local")
+    step = 1
+    while step < depth:
+        array = array + lax.ppermute(array, "local", [(z, z ^ step) for z in range(depth)])
+        step *= 2
+    return array
 
 
 def on_device(tokens, norm_gain, w_gate, w_up, w_down, routes, combine, grad_out):
@@ -303,17 +448,22 @@
     gain = norm_gain.reshape(1, -1)
     routes, weights = routes.T, combine.T
     wide = tokens.astype(F32)
-    packed = pack(tokens, gain, grad_out, routes, regions)
-    squares = lax.all_gather(jnp.sum(wide * wide, axis=1), "local")
-    rows = swap(packed, regions)
+    packed, early = pack(tokens, gain, grad_out, routes, regions)
+    early = lax.all_gather(early, "local")
+    squares = add_over_local(jnp.sum(wide * wide, axis=1).reshape(1, -1))
+    blocks = lax.all_gather(swap(packed, regions), "local")
     scales = swap(spread(squares, routes, regions, full), regions)
-    blocks = lax.all_gather(rows, "local")
-    hid, gate_g, up_g, scal = hidden_part(scales, blocks, w_gate, w_up, w_down, regions)
-    sums = lax.all_gather(scalars(swap(scal, regions), routes, weights, regions), "local")
-    partial = back_part(hid, gate_g, up_g, w_gate, w_up, w_down, regions, depth)
+    rows = swap(pack_early(early, routes, regions), regions)
+    sums = early_part(rows, w_gate, w_up, w_down, regions, depth)
+    hid, gate_g, up_g, scal = hidden_part(scales, blocks, w_gate, w_up, w_down, sums, regions)
+    inner = (hid, gate_g, up_g, w_gate, w_up, w_down, regions, depth)
+    back_rows = back_early(*inner)
+    partial = back_part(*inner)
+    sums = add_over_local(scalars(swap(scal, regions), routes, weights, regions))
     summed = lax.psum_scatter(partial, "local", scatter_dimension=0)
-    back = swap(summed, regions)
-    moe, grad, comb = final(back, tokens, gain, squares, sums, routes, weights, regions, full)
+    shares = combine_early(swap(back_rows, regions), routes, weights, regions, depth)
+    own = lax.psum_scatter(shares, "local", scatter_dimension=0)
+    moe, grad, comb = final(swap(summed, regions), own, tokens, gain, squares, sums, routes, weights, regions, full)
     return moe, grad, comb.T
 
 

time: 311 us -> 273 us (0.88)
  waiting for transfers between devices: 163 us -> 77.8 us
  starting transfers between devices: 7.49 us -> 34.6 us
  Pallas kernels: 26.4 us -> 47 us
  blocking collectives: 94 us -> 84.1 us
  local copies, waits for them, and re-layouts: 5.3 us -> 14.4 us
    reduce_scatter x1, waiting for transfers between devices: 89.7 us -> 0.01 us  [on_device(): summed = lax.psum_scatter(partial, 'local', scatter_dimension=0)]
    all_gather x1 -> x2, waiting for transfers between devices: 73.4 us -> 24.2 us  [the longest x1 24.2 us: on_device(): early = lax.all_gather(early, 'local')]
    all_gather x2 -> x0, blocking collectives: 43.5 us -> none  [the longest x1 24.5 us: on_device(): lax.all_gather(scalars(swap(scal, regions), routes, weights, regions), 'l...]
    all_to_all x3, blocking collectives: 50.5 us -> 84.1 us  [swap(): lax.all_to_all(split, 'region', split_axis=0, concat_axis=0, tiled=True)]
    all_to_all x1 -> x3, waiting for transfers between devices: 0.01 us -> 30.1 us  [swap(): lax.all_to_all(split, 'region', split_axis=0, concat_axis=0, tiled=True)]
    pallas_call x3 -> x7, Pallas kernels: 24.1 us -> 44.2 us  [the longest x1 10.3 us: back_early(): pl.pallas_call(functools.partial(back_early_kernel, regions), grid=(depth...]
    ppermute x0 -> x6, waiting for transfers between devices: none -> 19.2 us  [add_over_local(): lax.ppermute(array, 'local', [(z, z ^ step) for z in range(depth)])]
    all_to_all x1 -> x3, starting transfers between devices: 7.41 us -> 22.4 us  [swap(): lax.all_to_all(split, 'region', split_axis=0, concat_axis=0, tiled=True)]
  transfers between devices with their start and end apart: 3 -> 13, of which waited for: 2 -> 9; matrix products, arithmetic and copies ran while one was open for 0% -> 0% of each run, Pallas kernels for 0% -> 9%
where the time goes in v2:
time: 273 us; the launch traced here: 272 us
  blocking collectives  84.1 us (31%)
  waiting for transfers between devices  77.8 us (28%)
  Pallas kernels  47 us (17%)
  starting transfers between devices  34.6 us (13%)
  local copies, waits for them, and re-layouts  14.4 us (5%)
  between operations  13.9 us (5%)
    all_to_all x3, blocking collectives, swap(): lax.all_to_all(split, 'region', split_axis=0, concat_axis=0, tiled=True)  84.1 us
    all_to_all x3, waiting for transfers between devices, swap(): lax.all_to_all(split, 'region', split_axis=0, concat_axis=0, tiled=True)  30.1 us
    all_gather x1, waiting for transfers between devices, on_device(): early = lax.all_gather(early, 'local')  24.2 us
    all_to_all x3, starting transfers between devices, swap(): lax.all_to_all(split, 'region', split_axis=0, concat_axis=0, tiled=True)  22.4 us
    ppermute x6, waiting for transfers between devices, add_over_local(): lax.ppermute(array, 'local', [(z, z ^ step) for z in range(depth)])  19.2 us
    unnamed x26, local copies, waits for them, and re-layouts  13.7 us
    ppermute x6, starting transfers between devices, add_over_local(): lax.ppermute(array, 'local', [(z, z ^ step) for z in range(depth)])  12.1 us
    pallas_call x1, Pallas kernels, back_early(): pl.pallas_call(functools.partial(back_early_kernel, regions), grid=(depth...  10.3 us
  transfers between devices with their start and end apart: 13, of which 9 were waited for; matrix products, arithmetic and copies ran while one was open for 0% of the time, Pallas kernels for 9%

profile of v2, /device:TPU:2, one launch (start us, length us, event | category | flops | bytes accessed | tf_op | source)
XLA Modules:
  0.0 271.9 jit_solution(5497572766245900829)
XLA Ops:
  7.2 0.0 all-gather.6.cloned.1.call-start
  7.2 0.7 reshape.45.gain
  7.9 0.9 copy-done.4
  8.8 0.9 copy-done.7
  9.8 0.7 copy-done.9
  10.5 1.1 shard_map.104
  11.6 0.0 all-gather.4.cloned.1.call-start
  11.7 18.4 %all_to_all.30 = bf16[32,8,1280]{2,1,0:T(8,128)(2,1)} all-to-all(bf16[32,8,1280]{2,1,0:T(8,128)(2,1)S(1)} %bitcast.23), channel_id=1, replica_groups=mesh['region'=32,'local'=8] {'region'}, dimensions={0} | all-to-all | bytes 1310720 | tf_op jit(solution)/shard_map/all_to_all | solution.py:431
  30.1 24.2 %all-gather.6.cloned.1.call-done = bf16[1024,768]{1,0:T(8,128)(2,1)} async-done(((bf16[128,768]{1,0:T(8,128)(2,1)}), bf16[1024,768]{1,0:T(8,128)(2,1)}) %all-gather.6.cloned.1.call-update) | async-done | bytes 1572880 | tf_op jit(solution)/shard_map/all_gather | solution.py:452
  54.3 1.4 copy-done.6
  55.7 0.7 copy-done.10
  56.4 1.5 shard_map.105
  57.9 2.0 copy-done.3
  59.9 8.0 %all-to-all-start.2 = ((bf16[32,8,7680]{2,1,0:T(8,128)(2,1)}), bf16[32,8,7680]{2,1,0:T(8,128)(2,1)}, u32[]{:S(2)}, u32[]{:S(2)}) async-start(bf16[32,8,7680]{2,1,0:T(8,128)(2,1)} %bitcast.19), calls=%async_computation.2 | async-start | bytes 7864320 | tf_op jit(solution)/shard_map/all_to_all | solution.py:431
  67.9 0.1 multiply_reduce_fusion
  68.0 1.3 collective-permute-start
  69.4 2.3 collective-permute-done
  71.7 1.6 collective-permute-start.1
  73.3 2.8 %collective-permute-done.1 = f32[1,128]{1,0:T(1,128)S(1)} collective-permute-done((f32[1,128]{1,0:T(1,128)S(1)}, f32[1,128]{1,0:T(1,128)S(1)}, u32[]{:S(2)}, u32[]{:S(2)}) %collective-permute-start.1) | collective-permute-done | bytes 544 | tf_op jit(solution)/shard_map/ppermute | solution.py:439
  76.1 3.1 %collective-permute-start.2 = (f32[1,128]{1,0:T(1,128)S(1)}, f32[1,128]{1,0:T(1,128)S(1)}, u32[]{:S(2)}, u32[]{:S(2)}) collective-permute-start(f32[1,128]{1,0:T(1,128)S(1)} %add.23), channel_id=1, source_target_pairs={{0,4},{1,5},{2,6},{3,7},{4,0},{5,1},{6,2},{7,3},{8,12},{9,13},{10,... | collective-permute-start | bytes 1544 | tf_op jit(solution)/shard_map/ppermute | solution.py:439
  79.2 4.4 %collective-permute-done.2 = f32[1,128]{1,0:T(1,128)S(1)} collective-permute-done((f32[1,128]{1,0:T(1,128)S(1)}, f32[1,128]{1,0:T(1,128)S(1)}, u32[]{:S(2)}, u32[]{:S(2)}) %collective-permute-start.2) | collective-permute-done | bytes 544 | tf_op jit(solution)/shard_map/ppermute | solution.py:439
  83.6 1.0 shard_map.103
  84.6 30.1 %all-to-all-done.2 = bf16[32,8,7680]{2,1,0:T(8,128)(2,1)} async-done(((bf16[32,8,7680]{2,1,0:T(8,128)(2,1)}), bf16[32,8,7680]{2,1,0:T(8,128)(2,1)}, u32[]{:S(2)}, u32[]{:S(2)}) %all-to-all-start.2) | async-done | bytes 3932192 | tf_op jit(solution)/shard_map/all_to_all | solution.py:431
  114.7 9.3 %all-to-all-start = ((f32[32,8,128]{2,1,0:T(8,128)}), f32[32,8,128]{2,1,0:T(8,128)S(1)}, u32[]{:S(2)}, u32[]{:S(2)}) async-start(f32[32,8,128]{2,1,0:T(8,128)} %bitcast.2), calls=%async_computation | async-start | bytes 262144 | tf_op jit(solution)/shard_map/all_to_all | solution.py:431
  124.0 0.0 reduce-scatter.3.cloned.1.call-start
  124.0 2.0 copy-done
  126.1 8.9 %shard_map.106 = (f32[320,256]{1,0:T(8,128)S(1)}, f32[320,256]{1,0:T(8,128)S(1)}, f32[320,256]{1,0:T(8,128)S(1)}) custom-call(bf16[256,7680]{1,0:T(8,128)(2,1)} %bitcast.8.main.rest, bf16[256,7680]{1,0:T(8,128)(2,1)} %bitcast.8.main.rest, bf16[1,7168,256]{2,1,0:T(8,128)(2,1)S(1)} %copy-done, bf16[1,7168,256]{2,1,0:T(8,128)(2,1)} %up_w.7, ...), custom_call_target="tpu_custom_call" | custom-call | tf_op jit(solution)/shard_map/pallas_call | solution.py:214
  135.0 0.0 all-gather.4.cloned.1.call-done.block
  135.1 2.0 copy-done.1
  137.1 9.7 %shard_map.107 = (bf16[320,256]{1,0:T(8,128)(2,1)S(1)}, bf16[320,256]{1,0:T(8,128)(2,1)S(1)}, bf16[320,256]{1,0:T(8,128)(2,1)S(1)}, f32[256,128]{1,0:T(8,128)S(1)}) custom-call(f32[256,128]{1,0:T(8,128)S(1)} %bitcast.24, bf16[8,256,1280]{2,1,0:T(8,128)(2,1)} %all-gather.4.cloned.1.call-done.block, bf16[1,7168,256]{2,1,0:T(8,128)(2,1)S(1)} %copy-done.1, ...), custom_call_target="tpu_custom_call" | custom-call | tf_op jit(solution)/shard_map/pallas_call | solution.py:277
  146.8 9.4 %shard_map.108 = bf16[8,256,1280]{2,1,0:T(8,128)(2,1)} custom-call(bf16[320,256]{1,0:T(8,128)(2,1)S(1)} %get-tuple-element.20.hid, bf16[320,256]{1,0:T(8,128)(2,1)S(1)} %get-tuple-element.21.gate_g, bf16[320,256]{1,0:T(8,128)(2,1)S(1)} %get-tuple-element.22.up_g, bf16[1,7168,256]{2,1,0:T(8,128)(2,1)S(1)} %copy-done.1, bf16[1,7168,256]{2,1,0:T(8,128)(2,1)} %up_w.7, ...), custom_call_target="tpu_custom_call" | custom-call | tf_op jit(solution)/shard_map/pallas_call | solution.py:341
  156.2 0.0 reduce-scatter.5.cloned.1.call-start
  156.3 2.0 copy-done.2
  158.3 10.3 %shard_map.109 = bf16[256,7680]{1,0:T(8,128)(2,1)} custom-call(bf16[320,256]{1,0:T(8,128)(2,1)S(1)} %get-tuple-element.20.hid, bf16[320,256]{1,0:T(8,128)(2,1)S(1)} %get-tuple-element.21.gate_g, bf16[320,256]{1,0:T(8,128)(2,1)S(1)} %get-tuple-element.22.up_g, bf16[1,7168,256]{2,1,0:T(8,128)(2,1)S(1)} %copy-done.2, bf16[1,7168,256]{2,1,0:T(8,128)(2,1)} %up_w.7, ...), custom_call_target="tpu_custom_call" | custom-call | tf_op jit(solution)/shard_map/pallas_call | solution.py:317
  168.6 53.2 %all_to_all.31 = bf16[32,8,7680]{2,1,0:T(8,128)(2,1)S(1)} all-to-all(bf16[32,8,7680]{2,1,0:T(8,128)(2,1)} %bitcast.37), channel_id=1, replica_groups=mesh['region'=32,'local'=8] {'region'}, dimensions={0} | all-to-all | bytes 7864320 | tf_op jit(solution)/shard_map/all_to_all | solution.py:431
  221.9 3.3 %shard_map.110 = bf16[8,128,768]{2,1,0:T(8,128)(2,1)} custom-call(bf16[256,7680]{1,0:T(8,128)(2,1)S(1)} %bitcast.20, s32[2,128]{1,0:T(2,128)S(1)} %bitcast.31, f32[2,128]{1,0:T(2,128)S(1)} %bitcast.34), custom_call_target="tpu_custom_call" | custom-call | tf_op jit(solution)/shard_map/pallas_call | solution.py:394
  225.2 12.5 %all_to_all.32 = f32[32,8,128]{2,1,0:T(8,128)S(1)} all-to-all(f32[32,8,128]{2,1,0:T(8,128)S(1)} %bitcast.27), channel_id=1, replica_groups=mesh['region'=32,'local'=8] {'region'}, dimensions={0} | all-to-all | bytes 262144 | tf_op jit(solution)/shard_map/all_to_all | solution.py:431
  237.6 5.1 %all-to-all-start.3 = ((bf16[32,8,1280]{2,1,0:T(8,128)(2,1)}), bf16[32,8,1280]{2,1,0:T(8,128)(2,1)S(1)}, u32[]{:S(2)}, u32[]{:S(2)}) async-start(bf16[32,8,1280]{2,1,0:T(8,128)(2,1)} %bitcast.39), calls=%async_computation.4 | async-start | bytes 1310720 | tf_op jit(solution)/shard_map/all_to_all | solution.py:431
  242.7 0.3 shard_map.111
  243.0 1.3 collective-permute-start.3
  244.4 2.4 collective-permute-done.3
  246.7 1.6 collective-permute-start.4
  248.3 2.9 %collective-permute-done.4 = f32[8,128]{1,0:T(8,128)S(1)} collective-permute-done((f32[8,128]{1,0:T(8,128)S(1)}, f32[8,128]{1,0:T(8,128)S(1)}, u32[]{:S(2)}, u32[]{:S(2)}) %collective-permute-start.4) | collective-permute-done | bytes 4128 | tf_op jit(solution)/shard_map/ppermute | solution.py:439
  251.2 3.1 %collective-permute-start.5 = (f32[8,128]{1,0:T(8,128)S(1)}, f32[8,128]{1,0:T(8,128)S(1)}, u32[]{:S(2)}, u32[]{:S(2)}) collective-permute-start(f32[8,128]{1,0:T(8,128)S(1)} %add.26), channel_id=1, source_target_pairs={{0,4},{1,5},{2,6},{3,7},{4,0},{5,1},{6,2},{7,3},{8,12},{9,13},{10,... | collective-permute-start | bytes 12296 | tf_op jit(solution)/shard_map/ppermute | solution.py:439
  254.3 4.5 %collective-permute-done.5 = f32[8,128]{1,0:T(8,128)S(1)} collective-permute-done((f32[8,128]{1,0:T(8,128)S(1)}, f32[8,128]{1,0:T(8,128)S(1)}, u32[]{:S(2)}, u32[]{:S(2)}) %collective-permute-start.5) | collective-permute-done | bytes 4128 | tf_op jit(solution)/shard_map/ppermute | solution.py:439
  258.9 4.1 %reduce-scatter.5.cloned.1.call-done = bf16[1,128,768]{2,1,0:T(8,128)(2,1)} async-done(((bf16[8,128,768]{2,1,0:T(8,128)(2,1)}), bf16[1,128,768]{2,1,0:T(8,128)(2,1)}) %reduce-scatter.5.cloned.1.call-update) | async-done | bytes 196624 | tf_op jit(solution)/shard_map/reduce_scatter | solution.py:465
  263.0 0.9 copy-done.8
  263.9 1.4 shard_map.112
  (29 shorter events, 0.1 us)
Async XLA Ops:
  7.2 47.1 %all-gather.6.cloned.1.call-start = ((), (), s32[]{:S(2)}) async-start(), calls=%async_computation.11 | async-start | bytes 1769472 | tf_op jit(solution)/shard_map/all_gather | solution.py:452
  7.9 0.9 copy-start.4
  8.8 0.9 copy-start.7
  9.8 0.7 copy-start.9
  11.6 123.4 %all-gather.4.cloned.1.call-start = ((), (), s32[]{:S(2)}) async-start(), calls=%async_computation.8 | async-start | bytes 5898240 | tf_op jit(solution)/shard_map/all_gather | solution.py:454
  54.3 1.4 copy-start.6
  55.7 0.7 copy-start.10
  57.9 2.0 copy-start.3
  59.9 8.0 %copy-start.5 = (bf16[128,896]{1,0:T(8,128)(2,1)S(1)}, bf16[128,896]{1,0:T(8,128)(2,1)}, u32[]{:S(2)}) copy-start(bf16[128,896]{1,0:T(8,128)(2,1)} %tok.3) | copy-start | bytes 688132
  59.9 23.7 %copy-start.11 = (s32[128,2]{0,1:T(2,128)S(1)}, s32[128,2]{0,1:T(2,128)}, u32[]{:S(2)}) copy-start(s32[128,2]{0,1:T(2,128)} %param.13) | copy-start | bytes 3076
  59.9 54.8 %all-to-all-start.2 = ((bf16[32,8,7680]{2,1,0:T(8,128)(2,1)}), bf16[32,8,7680]{2,1,0:T(8,128)(2,1)}, u32[]{:S(2)}, u32[]{:S(2)}) async-start(bf16[32,8,7680]{2,1,0:T(8,128)(2,1)} %bitcast.19), calls=%async_computation.2 | async-start | bytes 7864320 | tf_op jit(solution)/shard_map/all_to_all | solution.py:431
  68.0 3.6 %collective-permute-start = (f32[1,128]{1,0:T(1,128)S(1)}, f32[1,128]{1,0:T(1,128)S(1)}, u32[]{:S(2)}, u32[]{:S(2)}) collective-permute-start(f32[1,128]{1,0:T(1,128)S(1)} %bitcast.40), channel_id=1, source_target_pairs={{0,1},{1,0},{2,3},{3,2},{4,5},{5,4},{6,7},{7,6},{8,9},{9,8},{10,11... | collective-permute-start | bytes 1544 | tf_op jit(solution)/shard_map/ppermute | solution.py:439
  71.7 4.4 %collective-permute-start.1 = (f32[1,128]{1,0:T(1,128)S(1)}, f32[1,128]{1,0:T(1,128)S(1)}, u32[]{:S(2)}, u32[]{:S(2)}) collective-permute-start(f32[1,128]{1,0:T(1,128)S(1)} %bitcast_add_fusion), channel_id=1, source_target_pairs={{0,2},{1,3},{2,0},{3,1},{4,6},{5,7},{6,4},{7,5},{8,10},{9,11},{10,... | collective-permute-start | bytes 1544 | tf_op jit(solution)/shard_map/ppermute | solution.py:439
  76.1 7.5 %collective-permute-start.2 = (f32[1,128]{1,0:T(1,128)S(1)}, f32[1,128]{1,0:T(1,128)S(1)}, u32[]{:S(2)}, u32[]{:S(2)}) collective-permute-start(f32[1,128]{1,0:T(1,128)S(1)} %add.23), channel_id=1, source_target_pairs={{0,4},{1,5},{2,6},{3,7},{4,0},{5,1},{6,2},{7,3},{8,12},{9,13},{10,... | collective-permute-start | bytes 1544 | tf_op jit(solution)/shard_map/ppermute | solution.py:439
  114.7 20.4 %all-to-all-start = ((f32[32,8,128]{2,1,0:T(8,128)}), f32[32,8,128]{2,1,0:T(8,128)S(1)}, u32[]{:S(2)}, u32[]{:S(2)}) async-start(f32[32,8,128]{2,1,0:T(8,128)} %bitcast.2), calls=%async_computation | async-start | bytes 262144 | tf_op jit(solution)/shard_map/all_to_all | solution.py:431
  124.0 113.6 %reduce-scatter.3.cloned.1.call-start = ((), (), s32[]{:S(2)}) async-start(), calls=%async_computation.9 | async-start | bytes 5898240 | tf_op jit(solution)/shard_map/reduce_scatter | solution.py:463
  124.0 2.0 copy-start
  135.1 2.0 copy-start.1
  156.2 106.8 %reduce-scatter.5.cloned.1.call-start = ((), (), s32[]{:S(2)}) async-start(), calls=%async_computation.10 | async-start | bytes 1769472 | tf_op jit(solution)/shard_map/reduce_scatter | solution.py:465
  156.3 2.0 copy-start.2
  168.6 53.2 %copy-start.12 = (f32[128,2]{0,1:T(2,128)S(1)}, f32[128,2]{0,1:T(2,128)}, u32[]{:S(2)}) copy-start(f32[128,2]{0,1:T(2,128)} %param.14) | copy-start | bytes 3076
  237.6 25.4 %all-to-all-start.3 = ((bf16[32,8,1280]{2,1,0:T(8,128)(2,1)}), bf16[32,8,1280]{2,1,0:T(8,128)(2,1)S(1)}, u32[]{:S(2)}, u32[]{:S(2)}) async-start(bf16[32,8,1280]{2,1,0:T(8,128)(2,1)} %bitcast.39), calls=%async_computation.4 | async-start | bytes 1310720 | tf_op jit(solution)/shard_map/all_to_all | solution.py:431
  243.0 3.7 %collective-permute-start.3 = (f32[8,128]{1,0:T(8,128)S(1)}, f32[8,128]{1,0:T(8,128)S(1)}, u32[]{:S(2)}, u32[]{:S(2)}) collective-permute-start(f32[8,128]{1,0:T(8,128)S(1)} %shard_map.111), channel_id=1, source_target_pairs={{0,1},{1,0},{2,3},{3,2},{4,5},{5,4},{6,7},{7,6},{8,9},{9,8},{10,11... | collective-permute-start | bytes 12296 | tf_op jit(solution)/shard_map/ppermute | solution.py:439
  246.7 4.5 %collective-permute-start.4 = (f32[8,128]{1,0:T(8,128)S(1)}, f32[8,128]{1,0:T(8,128)S(1)}, u32[]{:S(2)}, u32[]{:S(2)}) collective-permute-start(f32[8,128]{1,0:T(8,128)S(1)} %add.25), channel_id=1, source_target_pairs={{0,2},{1,3},{2,0},{3,1},{4,6},{5,7},{6,4},{7,5},{8,10},{9,11},{10,... | collective-permute-start | bytes 12296 | tf_op jit(solution)/shard_map/ppermute | solution.py:439
  251.2 7.6 %collective-permute-start.5 = (f32[8,128]{1,0:T(8,128)S(1)}, f32[8,128]{1,0:T(8,128)S(1)}, u32[]{:S(2)}, u32[]{:S(2)}) collective-permute-start(f32[8,128]{1,0:T(8,128)S(1)} %add.26), channel_id=1, source_target_pairs={{0,4},{1,5},{2,6},{3,7},{4,0},{5,1},{6,2},{7,3},{8,12},{9,13},{10,... | collective-permute-start | bytes 12296 | tf_op jit(solution)/shard_map/ppermute | solution.py:439
  263.0 0.9 copy-start.8
Sparse Core Ops, SparseCore 0:
  11.7 42.4 all-gather.5
  56.1 63.6 all-gather.3
  156.4 63.8 reduce-scatter.2
  225.3 37.6 reduce-scatter.4

commit v3 on v1

v3 whole, which is shorter than its diff:
```python
import functools

import jax
import jax.numpy as jnp
from jax import lax
from jax.experimental import pallas as pl
from jax.experimental.pallas import tpu as pltpu
from jax.sharding import PartitionSpec as P

BF = jnp.bfloat16
F32 = jnp.float32
NT = (((1,), (1,)), ((), ()))
TN = (((0,), (0,)), ((), ()))
VMEM_LIMIT = 48 * 1024 * 1024
EARLY = 384


def fold_lanes(width):
    return 128 * -(-width // 256)


def packed_lanes(width):
    return 2 * width + fold_lanes(width)


def dot(a, b, dims=(((1,), (0,)), ((), ())), precision=None):
    return lax.dot_general(a, b, dims, precision=precision, preferred_element_type=F32)


def params(**kw):
    return pltpu.CompilerParams(vmem_limit_bytes=VMEM_LIMIT, **kw)


def whole(shape):
    return pl.BlockSpec(shape, lambda *_: (0,) * len(shape))


def fold_matrix(regions):
    rows = 8 * regions
    i = lax.broadcasted_iota(jnp.int32, (rows, rows), 0)
    j = lax.broadcasted_iota(jnp.int32, (rows, rows), 1)
    return (j == 4 * (i % (2 * regions)) + i // (2 * regions)).astype(BF)


def encode(main, rest, fold):
    width = main.shape[1] // 2
    lanes = fold_lanes(width)
    pad = 2 * lanes - width
    parts = []
    for side in range(2):
        parts.append(rest[:, side * width : side * width + lanes])
        tail = rest[:, side * width + lanes : (side + 1) * width]
        if pad:
            tail = jnp.concatenate([tail, jnp.zeros((rest.shape[0], pad), rest.dtype)], axis=1)
        parts.append(tail)
    stacked = jnp.concatenate(parts, axis=0)
    return jnp.concatenate([main, dot(fold, stacked, TN).astype(BF)], axis=1)


def decode(block, width, fold):
    lanes = fold_lanes(width)
    rows = block.shape[0]
    rest = dot(fold, block[:, 2 * width :]).astype(BF)
    few = rows // 4
    sides = []
    for side in range(2):
        head = rest[(2 * side) * few : (2 * side + 1) * few]
        tail = rest[(2 * side + 1) * few : (2 * side + 2) * few, : width - lanes]
        low = jnp.concatenate([head, tail], axis=1)
        sides.append(jnp.concatenate([block[:, side * width : (side + 1) * width], low], axis=0))
    return sides


def slot_ids(regions, tokens):
    s = lax.broadcasted_iota(jnp.int32, (10 * regions, tokens), 0)
    late = s - 8 * regions
    expert = jnp.where(late < 0, s // 8, late // 2)
    slot = jnp.where(late < 0, s % 8, 8 + late % 2)
    return expert, slot


def ranks(named):
    count = named.shape[1]
    before = lax.broadcasted_iota(jnp.int32, (count, count), 0)
    after = lax.broadcasted_iota(jnp.int32, (count, count), 1)
    return dot(named.astype(F32).astype(BF), (before < after).astype(F32).astype(BF))


def placed(routes, regions):
    expert, slot = slot_ids(regions, routes.shape[1])
    named = [routes[k : k + 1, :] == expert for k in range(2)]
    at = ranks(named[0] | named[1]) == slot.astype(F32)
    return [n & at for n in named]


def placed_packed(routes, regions):
    s = lax.broadcasted_iota(jnp.int32, (8 * regions, routes.shape[1]), 0)
    expert = s // 8
    named = [routes[k : k + 1, :] == expert for k in range(2)]
    rank = ranks(named[0] | named[1])
    main = rank == (s % 8).astype(F32)
    late = (rank == (8 + (s % 8) // 4).astype(F32)) & (s % 4 == 0)
    return [n & main for n in named], [n & late for n in named]


def pack_kernel(regions, tok, gain, grad, routes, out, early):
    at = placed(routes[...], regions)
    pick = (at[0] | at[1]).astype(F32).astype(BF)
    late = out.shape[1] * 2 // 5
    scaled = (tok[...].astype(F32) * gain[...]).astype(BF)
    rows = dot(pick, jnp.concatenate([scaled[:, :late], grad[:, :late]], axis=1)).astype(BF)
    cut = 8 * regions
    out[...] = encode(rows[:cut], rows[cut:], fold_matrix(regions))
    early[...] = jnp.concatenate([scaled[:, late:], grad[:, late:]], axis=1)


def pack(tok, gain, grad, routes, regions):
    count, width = tok.shape
    shapes = [
        jax.ShapeDtypeStruct((8 * regions, packed_lanes(width - EARLY)), BF),
        jax.ShapeDtypeStruct((count, 2 * EARLY), BF),
    ]
    return once(functools.partial(pack_kernel, regions), shapes, tok, gain, grad, routes)


def inverse(squares, full):
    return lax.rsqrt(squares / full + 1e-06)


def triple(value):
    high = value.astype(BF)
    value = value - high.astype(F32)
    middle = value.astype(BF)
    return [high, middle, (value - middle.astype(F32)).astype(BF)]


def in_lanes(columns, rows):
    lane = lax.broadcasted_iota(jnp.int32, (rows, 128), 1)
    out = jnp.zeros((rows, 128), F32)
    for at, column in enumerate(columns):
        if column is not None:
            out = jnp.where(lane == at, column.astype(F32), out)
    return out.astype(BF)


def from_lanes(block, at):
    block = block.astype(F32)
    return block[:, at : at + 1] + block[:, at + 1 : at + 2] + block[:, at + 2 : at + 3]


def pack_early_kernel(regions, depth, full, routes, squares, *refs):
    blocks, out = refs[:-1], refs[-1]
    lanes = blocks[0].shape[1]
    early = {0: blocks[0][...]}
    half = depth // 2
    for hop in range(1, half):
        early[depth - hop] = blocks[2 * hop - 1][...]
        early[hop] = blocks[2 * hop][...]
    early[half] = jnp.concatenate([blocks[-2][...], blocks[-1][...]], axis=0)
    at = placed(routes[...], regions)
    pick = (at[0] | at[1]).astype(F32).astype(BF)
    cut = 8 * regions
    rests = []
    for z in range(depth):
        rows = dot(pick, early[z]).astype(BF)
        out[:, z * lanes : (z + 1) * lanes] = rows[:cut]
        rests.append(rows[cut:])
    for half in range(depth // 4):
        stacked = jnp.concatenate([rests[part * (depth // 4) + half] for part in range(4)], axis=0)
        at_lane = (depth + half) * lanes
        out[:, at_lane : at_lane + lanes] = dot(fold_matrix(regions), stacked, TN).astype(BF)
    inv = inverse(squares[...], full)
    columns = []
    for found in placed_packed(routes[...], regions):
        columns += triple(jnp.sum(jnp.where(found[0] | found[1], inv, 0.0), axis=1, keepdims=True))
    out[:, -128:] = in_lanes(columns, cut)


def once(kernel, out_shape, *operands):
    many = isinstance(out_shape, list)
    specs = [whole(shape.shape) for shape in (out_shape if many else [out_shape])]
    return pl.pallas_call(
        kernel,
        grid=(1,),
        in_specs=[whole(operand.shape) for operand in operands],
        out_specs=specs if many else specs[0],
        out_shape=out_shape,
        compiler_params=params(),
    )(*operands)


def early_shape(regions, depth):
    return (8 * regions, 2 * EARLY * depth * 5 // 4 + 128)


def pack_early(blocks, squares, routes, regions, depth, full):
    shape = jax.ShapeDtypeStruct(early_shape(regions, depth), BF)
    return once(functools.partial(pack_early_kernel, regions, depth, full), shape, routes, squares, *blocks)


def relative_specs(width, units, depth):
    return [
        pl.BlockSpec((1, width, units), lambda z, me: (0, (z + me[0]) % depth, 0)),
        pl.BlockSpec((1, width, units), lambda z, me: (0, (z + me[0]) % depth, 0)),
        pl.BlockSpec((1, units, width), lambda z, me: (0, 0, (z + me[0]) % depth)),
    ]


def hidden_kernel(
    regions, me, scales, block, main, rest, gate_w, up_w, down_w, hid_out, gate_out, up_out, scal_out, acc_g, acc_u, acc_h, fold
):
    step = pl.program_id(0)
    width = gate_w.shape[1]
    few = 2 * regions
    quarter = pl.num_programs(0) // 4

    @pl.when(step == 0)
    def _():
        fold[...] = fold_matrix(regions)
        acc_g[...] = jnp.zeros_like(acc_g)
        acc_u[...] = jnp.zeros_like(acc_u)
        acc_h[...] = jnp.zeros_like(acc_h)

    late_in, late_grad = decode(block[0], width - EARLY, fold[...])
    pick = fold[pl.ds(pl.multiple_of((step // quarter) * few, few), few), :]
    early = jnp.concatenate([main[...], dot(pick, rest[...]).astype(BF)], axis=0)
    rows_in = jnp.concatenate([late_in, early[:, :EARLY]], axis=1)
    rows_grad = jnp.concatenate([late_grad, early[:, EARLY:]], axis=1)
    acc_g[...] += dot(rows_in, gate_w[0])
    acc_u[...] += dot(rows_in, up_w[0])
    acc_h[...] += dot(rows_grad, down_w[0], NT)

    @pl.when(step == pl.num_programs(0) - 1)
    def _():
        cut = 8 * regions
        first = fold[0:few, :]
        inv = jnp.concatenate([from_lanes(scales[...], 0), from_lanes(dot(first, scales[...]), 3)], axis=0)
        gate_raw, up_raw, grad_hidden = acc_g[...], acc_u[...], acc_h[...]
        gate_pre, up_pre = gate_raw * inv, up_raw * inv
        sig = jax.nn.sigmoid(gate_pre)
        act = gate_pre * sig
        hidden = (act * up_pre).astype(BF)
        grad_gate = (grad_hidden * up_pre * sig * (1.0 + gate_pre * (1.0 - sig))).astype(BF)
        grad_up = (grad_hidden * act).astype(BF)
        hid_out[...] = hidden
        gate_out[...] = grad_gate
        up_out[...] = grad_up
        comb = jnp.sum(hidden.astype(F32) * grad_hidden, axis=1, keepdims=True)
        inner = jnp.sum(grad_gate.astype(F32) * gate_raw + grad_up.astype(F32) * up_raw, axis=1, keepdims=True)
        here = in_lanes(triple(comb[:cut]) + triple(inner[:cut]), cut)
        there = in_lanes([None] * 6 + triple(comb[cut:]) + triple(inner[cut:]), few)
        scal_out[...] = here + dot(first, there, TN).astype(BF)


def hidden_part(me, blocks, rows, gate_w, up_w, down_w, regions):
    depth, cut, lanes = blocks.shape
    width, units = gate_w.shape[1] // depth, gate_w.shape[2]
    total = 10 * regions
    return pl.pallas_call(
        functools.partial(hidden_kernel, regions),
        grid_spec=pltpu.PrefetchScalarGridSpec(
            num_scalar_prefetch=1,
            grid=(depth,),
            in_specs=[
                pl.BlockSpec((cut, 128), lambda z, me: (0, 2 * EARLY * depth * 5 // 512)),
                pl.BlockSpec((1, cut, lanes), lambda z, me: ((z + me[0]) % depth, 0, 0)),
                pl.BlockSpec((cut, 2 * EARLY), lambda z, me: (0, z)),
                pl.BlockSpec((cut, 2 * EARLY), lambda z, me: (0, depth + z % (depth // 4))),
            ]
            + relative_specs(width, units, depth),
            out_specs=[whole((total, units))] * 3 + [whole((cut, 128))],
            scratch_shapes=[pltpu.VMEM((total, units), F32)] * 3 + [pltpu.VMEM((cut, cut), BF)],
        ),
        out_shape=[jax.ShapeDtypeStruct((total, units), BF)] * 3 + [jax.ShapeDtypeStruct((cut, 128), BF)],
        compiler_params=params(),
    )(me, rows, blocks, rows, rows, gate_w, up_w, down_w)


def back_kernel(regions, me, hid, gate_g, up_g, scal, gate_w, up_w, down_w, late_out, early_out, fold):
    depth = pl.num_programs(0)
    step = pl.program_id(0)
    late = gate_w.shape[1] - EARLY
    lanes = 2 * EARLY
    few = 2 * regions
    cut = 8 * regions
    quarter = depth // 4

    @pl.when(step == 0)
    def _():
        fold[...] = fold_matrix(regions)
        early_out[:, -128:] = scal[...]

    moe = dot(hid[...], down_w[0]).astype(BF)
    grad = (dot(gate_g[...], gate_w[0], NT) + dot(up_g[...], up_w[0], NT)).astype(BF)
    both = jnp.concatenate([moe[:, :late], grad[:, :late]], axis=1)
    late_out[0] = encode(both[:cut], both[cut:], fold[...])
    both = jnp.concatenate([moe[:, late:], grad[:, late:]], axis=1)
    early_out[:, pl.ds(pl.multiple_of(step * lanes, 128), lanes)] = both[:cut]
    spot = pl.ds(pl.multiple_of((depth + step % quarter) * lanes, 128), lanes)
    pick = fold[pl.ds(pl.multiple_of((step // quarter) * few, few), few), :]
    low = dot(pick, both[cut:], TN).astype(BF)

    @pl.when(step < quarter)
    def _():
        early_out[:, spot] = low

    @pl.when(step >= quarter)
    def _():
        early_out[:, spot] = early_out[:, spot] + low


def back_part(me, hid, gate_g, up_g, scal, gate_w, up_w, down_w, regions, depth):
    width, units = gate_w.shape[1] // depth, gate_w.shape[2]
    total = 10 * regions
    cut = 8 * regions
    lanes = packed_lanes(width - EARLY)
    shape = early_shape(regions, depth)
    return pl.pallas_call(
        functools.partial(back_kernel, regions),
        grid_spec=pltpu.PrefetchScalarGridSpec(
            num_scalar_prefetch=1,
            grid=(depth,),
            in_specs=[whole((total, units))] * 3 + [whole((cut, 128))] + relative_specs(width, units, depth),
            out_specs=[pl.BlockSpec((1, cut, lanes), lambda z, me: ((z + me[0]) % depth, 0, 0)), whole(shape)],
            scratch_shapes=[pltpu.VMEM((cut, cut), BF)],
        ),
        out_shape=[jax.ShapeDtypeStruct((depth, cut, lanes), BF), jax.ShapeDtypeStruct(shape, BF)],
        compiler_params=params(),
    )(me, hid, gate_g, up_g, scal, gate_w, up_w, down_w)


def scalars(here, routes, weights, regions):
    main, late = placed_packed(routes, regions)
    parts = []
    inner = 0.0
    for k in range(2):
        comb = jnp.where(main[k], from_lanes(here, 0), 0.0) + jnp.where(late[k], from_lanes(here, 6), 0.0)
        part = jnp.where(main[k], from_lanes(here, 3), 0.0) + jnp.where(late[k], from_lanes(here, 9), 0.0)
        parts.append(jnp.sum(comb, axis=0, keepdims=True))
        inner = inner + weights[k : k + 1, :] * jnp.sum(part, axis=0, keepdims=True)
    row = lax.broadcasted_iota(jnp.int32, (8, routes.shape[1]), 0)
    return jnp.where(row == 0, parts[0], jnp.where(row == 1, parts[1], jnp.where(row == 2, inner, 0.0)))


def combining(routes, weights, regions):
    at = placed(routes, regions)
    weight = jnp.where(at[0], weights[0:1, :], 0.0) + jnp.where(at[1], weights[1:2, :], 0.0)
    high = weight.astype(BF)
    return high, (weight - high.astype(F32)).astype(BF)


def combine_early_kernel(regions, back, routes, weights, out, scal_out):
    scal_out[...] = scalars(back[:, -128:], routes[...], weights[...], regions)
    depth, _, lanes = out.shape
    high, low = combining(routes[...], weights[...], regions)
    quarter = depth // 4
    rests = [dot(fold_matrix(regions), back[:, (depth + half) * lanes : (depth + half + 1) * lanes]).astype(BF) for half in range(quarter)]
    few = 2 * regions
    for z in range(depth):
        part = z // quarter
        rest = rests[z % quarter][part * few : (part + 1) * few]
        rows = jnp.concatenate([back[:, z * lanes : (z + 1) * lanes], rest], axis=0)
        out[z] = (dot(high, rows, TN) + dot(low, rows, TN)).astype(BF)


def combine_early(back, routes, weights, regions, depth):
    count = routes.shape[1]
    shapes = [jax.ShapeDtypeStruct((depth, count, 2 * EARLY), BF), jax.ShapeDtypeStruct((8, count), F32)]
    return once(functools.partial(combine_early_kernel, regions), shapes, back, routes, weights)


def final_kernel(regions, full, back, own, left, right, tok, gain, squares, sums, routes, weights, moe_out, grad_out, comb_out):
    late = tok.shape[1] - EARLY
    high, low = combining(routes[...], weights[...], regions)
    moe, grad = [dot(high, rows, TN) + dot(low, rows, TN) for rows in decode(back[...], late, fold_matrix(regions))]
    early = own[0].astype(F32) + left[...].astype(F32) + right[...].astype(F32)
    moe_out[:, :late] = moe.astype(BF)
    moe_out[:, late:] = early[:, :EARLY].astype(BF)
    total = sums[...]
    comb_out[...] = total[0:2]
    row = lax.broadcasted_iota(jnp.int32, total.shape, 0)
    columns = jnp.transpose(jnp.where(row == 3, inverse(squares[...], full), total))
    inner, inv = columns[:, 2:3], columns[:, 3:4]
    scaled = gain[...] * jnp.concatenate([grad, early[:, EARLY:]], axis=1)
    grad_out[...] = (inv * scaled - tok[...].astype(F32) * (inv * inv * inv * inner / full)).astype(BF)


def final(back, early, tok, gain, squares, sums, routes, weights, regions, full):
    count, width = tok.shape
    shapes = [
        jax.ShapeDtypeStruct((count, width), BF),
        jax.ShapeDtypeStruct((count, width), BF),
        jax.ShapeDtypeStruct((2, count), F32),
    ]
    kernel = functools.partial(final_kernel, regions, full)
    return once(kernel, shapes, back, *early, tok, gain, squares, sums, routes, weights)


def swap(array, regions):
    split = array.reshape(regions, 8, array.shape[1])
    moved = lax.all_to_all(split, "region", split_axis=0, concat_axis=0, tiled=True)
    return moved.reshape(array.shape)


def add_over_local(array):
    depth = lax.axis_size("local")
    step = 1
    while step < depth:
        array = array + lax.ppermute(array, "local", [(z, z ^ step) for z in range(depth)])
        step *= 2
    return array


def hop(array, step):
    depth = lax.axis_size("local")
    return lax.ppermute(array, "local", [(z, (z + step) % depth) for z in range(depth)])


def ring_gather(own, squares):
    half = lax.axis_size("local") // 2
    low, high = own, own
    blocks = [own]
    for at in range(half - 1):
        low, high = hop(low, 1), hop(high, -1)
        if 1 << at < 2 * half:
            other = lax.ppermute(squares, "local", [(z, z ^ (1 << at)) for z in range(2 * half)])
            low, high, other = lax.optimization_barrier((low, high, other))
            squares = squares + other
        blocks += [low, high]
    at = half - 1
    while 1 << at < 2 * half:
        squares = squares + lax.ppermute(squares, "local", [(z, z ^ (1 << at)) for z in range(2 * half)])
        at += 1
    cut = own.shape[0] // 2
    return blocks + [hop(low[:cut], 1), hop(high[cut:], -1)], squares


def ring_scatter(shares):
    depth = shares.shape[0]
    half = depth // 2
    cut = shares.shape[1] // 2
    right, left = hop(shares[half, :cut], 1), hop(shares[half, cut:], -1)
    add = lambda a, b: (a.astype(F32) + b.astype(F32)).astype(BF)
    right = jnp.concatenate([add(shares[half - 1, :cut], right), shares[half - 1, cut:]], axis=0)
    left = jnp.concatenate([shares[half + 1, :cut], add(shares[half + 1, cut:], left)], axis=0)
    for j in range(half - 2, -1, -1):
        right, left = hop(right, 1), hop(left, -1)
        if j:
            right, left = add(shares[j], right), add(shares[depth - j], left)
    return right, left


def on_device(tokens, norm_gain, w_gate, w_up, w_down, routes, combine, grad_out):
    regions = lax.axis_size("region")
    depth = lax.axis_size("local")
    me = lax.axis_index("local").astype(jnp.int32).reshape(1)
    full = depth * tokens.shape[1]
    gain = norm_gain.reshape(1, -1)
    routes, weights = routes.T, combine.T
    wide = tokens.astype(F32)
    packed, early = pack(tokens, gain, grad_out, routes, regions)
    around, squares = ring_gather(early, jnp.sum(wide * wide, axis=1).reshape(1, -1))
    arrived, _ = lax.optimization_barrier((swap(packed, regions), around[-3]))
    blocks = lax.all_gather(arrived, "local")
    rows = swap(pack_early(around, squares, routes, regions, depth, full), regions)
    hidden = hidden_part(me, blocks, rows, w_gate, w_up, w_down, regions)
    partial, back_rows = back_part(me, *hidden, w_gate, w_up, w_down, regions, depth)
    summed = lax.psum_scatter(partial, "local", scatter_dimension=0)
    shares, sums = combine_early(swap(back_rows, regions), routes, weights, regions, depth)
    own = (shares, *ring_scatter(shares))
    sums = add_over_local(sums)
    moe, grad, comb = final(swap(summed, regions), own, tokens, gain, squares, sums, routes, weights, regions, full)
    return moe, grad, comb.T


def solution(mesh):
    specs = (
        P("region", "local"),
        P("local"),
        P("region", None, "local"),
        P("region", None, "local"),
        P("region", "local", None),
        P("region", None),
        P("region", None),
        P("region", "local"),
    )
    return jax.shard_map(
        on_device,
        mesh=mesh,
        in_specs=specs,
        out_specs=(P("region", "local"), P("region", "local"), P("region", None)),
        check_vma=False,
    )
```

time: 311 us -> 261 us (0.84)
  waiting for transfers between devices: 163 us -> 87.1 us
  starting transfers between devices: 7.49 us -> 60.7 us
  blocking collectives: 94 us -> 55.5 us
  Pallas kernels: 26.4 us -> 31.4 us
  local copies, waits for them, and re-layouts: 5.3 us -> 8.89 us
    reduce_scatter x1, waiting for transfers between devices: 89.7 us -> 0.01 us  [on_device(): summed = lax.psum_scatter(partial, 'local', scatter_dimension=0)]
    all_gather x1, waiting for transfers between devices: 73.4 us -> 0.01 us  [on_device(): blocks = lax.all_gather(arrived, 'local')]
    all_to_all x1 -> x3, waiting for transfers between devices: 0.01 us -> 47.4 us  [swap(): lax.all_to_all(split, 'region', split_axis=0, concat_axis=0, tiled=True)]
    all_gather x2 -> x0, blocking collectives: 43.5 us -> none  [the longest x1 24.5 us: on_device(): lax.all_gather(scalars(swap(scal, regions), routes, weights, regions), 'l...]
    ppermute x0 -> x22, waiting for transfers between devices: none -> 39.6 us  [the longest x16 18.8 us: hop(): lax.ppermute(array, 'local', [(z, (z + step) % depth) for z in range(dept...]
    ppermute x0 -> x22, starting transfers between devices: none -> 39.4 us  [the longest x16 27.5 us: hop(): lax.ppermute(array, 'local', [(z, (z + step) % depth) for z in range(dept...]
    all_to_all x1 -> x3, starting transfers between devices: 7.41 us -> 21.1 us  [swap(): lax.all_to_all(split, 'region', split_axis=0, concat_axis=0, tiled=True)]
    pallas_call x6, Pallas kernels: 26.4 us -> 31.4 us  [the longest x1 12.5 us: back_part(): pl.pallas_call(functools.partial(back_kernel, regions), grid_spec=pltpu.P...]
  transfers between devices with their start and end apart: 3 -> 27, of which waited for: 2 -> 13; matrix products, arithmetic and copies ran while one was open for 0% -> 1% of each run, Pallas kernels for 0% -> 2%
where the time goes in v3:
time: 261 us; the launch traced here: 259 us
  waiting for transfers between devices  87.1 us (33%)
  starting transfers between devices  60.7 us (23%)
  blocking collectives  55.5 us (21%)
  Pallas kernels  31.4 us (12%)
  between operations  14.3 us (5%)
  local copies, waits for them, and re-layouts  8.89 us (3%)
    all_to_all x1, blocking collectives, swap(): lax.all_to_all(split, 'region', split_axis=0, concat_axis=0, tiled=True)  55.5 us
    all_to_all x3, waiting for transfers between devices, swap(): lax.all_to_all(split, 'region', split_axis=0, concat_axis=0, tiled=True)  47.4 us
    ppermute x16, starting transfers between devices, hop(): lax.ppermute(array, 'local', [(z, (z + step) % depth) for z in range(dept...  27.5 us
    all_to_all x3, starting transfers between devices, swap(): lax.all_to_all(split, 'region', split_axis=0, concat_axis=0, tiled=True)  21.1 us
    ppermute x16, waiting for transfers between devices, hop(): lax.ppermute(array, 'local', [(z, (z + step) % depth) for z in range(dept...  18.8 us
    pallas_call x1, Pallas kernels, back_part(): pl.pallas_call(functools.partial(back_kernel, regions), grid_spec=pltpu.P...  12.5 us
    pallas_call x1, Pallas kernels, hidden_part(): pl.pallas_call(functools.partial(hidden_kernel, regions), grid_spec=pltpu...  12 us
    ppermute x3, waiting for transfers between devices, ring_gather(): lax.ppermute(squares, 'local', [(z, z ^ 1 << at) for z in range(2 * half)])  11.7 us
  transfers between devices with their start and end apart: 27, of which 13 were waited for; matrix products, arithmetic and copies ran while one was open for 1% of the time, Pallas kernels for 2%

profile of v3, /device:TPU:2, one launch (start us, length us, event | category | flops | bytes accessed | tf_op | source)
XLA Modules:
  0.0 259.4 jit_solution(16671439556079092614)
XLA Ops:
  7.2 0.7 reshape.50.gain
  7.9 0.9 copy-done.2
  8.8 0.9 copy-done.4
  9.7 0.7 copy-done.5
  10.4 1.5 shard_map.103
  11.9 7.6 %all-to-all-start.1 = ((bf16[32,8,1280]{2,1,0:T(8,128)(2,1)}), bf16[32,8,1280]{2,1,0:T(8,128)(2,1)S(1)}, u32[]{:S(2)}, u32[]{:S(2)}) async-start(bf16[32,8,1280]{2,1,0:T(8,128)(2,1)} %bitcast.5), calls=%async_computation.1 | async-start | bytes 1310720 | tf_op jit(solution)/shard_map/all_to_all | solution.py:401
  19.6 2.0 collective-permute-start
  21.6 4.0 %collective-permute-start.1 = (bf16[128,768]{1,0:T(8,128)(2,1)S(1)}, bf16[128,768]{1,0:T(8,128)(2,1)S(1)}, u32[]{:S(2)}, u32[]{:S(2)}) collective-permute-start(bf16[128,768]{1,0:T(8,128)(2,1)S(1)} %get-tuple-element.26.refs_0_), channel_id=1, source_target_pairs={{0,7},{1,0},{2,1},{3,2},{4,3},{5,4},{6,5},{7,6},{8,15},{9,8},{10,9... | collective-permute-start | bytes 589832 | tf_op jit(solution)/shard_map/ppermute | solution.py:416
  25.6 1.1 multiply_reduce_fusion
  26.8 3.5 %collective-permute-done.2 = f32[1,128]{1,0:T(1,128)S(1)} collective-permute-done((f32[1,128]{1,0:T(1,128)S(1)}, f32[1,128]{1,0:T(1,128)S(1)}, u32[]{:S(2)}, u32[]{:S(2)}) %collective-permute-start.2) | collective-permute-done | bytes 544 | tf_op jit(solution)/shard_map/ppermute | solution.py:426
  30.7 3.2 %collective-permute-start.4 = (bf16[128,768]{1,0:T(8,128)(2,1)S(1)}, bf16[128,768]{1,0:T(8,128)(2,1)S(1)}, u32[]{:S(2)}, u32[]{:S(2)}) collective-permute-start(bf16[128,768]{1,0:T(8,128)(2,1)S(1)} %collective-permute-done.1.refs_2_), channel_id=1, source_target_pairs={{0,7},{1,0},{2,1},{3,2},{4,3},{5,4},{6,5},{7,6},{8,15},{9,8},{10,9... | collective-permute-start | bytes 589832 | tf_op jit(solution)/shard_map/ppermute | solution.py:416
  34.0 1.9 collective-permute-start.5
  35.9 3.8 %collective-permute-done.5 = f32[1,128]{1,0:T(1,128)S(1)} collective-permute-done((f32[1,128]{1,0:T(1,128)S(1)}, f32[1,128]{1,0:T(1,128)S(1)}, u32[]{:S(2)}, u32[]{:S(2)}) %collective-permute-start.5) | collective-permute-done | bytes 544 | tf_op jit(solution)/shard_map/ppermute | solution.py:426
  39.6 1.9 collective-permute-start.6
  41.5 1.4 collective-permute-start.7
  42.9 3.1 %collective-permute-start.8 = (f32[1,128]{1,0:T(1,128)S(1)}, f32[1,128]{1,0:T(1,128)S(1)}, u32[]{:S(2)}, u32[]{:S(2)}) collective-permute-start(f32[1,128]{1,0:T(1,128)S(1)} %add.39), channel_id=1, source_target_pairs={{0,4},{1,5},{2,6},{3,7},{4,0},{5,1},{6,2},{7,3},{8,12},{9,13},{10,... | collective-permute-start | bytes 1544 | tf_op jit(solution)/shard_map/ppermute | solution.py:426
  45.9 4.4 %collective-permute-done.8 = f32[1,128]{1,0:T(1,128)S(1)} collective-permute-done((f32[1,128]{1,0:T(1,128)S(1)}, f32[1,128]{1,0:T(1,128)S(1)}, u32[]{:S(2)}, u32[]{:S(2)}) %collective-permute-start.8) | collective-permute-done | bytes 544 | tf_op jit(solution)/shard_map/ppermute | solution.py:426
  50.3 0.8 copy-done.9
  51.2 0.7 collective-permute-start.9
  52.0 2.6 collective-permute-start.10
  54.6 2.6 collective-permute-done.9.refs_7_
  57.1 0.7 copy-done.6
  57.8 1.7 shard_map.104
  59.6 2.0 copy-done
  61.6 7.4 %all-to-all-start = ((bf16[32,8,7808]{2,1,0:T(8,128)(2,1)}), bf16[32,8,7808]{2,1,0:T(8,128)(2,1)}, u32[]{:S(2)}, u32[]{:S(2)}) async-start(bf16[32,8,7808]{2,1,0:T(8,128)(2,1)} %bitcast.41), calls=%async_computation | async-start | bytes 7995392 | tf_op jit(solution)/shard_map/all_to_all | solution.py:401
  69.3 47.4 %all-to-all-done = bf16[32,8,7808]{2,1,0:T(8,128)(2,1)} async-done(((bf16[32,8,7808]{2,1,0:T(8,128)(2,1)}), bf16[32,8,7808]{2,1,0:T(8,128)(2,1)}, u32[]{:S(2)}, u32[]{:S(2)}) %all-to-all-start) | async-done | bytes 3997728 | tf_op jit(solution)/shard_map/all_to_all | solution.py:401
  116.7 2.0 copy-done.1
  118.8 12.0 %shard_map.105 = (bf16[320,256]{1,0:T(8,128)(2,1)S(1)}, bf16[320,256]{1,0:T(8,128)(2,1)S(1)}, bf16[320,256]{1,0:T(8,128)(2,1)S(1)}, bf16[256,128]{1,0:T(8,128)(2,1)S(1)}) custom-call(s32[1]{0:T(128)} %bitcast.me, bf16[256,7808]{1,0:T(8,128)(2,1)} %bitcast.4.scales.main.rest, bf16[8,256,1280]{2,1,0:T(8,128)(2,1)} %bitcast.50, ...), custom_call_target="tpu_custom_call" | custom-call | tf_op jit(solution)/shard_map/pallas_call | solution.py:259
  130.8 12.5 %shard_map.106 = (bf16[8,256,1280]{2,1,0:T(8,128)(2,1)}, bf16[256,7808]{1,0:T(8,128)(2,1)}) custom-call(s32[1]{0:T(128)} %bitcast.me, bf16[320,256]{1,0:T(8,128)(2,1)S(1)} %get-tuple-element.38.hid, bf16[320,256]{1,0:T(8,128)(2,1)S(1)} %get-tuple-element.39.gate_g, bf16[320,256]{1,0:T(8,128)(2,1)S(1)} %get-tuple-element.40.up_g, ...), custom_call_target="tpu_custom_call" | custom-call | tf_op jit(solution)/shard_map/pallas_call | solution.py:318
  143.3 55.5 %all_to_all.20 = bf16[32,8,7808]{2,1,0:T(8,128)(2,1)S(1)} all-to-all(bf16[32,8,7808]{2,1,0:T(8,128)(2,1)} %bitcast.51), channel_id=1, replica_groups=mesh['region'=32,'local'=8] {'region'}, dimensions={0} | all-to-all | bytes 7995392 | tf_op jit(solution)/shard_map/all_to_all | solution.py:401
  198.9 2.2 shard_map.107
  201.2 3.3 %collective-permute-start.15 = (bf16[64,768]{1,0:T(8,128)(2,1)S(1)}, bf16[64,768]{1,0:T(8,128)(2,1)S(1)}, u32[]{:S(2)}, u32[]{:S(2)}) collective-permute-start(bf16[64,768]{1,0:T(8,128)(2,1)S(1)} %get-tuple-element.52), channel_id=1, source_target_pairs={{0,7},{1,0},{2,1},{3,2},{4,3},{5,4},{6,5},{7,6},{8,15},{9,8},{10,9... | collective-permute-start | bytes 294920 | tf_op jit(solution)/shard_map/ppermute | solution.py:416
  204.5 4.3 %collective-permute-done.15 = bf16[64,768]{1,0:T(8,128)(2,1)S(1)} collective-permute-done((bf16[64,768]{1,0:T(8,128)(2,1)S(1)}, bf16[64,768]{1,0:T(8,128)(2,1)S(1)}, u32[]{:S(2)}, u32[]{:S(2)}) %collective-permute-start.15) | collective-permute-done | bytes 98336 | tf_op jit(solution)/shard_map/ppermute | solution.py:416
  208.8 2.1 collective-permute-done.11
  211.0 1.2 collective-permute-start.16
  212.2 1.0 collective-permute-start.12
  213.2 4.4 %collective-permute-done.16 = bf16[128,768]{1,0:T(8,128)(2,1)S(1)} collective-permute-done((bf16[128,768]{1,0:T(8,128)(2,1)S(1)}, bf16[128,768]{1,0:T(8,128)(2,1)S(1)}, u32[]{:S(2)}, u32[]{:S(2)}) %collective-permute-start.16) | collective-permute-done | bytes 196640 | tf_op jit(solution)/shard_map/ppermute | solution.py:416
  217.6 2.8 %collective-permute-start.17 = (bf16[128,768]{1,0:T(8,128)(2,1)S(1)}, bf16[128,768]{1,0:T(8,128)(2,1)S(1)}, u32[]{:S(2)}, u32[]{:S(2)}) collective-permute-start(bf16[128,768]{1,0:T(8,128)(2,1)S(1)} %fusion), channel_id=1, source_target_pairs={{0,7},{1,0},{2,1},{3,2},{4,3},{5,4},{6,5},{7,6},{8,15},{9,8},{10,9... | collective-permute-start | bytes 589832 | tf_op jit(solution)/shard_map/ppermute | solution.py:416
  220.4 6.1 %all-to-all-start.2 = ((bf16[32,8,1280]{2,1,0:T(8,128)(2,1)}), bf16[32,8,1280]{2,1,0:T(8,128)(2,1)S(1)}, u32[]{:S(2)}, u32[]{:S(2)}) async-start(bf16[32,8,1280]{2,1,0:T(8,128)(2,1)} %bitcast.53), calls=%async_computation.3 | async-start | bytes 1310720 | tf_op jit(solution)/shard_map/all_to_all | solution.py:401
  226.6 0.6 collective-permute-start.13
  227.2 2.7 %collective-permute-start.18 = (bf16[128,768]{1,0:T(8,128)(2,1)S(1)}, bf16[128,768]{1,0:T(8,128)(2,1)S(1)}, u32[]{:S(2)}, u32[]{:S(2)}) collective-permute-start(bf16[128,768]{1,0:T(8,128)(2,1)S(1)} %get-tuple-element.49), channel_id=1, source_target_pairs={{0,7},{1,0},{2,1},{3,2},{4,3},{5,4},{6,5},{7,6},{8,15},{9,8},{10,9... | collective-permute-start | bytes 589832 | tf_op jit(solution)/shard_map/ppermute | solution.py:416
  229.9 4.9 %collective-permute-done.13 = bf16[128,768]{1,0:T(8,128)(2,1)S(1)} collective-permute-done((bf16[128,768]{1,0:T(8,128)(2,1)S(1)}, bf16[128,768]{1,0:T(8,128)(2,1)S(1)}, u32[]{:S(2)}, u32[]{:S(2)}) %collective-permute-start.13) | collective-permute-done | bytes 196640 | tf_op jit(solution)/shard_map/ppermute | solution.py:416
  235.1 3.9 %collective-permute-done.19 = f32[8,128]{1,0:T(8,128)S(1)} collective-permute-done((f32[8,128]{1,0:T(8,128)S(1)}, f32[8,128]{1,0:T(8,128)S(1)}, u32[]{:S(2)}, u32[]{:S(2)}) %collective-permute-start.19) | collective-permute-done | bytes 4128 | tf_op jit(solution)/shard_map/ppermute | solution.py:409
  239.0 2.7 %collective-permute-start.20 = (f32[8,128]{1,0:T(8,128)S(1)}, f32[8,128]{1,0:T(8,128)S(1)}, u32[]{:S(2)}, u32[]{:S(2)}) collective-permute-start(f32[8,128]{1,0:T(8,128)S(1)} %add.47), channel_id=1, source_target_pairs={{0,2},{1,3},{2,0},{3,1},{4,6},{5,7},{6,4},{7,5},{8,10},{9,11},{10,... | collective-permute-start | bytes 12296 | tf_op jit(solution)/shard_map/ppermute | solution.py:409
  241.7 1.8 collective-permute-done.20
  243.5 4.0 %collective-permute-start.21 = (f32[8,128]{1,0:T(8,128)S(1)}, f32[8,128]{1,0:T(8,128)S(1)}, u32[]{:S(2)}, u32[]{:S(2)}) collective-permute-start(f32[8,128]{1,0:T(8,128)S(1)} %add.48), channel_id=1, source_target_pairs={{0,4},{1,5},{2,6},{3,7},{4,0},{5,1},{6,2},{7,3},{8,12},{9,13},{10,... | collective-permute-start | bytes 12296 | tf_op jit(solution)/shard_map/ppermute | solution.py:409
  247.6 3.5 %collective-permute-done.21 = f32[8,128]{1,0:T(8,128)S(1)} collective-permute-done((f32[8,128]{1,0:T(8,128)S(1)}, f32[8,128]{1,0:T(8,128)S(1)}, u32[]{:S(2)}, u32[]{:S(2)}) %collective-permute-start.21) | collective-permute-done | bytes 4128 | tf_op jit(solution)/shard_map/ppermute | solution.py:409
  251.1 1.4 shard_map.108
  (52 shorter events, 1.4 us)
Async XLA Ops:
  7.9 0.9 copy-start.2
  8.8 0.9 copy-start.4
  9.7 0.7 copy-start.5
  11.9 38.4 %all-to-all-start.1 = ((bf16[32,8,1280]{2,1,0:T(8,128)(2,1)}), bf16[32,8,1280]{2,1,0:T(8,128)(2,1)S(1)}, u32[]{:S(2)}, u32[]{:S(2)}) async-start(bf16[32,8,1280]{2,1,0:T(8,128)(2,1)} %bitcast.5), calls=%async_computation.1 | async-start | bytes 1310720 | tf_op jit(solution)/shard_map/all_to_all | solution.py:401
  19.5 97.2 %all-gather.3.cloned.1.call-start = ((), (), s32[]{:S(2)}) async-start(), calls=%async_computation.6 | async-start | bytes 5898240 | tf_op jit(solution)/shard_map/all_gather | solution.py:464
  19.6 11.2 %collective-permute-start = (bf16[128,768]{1,0:T(8,128)(2,1)S(1)}, bf16[128,768]{1,0:T(8,128)(2,1)S(1)}, u32[]{:S(2)}, u32[]{:S(2)}) collective-permute-start(bf16[128,768]{1,0:T(8,128)(2,1)S(1)} %get-tuple-element.26.refs_0_), channel_id=1, source_target_pairs={{0,1},{1,2},{2,3},{3,4},{4,5},{5,6},{6,7},{7,0},{8,9},{9,10},{10,1... | collective-permute-start | bytes 589832 | tf_op jit(solution)/shard_map/ppermute | solution.py:416
  21.6 9.2 %collective-permute-start.1 = (bf16[128,768]{1,0:T(8,128)(2,1)S(1)}, bf16[128,768]{1,0:T(8,128)(2,1)S(1)}, u32[]{:S(2)}, u32[]{:S(2)}) collective-permute-start(bf16[128,768]{1,0:T(8,128)(2,1)S(1)} %get-tuple-element.26.refs_0_), channel_id=1, source_target_pairs={{0,7},{1,0},{2,1},{3,2},{4,3},{5,4},{6,5},{7,6},{8,15},{9,8},{10,9... | collective-permute-start | bytes 589832 | tf_op jit(solution)/shard_map/ppermute | solution.py:416
  26.7 3.6 %collective-permute-start.2 = (f32[1,128]{1,0:T(1,128)S(1)}, f32[1,128]{1,0:T(1,128)S(1)}, u32[]{:S(2)}, u32[]{:S(2)}) collective-permute-start(f32[1,128]{1,0:T(1,128)S(1)} %bitcast.54), channel_id=1, source_target_pairs={{0,1},{1,0},{2,3},{3,2},{4,5},{5,4},{6,7},{7,6},{8,9},{9,8},{10,11... | collective-permute-start | bytes 1544 | tf_op jit(solution)/shard_map/ppermute | solution.py:426
  30.7 8.9 %collective-permute-start.3 = (bf16[128,768]{1,0:T(8,128)(2,1)S(1)}, bf16[128,768]{1,0:T(8,128)(2,1)S(1)}, u32[]{:S(2)}, u32[]{:S(2)}) collective-permute-start(bf16[128,768]{1,0:T(8,128)(2,1)S(1)} %collective-permute-done.refs_1_), channel_id=1, source_target_pairs={{0,1},{1,2},{2,3},{3,4},{4,5},{5,6},{6,7},{7,0},{8,9},{9,10},{10,1... | collective-permute-start | bytes 589832 | tf_op jit(solution)/shard_map/ppermute | solution.py:416
  30.7 8.9 %collective-permute-start.4 = (bf16[128,768]{1,0:T(8,128)(2,1)S(1)}, bf16[128,768]{1,0:T(8,128)(2,1)S(1)}, u32[]{:S(2)}, u32[]{:S(2)}) collective-permute-start(bf16[128,768]{1,0:T(8,128)(2,1)S(1)} %collective-permute-done.1.refs_2_), channel_id=1, source_target_pairs={{0,7},{1,0},{2,1},{3,2},{4,3},{5,4},{6,5},{7,6},{8,15},{9,8},{10,9... | collective-permute-start | bytes 589832 | tf_op jit(solution)/shard_map/ppermute | solution.py:416
  34.0 5.7 %collective-permute-start.5 = (f32[1,128]{1,0:T(1,128)S(1)}, f32[1,128]{1,0:T(1,128)S(1)}, u32[]{:S(2)}, u32[]{:S(2)}) collective-permute-start(f32[1,128]{1,0:T(1,128)S(1)} %bitcast_add_fusion), channel_id=1, source_target_pairs={{0,2},{1,3},{2,0},{3,1},{4,6},{5,7},{6,4},{7,5},{8,10},{9,11},{10,... | collective-permute-start | bytes 1544 | tf_op jit(solution)/shard_map/ppermute | solution.py:426
  39.6 10.7 %collective-permute-start.6 = (bf16[128,768]{1,0:T(8,128)(2,1)S(1)}, bf16[128,768]{1,0:T(8,128)(2,1)S(1)}, u32[]{:S(2)}, u32[]{:S(2)}) collective-permute-start(bf16[128,768]{1,0:T(8,128)(2,1)S(1)} %collective-permute-done.3.refs_3_), channel_id=1, source_target_pairs={{0,1},{1,2},{2,3},{3,4},{4,5},{5,6},{6,7},{7,0},{8,9},{9,10},{10,1... | collective-permute-start | bytes 589832 | tf_op jit(solution)/shard_map/ppermute | solution.py:416
  41.5 8.8 %collective-permute-start.7 = (bf16[128,768]{1,0:T(8,128)(2,1)S(1)}, bf16[128,768]{1,0:T(8,128)(2,1)S(1)}, u32[]{:S(2)}, u32[]{:S(2)}) collective-permute-start(bf16[128,768]{1,0:T(8,128)(2,1)S(1)} %collective-permute-done.4.refs_4_), channel_id=1, source_target_pairs={{0,7},{1,0},{2,1},{3,2},{4,3},{5,4},{6,5},{7,6},{8,15},{9,8},{10,9... | collective-permute-start | bytes 589832 | tf_op jit(solution)/shard_map/ppermute | solution.py:416
  42.9 7.4 %collective-permute-start.8 = (f32[1,128]{1,0:T(1,128)S(1)}, f32[1,128]{1,0:T(1,128)S(1)}, u32[]{:S(2)}, u32[]{:S(2)}) collective-permute-start(f32[1,128]{1,0:T(1,128)S(1)} %add.39), channel_id=1, source_target_pairs={{0,4},{1,5},{2,6},{3,7},{4,0},{5,1},{6,2},{7,3},{8,12},{9,13},{10,... | collective-permute-start | bytes 1544 | tf_op jit(solution)/shard_map/ppermute | solution.py:426
  50.3 0.8 copy-start.9
  51.2 5.9 %collective-permute-start.9 = (bf16[64,768]{1,0:T(8,128)(2,1)S(1)}, bf16[64,768]{1,0:T(8,128)(2,1)S(1)}, u32[]{:S(2)}, u32[]{:S(2)}) collective-permute-start(bf16[64,768]{1,0:T(8,128)(2,1)S(1)} %slice.36), channel_id=1, source_target_pairs={{0,1},{1,2},{2,3},{3,4},{4,5},{5,6},{6,7},{7,0},{8,9},{9,10},{10,1... | collective-permute-start | bytes 294920 | tf_op jit(solution)/shard_map/ppermute | solution.py:416
  52.0 5.2 %collective-permute-start.10 = (bf16[64,768]{1,0:T(8,128)(2,1)S(1)}, bf16[64,768]{1,0:T(8,128)(2,1)S(1)}, u32[]{:S(2)}, u32[]{:S(2)}) collective-permute-start(bf16[64,768]{1,0:T(8,128)(2,1)S(1)} %slice.37), channel_id=1, source_target_pairs={{0,7},{1,0},{2,1},{3,2},{4,3},{5,4},{6,5},{7,6},{8,15},{9,8},{10,9... | collective-permute-start | bytes 294920 | tf_op jit(solution)/shard_map/ppermute | solution.py:416
  57.1 0.7 copy-start.6
  59.6 2.0 copy-start
  61.6 55.1 %all-to-all-start = ((bf16[32,8,7808]{2,1,0:T(8,128)(2,1)}), bf16[32,8,7808]{2,1,0:T(8,128)(2,1)}, u32[]{:S(2)}, u32[]{:S(2)}) async-start(bf16[32,8,7808]{2,1,0:T(8,128)(2,1)} %bitcast.41), calls=%async_computation | async-start | bytes 7995392 | tf_op jit(solution)/shard_map/all_to_all | solution.py:401
  69.0 151.4 %reduce-scatter.2.cloned.1.call-start = ((), (), s32[]{:S(2)}) async-start(), calls=%async_computation.5 | async-start | bytes 5898240 | tf_op jit(solution)/shard_map/reduce_scatter | solution.py:468
  116.7 2.0 copy-start.1
  143.3 55.6 %copy-start.7 = (s32[128,2]{0,1:T(2,128)S(1)}, s32[128,2]{0,1:T(2,128)}, u32[]{:S(2)}) copy-start(s32[128,2]{0,1:T(2,128)} %param.13) | copy-start | bytes 3076
  143.3 55.6 %copy-start.8 = (f32[128,2]{0,1:T(2,128)S(1)}, f32[128,2]{0,1:T(2,128)}, u32[]{:S(2)}) copy-start(f32[128,2]{0,1:T(2,128)} %param.14) | copy-start | bytes 3076
  201.1 49.9 %copy-start.3 = (bf16[128,896]{1,0:T(8,128)(2,1)S(1)}, bf16[128,896]{1,0:T(8,128)(2,1)}, u32[]{:S(2)}) copy-start(bf16[128,896]{1,0:T(8,128)(2,1)} %tok.3) | copy-start | bytes 688132
  201.2 7.7 %collective-permute-start.15 = (bf16[64,768]{1,0:T(8,128)(2,1)S(1)}, bf16[64,768]{1,0:T(8,128)(2,1)S(1)}, u32[]{:S(2)}, u32[]{:S(2)}) collective-permute-start(bf16[64,768]{1,0:T(8,128)(2,1)S(1)} %get-tuple-element.52), channel_id=1, source_target_pairs={{0,7},{1,0},{2,1},{3,2},{4,3},{5,4},{6,5},{7,6},{8,15},{9,8},{10,9... | collective-permute-start | bytes 294920 | tf_op jit(solution)/shard_map/ppermute | solution.py:416
  204.5 6.4 %collective-permute-start.11 = (bf16[64,768]{1,0:T(8,128)(2,1)S(1)}, bf16[64,768]{1,0:T(8,128)(2,1)S(1)}, u32[]{:S(2)}, u32[]{:S(2)}) collective-permute-start(bf16[64,768]{1,0:T(8,128)(2,1)S(1)} %get-tuple-element.54), channel_id=1, source_target_pairs={{0,1},{1,2},{2,3},{3,4},{4,5},{5,6},{6,7},{7,0},{8,9},{9,10},{10,1... | collective-permute-start | bytes 294920 | tf_op jit(solution)/shard_map/ppermute | solution.py:416
  211.0 6.6 %collective-permute-start.16 = (bf16[128,768]{1,0:T(8,128)(2,1)S(1)}, bf16[128,768]{1,0:T(8,128)(2,1)S(1)}, u32[]{:S(2)}, u32[]{:S(2)}) collective-permute-start(bf16[128,768]{1,0:T(8,128)(2,1)S(1)} %pad_maximum_fusion.1), channel_id=1, source_target_pairs={{0,7},{1,0},{2,1},{3,2},{4,3},{5,4},{6,5},{7,6},{8,15},{9,8},{10,9... | collective-permute-start | bytes 589832 | tf_op jit(solution)/shard_map/ppermute | solution.py:416
  212.2 14.3 %collective-permute-start.12 = (bf16[128,768]{1,0:T(8,128)(2,1)S(1)}, bf16[128,768]{1,0:T(8,128)(2,1)S(1)}, u32[]{:S(2)}, u32[]{:S(2)}) collective-permute-start(bf16[128,768]{1,0:T(8,128)(2,1)S(1)} %pad_maximum_fusion), channel_id=1, source_target_pairs={{0,1},{1,2},{2,3},{3,4},{4,5},{5,6},{6,7},{7,0},{8,9},{9,10},{10,1... | collective-permute-start | bytes 589832 | tf_op jit(solution)/shard_map/ppermute | solution.py:416
  217.6 8.9 %collective-permute-start.17 = (bf16[128,768]{1,0:T(8,128)(2,1)S(1)}, bf16[128,768]{1,0:T(8,128)(2,1)S(1)}, u32[]{:S(2)}, u32[]{:S(2)}) collective-permute-start(bf16[128,768]{1,0:T(8,128)(2,1)S(1)} %fusion), channel_id=1, source_target_pairs={{0,7},{1,0},{2,1},{3,2},{4,3},{5,4},{6,5},{7,6},{8,15},{9,8},{10,9... | collective-permute-start | bytes 589832 | tf_op jit(solution)/shard_map/ppermute | solution.py:416
  220.4 30.7 %all-to-all-start.2 = ((bf16[32,8,1280]{2,1,0:T(8,128)(2,1)}), bf16[32,8,1280]{2,1,0:T(8,128)(2,1)S(1)}, u32[]{:S(2)}, u32[]{:S(2)}) async-start(bf16[32,8,1280]{2,1,0:T(8,128)(2,1)} %bitcast.53), calls=%async_computation.3 | async-start | bytes 1310720 | tf_op jit(solution)/shard_map/all_to_all | solution.py:401
  226.6 8.2 %collective-permute-start.13 = (bf16[128,768]{1,0:T(8,128)(2,1)S(1)}, bf16[128,768]{1,0:T(8,128)(2,1)S(1)}, u32[]{:S(2)}, u32[]{:S(2)}) collective-permute-start(bf16[128,768]{1,0:T(8,128)(2,1)S(1)} %get-tuple-element.50), channel_id=1, source_target_pairs={{0,1},{1,2},{2,3},{3,4},{4,5},{5,6},{6,7},{7,0},{8,9},{9,10},{10,1... | collective-permute-start | bytes 589832 | tf_op jit(solution)/shard_map/ppermute | solution.py:416
  227.2 23.8 %collective-permute-start.18 = (bf16[128,768]{1,0:T(8,128)(2,1)S(1)}, bf16[128,768]{1,0:T(8,128)(2,1)S(1)}, u32[]{:S(2)}, u32[]{:S(2)}) collective-permute-start(bf16[128,768]{1,0:T(8,128)(2,1)S(1)} %get-tuple-element.49), channel_id=1, source_target_pairs={{0,7},{1,0},{2,1},{3,2},{4,3},{5,4},{6,5},{7,6},{8,15},{9,8},{10,9... | collective-permute-start | bytes 589832 | tf_op jit(solution)/shard_map/ppermute | solution.py:416
  234.9 16.1 %collective-permute-start.14 = (bf16[128,768]{1,0:T(8,128)(2,1)S(1)}, bf16[128,768]{1,0:T(8,128)(2,1)S(1)}, u32[]{:S(2)}, u32[]{:S(2)}) collective-permute-start(bf16[128,768]{1,0:T(8,128)(2,1)S(1)} %fusion.3), channel_id=1, source_target_pairs={{0,1},{1,2},{2,3},{3,4},{4,5},{5,6},{6,7},{7,0},{8,9},{9,10},{10,1... | collective-permute-start | bytes 589832 | tf_op jit(solution)/shard_map/ppermute | solution.py:416
  235.0 4.0 %collective-permute-start.19 = (f32[8,128]{1,0:T(8,128)S(1)}, f32[8,128]{1,0:T(8,128)S(1)}, u32[]{:S(2)}, u32[]{:S(2)}) collective-permute-start(f32[8,128]{1,0:T(8,128)S(1)} %get-tuple-element.45), channel_id=1, source_target_pairs={{0,1},{1,0},{2,3},{3,2},{4,5},{5,4},{6,7},{7,6},{8,9},{9,8},{10,11... | collective-permute-start | bytes 12296 | tf_op jit(solution)/shard_map/ppermute | solution.py:409
  239.0 4.5 %collective-permute-start.20 = (f32[8,128]{1,0:T(8,128)S(1)}, f32[8,128]{1,0:T(8,128)S(1)}, u32[]{:S(2)}, u32[]{:S(2)}) collective-permute-start(f32[8,128]{1,0:T(8,128)S(1)} %add.47), channel_id=1, source_target_pairs={{0,2},{1,3},{2,0},{3,1},{4,6},{5,7},{6,4},{7,5},{8,10},{9,11},{10,... | collective-permute-start | bytes 12296 | tf_op jit(solution)/shard_map/ppermute | solution.py:409
  243.5 7.5 %collective-permute-start.21 = (f32[8,128]{1,0:T(8,128)S(1)}, f32[8,128]{1,0:T(8,128)S(1)}, u32[]{:S(2)}, u32[]{:S(2)}) collective-permute-start(f32[8,128]{1,0:T(8,128)S(1)} %add.48), channel_id=1, source_target_pairs={{0,4},{1,5},{2,6},{3,7},{4,0},{5,1},{6,2},{7,3},{8,12},{9,13},{10,... | collective-permute-start | bytes 12296 | tf_op jit(solution)/shard_map/ppermute | solution.py:409
Sparse Core Ops, SparseCore 0:
  51.3 63.2 all-gather.2
  143.4 66.5 reduce-scatter.1

commit v4 on v3

--- a/solution.py
+++ b/solution.py
@@ -11,7 +11,9 @@
 F32 = jnp.float32
 NT = (((1,), (1,)), ((), ()))
 TN = (((0,), (0,)), ((), ()))
-VMEM_LIMIT = 48 * 1024 * 1024
+VMEM_MOST = 63 * 1024 * 1024
+VMEM_SOME = 40 * 1024 * 1024
+EXTRA = 16
 EARLY = 384
 
 
@@ -27,8 +29,8 @@
     return lax.dot_general(a, b, dims, precision=precision, preferred_element_type=F32)
 
 
-def params(**kw):
-    return pltpu.CompilerParams(vmem_limit_bytes=VMEM_LIMIT, **kw)
+def params(limit=VMEM_MOST):
+    return pltpu.CompilerParams(vmem_limit_bytes=limit)
 
 
 def whole(shape):
@@ -103,28 +105,17 @@
     return [n & main for n in named], [n & late for n in named]
 
 
-def pack_kernel(regions, tok, gain, grad, routes, out, early):
-    at = placed(routes[...], regions)
-    pick = (at[0] | at[1]).astype(F32).astype(BF)
-    late = out.shape[1] * 2 // 5
-    scaled = (tok[...].astype(F32) * gain[...]).astype(BF)
-    rows = dot(pick, jnp.concatenate([scaled[:, :late], grad[:, :late]], axis=1)).astype(BF)
-    cut = 8 * regions
-    out[...] = encode(rows[:cut], rows[cut:], fold_matrix(regions))
-    early[...] = jnp.concatenate([scaled[:, late:], grad[:, late:]], axis=1)
-
-
-def pack(tok, gain, grad, routes, regions):
-    count, width = tok.shape
-    shapes = [
-        jax.ShapeDtypeStruct((8 * regions, packed_lanes(width - EARLY)), BF),
-        jax.ShapeDtypeStruct((count, 2 * EARLY), BF),
-    ]
-    return once(functools.partial(pack_kernel, regions), shapes, tok, gain, grad, routes)
-
-
-def inverse(squares, full):
-    return lax.rsqrt(squares / full + 1e-06)
+def once(kernel, out_shape, *operands, limit=VMEM_SOME):
+    many = isinstance(out_shape, list)
+    specs = [whole(shape.shape) for shape in (out_shape if many else [out_shape])]
+    return pl.pallas_call(
+        kernel,
+        grid=(1,),
+        in_specs=[whole(operand.shape) for operand in operands],
+        out_specs=specs if many else specs[0],
+        out_shape=out_shape,
+        compiler_params=params(limit),
+    )(*operands)
 
 
 def triple(value):
@@ -148,7 +139,45 @@
     return block[:, at : at + 1] + block[:, at + 1 : at + 2] + block[:, at + 2 : at + 3]
 
 
-def pack_early_kernel(regions, depth, full, routes, squares, *refs):
+def in_rows(rows, lanes):
+    count = rows[0].shape[1]
+    row = lax.broadcasted_iota(jnp.int32, (EXTRA, count), 0)
+    out = jnp.zeros((EXTRA, count), F32)
+    for at, value in enumerate(rows):
+        out = jnp.where(row == at, value.astype(F32), out)
+    out = out.astype(BF)
+    return jnp.concatenate([out, jnp.zeros((EXTRA, lanes - count), BF)], axis=1)
+
+
+def pack_kernel(regions, tok, gain, grad, routes, out, early):
+    at = placed(routes[...], regions)
+    pick = (at[0] | at[1]).astype(F32).astype(BF)
+    late = out.shape[1] * 2 // 5
+    count = tok.shape[0]
+    wide = tok[...].astype(F32)
+    scaled = (wide * gain[...]).astype(BF)
+    rows = dot(pick, jnp.concatenate([scaled[:, :late], grad[:, :late]], axis=1)).astype(BF)
+    cut = 8 * regions
+    out[...] = encode(rows[:cut], rows[cut:], fold_matrix(regions))
+    early[:count] = jnp.concatenate([scaled[:, late:], grad[:, late:]], axis=1)
+    squares = jnp.broadcast_to(jnp.sum(wide * wide, axis=1, keepdims=True), (count, 128))
+    early[count:] = in_rows(triple(jnp.transpose(squares)[0:1]), early.shape[1])
+
+
+def pack(tok, gain, grad, routes, regions):
+    count, width = tok.shape
+    shapes = [
+        jax.ShapeDtypeStruct((8 * regions, packed_lanes(width - EARLY)), BF),
+        jax.ShapeDtypeStruct((count + EXTRA, 2 * EARLY), BF),
+    ]
+    return once(functools.partial(pack_kernel, regions), shapes, tok, gain, grad, routes, limit=VMEM_MOST)
+
+
+def inverse(squares, full):
+    return lax.rsqrt(squares / full + 1e-06)
+
+
+def pack_early_kernel(regions, depth, full, routes, *refs):
     blocks, out = refs[:-1], refs[-1]
     lanes = blocks[0].shape[1]
     early = {0: blocks[0][...]}
@@ -161,41 +190,32 @@
     pick = (at[0] | at[1]).astype(F32).astype(BF)
     cut = 8 * regions
     rests = []
+    count = routes.shape[1]
+    squares = 0.0
     for z in range(depth):
-        rows = dot(pick, early[z]).astype(BF)
+        rows = dot(pick, early[z][:count]).astype(BF)
+        extra = early[z][count:, :count].astype(F32)
+        squares = squares + extra[0:1] + extra[1:2] + extra[2:3]
         out[:, z * lanes : (z + 1) * lanes] = rows[:cut]
         rests.append(rows[cut:])
     for half in range(depth // 4):
         stacked = jnp.concatenate([rests[part * (depth // 4) + half] for part in range(4)], axis=0)
         at_lane = (depth + half) * lanes
         out[:, at_lane : at_lane + lanes] = dot(fold_matrix(regions), stacked, TN).astype(BF)
-    inv = inverse(squares[...], full)
+    inv = inverse(squares, full)
     columns = []
     for found in placed_packed(routes[...], regions):
         columns += triple(jnp.sum(jnp.where(found[0] | found[1], inv, 0.0), axis=1, keepdims=True))
     out[:, -128:] = in_lanes(columns, cut)
 
 
-def once(kernel, out_shape, *operands):
-    many = isinstance(out_shape, list)
-    specs = [whole(shape.shape) for shape in (out_shape if many else [out_shape])]
-    return pl.pallas_call(
-        kernel,
-        grid=(1,),
-        in_specs=[whole(operand.shape) for operand in operands],
-        out_specs=specs if many else specs[0],
-        out_shape=out_shape,
-        compiler_params=params(),
-    )(*operands)
-
-
 def early_shape(regions, depth):
     return (8 * regions, 2 * EARLY * depth * 5 // 4 + 128)
 
 
-def pack_early(blocks, squares, routes, regions, depth, full):
+def pack_early(blocks, routes, regions, depth, full):
     shape = jax.ShapeDtypeStruct(early_shape(regions, depth), BF)
-    return once(functools.partial(pack_early_kernel, regions, depth, full), shape, routes, squares, *blocks)
+    return once(functools.partial(pack_early_kernel, regions, depth, full), shape, routes, *blocks)
 
 
 def relative_specs(width, units, depth):
@@ -338,8 +358,7 @@
         part = jnp.where(main[k], from_lanes(here, 3), 0.0) + jnp.where(late[k], from_lanes(here, 9), 0.0)
         parts.append(jnp.sum(comb, axis=0, keepdims=True))
         inner = inner + weights[k : k + 1, :] * jnp.sum(part, axis=0, keepdims=True)
-    row = lax.broadcasted_iota(jnp.int32, (8, routes.shape[1]), 0)
-    return jnp.where(row == 0, parts[0], jnp.where(row == 1, parts[1], jnp.where(row == 2, inner, 0.0)))
+    return parts + [inner]
 
 
 def combining(routes, weights, regions):
@@ -349,51 +368,124 @@
     return high, (weight - high.astype(F32)).astype(BF)
 
 
-def combine_early_kernel(regions, back, routes, weights, out, scal_out):
-    scal_out[...] = scalars(back[:, -128:], routes[...], weights[...], regions)
-    depth, _, lanes = out.shape
+def combine_early_kernel(regions, squares, back, routes, weights, out, right, left):
+    depth, rows_out, lanes = out.shape
+    count = rows_out - EXTRA
     high, low = combining(routes[...], weights[...], regions)
     quarter = depth // 4
-    rests = [dot(fold_matrix(regions), back[:, (depth + half) * lanes : (depth + half + 1) * lanes]).astype(BF) for half in range(quarter)]
     few = 2 * regions
+    values = []
+    for value in scalars(back[:, -128:], routes[...], weights[...], regions):
+        values += triple(value)
+    count = routes.shape[1]
+    values += [squares[at : at + 1, :count] for at in range(3)]
+    extra = in_rows(values, lanes)
+    fold = fold_matrix(regions)
+    rests = [dot(fold, back[:, (depth + half) * lanes : (depth + half + 1) * lanes]).astype(BF) for half in range(quarter)]
     for z in range(depth):
         part = z // quarter
         rest = rests[z % quarter][part * few : (part + 1) * few]
         rows = jnp.concatenate([back[:, z * lanes : (z + 1) * lanes], rest], axis=0)
-        out[z] = (dot(high, rows, TN) + dot(low, rows, TN)).astype(BF)
-
-
-def combine_early(back, routes, weights, regions, depth):
+        share = (dot(high, rows, TN) + dot(low, rows, TN)).astype(BF)
+        out[z, :count] = share
+        out[z, count:] = extra
+        if z == depth // 2:
+            right[...] = jnp.concatenate([share[: count // 2], extra], axis=0)
+            left[...] = jnp.concatenate([share[count // 2 :], extra], axis=0)
+
+
+def combine_early(early, back, routes, weights, regions, depth):
     count = routes.shape[1]
-    shapes = [jax.ShapeDtypeStruct((depth, count, 2 * EARLY), BF), jax.ShapeDtypeStruct((8, count), F32)]
-    return once(functools.partial(combine_early_kernel, regions), shapes, back, routes, weights)
-
-
-def final_kernel(regions, full, back, own, left, right, tok, gain, squares, sums, routes, weights, moe_out, grad_out, comb_out):
+    squares = early[count:]
+    lanes = 2 * EARLY
+    shapes = [
+        jax.ShapeDtypeStruct((depth, count + EXTRA, lanes), BF),
+        jax.ShapeDtypeStruct((count // 2 + EXTRA, lanes), BF),
+        jax.ShapeDtypeStruct((count // 2 + EXTRA, lanes), BF),
+    ]
+    return once(functools.partial(combine_early_kernel, regions), shapes, squares, back, routes, weights)
+
+
+def forward_kernel(for_right, for_left, right, left, right_out, left_out):
+    rows = for_right.shape[1]
+    count = rows - EXTRA
+    arrived = right.shape[0] - EXTRA
+    for own, got, out, start in ((for_right, right, right_out, 0), (for_left, left, left_out, count - arrived)):
+        if arrived < count:
+            out[:count] = own[0, :count]
+        spot = slice(start, start + arrived)
+        out[spot] = (own[0, spot].astype(F32) + got[:arrived].astype(F32)).astype(BF)
+        out[count:] = jnp.concatenate([own[0, count:, :128], got[arrived:, :-128]], axis=1)
+
+
+def forward(shares, at, right, left):
+    depth, rows, lanes = shares.shape
+    shape = jax.ShapeDtypeStruct((rows, lanes), BF)
+    return pl.pallas_call(
+        forward_kernel,
+        grid=(1,),
+        in_specs=[
+            pl.BlockSpec((1, rows, lanes), lambda _: (at, 0, 0)),
+            pl.BlockSpec((1, rows, lanes), lambda _: (depth - at, 0, 0)),
+            whole(right.shape),
+            whole(left.shape),
+        ],
+        out_specs=[whole((rows, lanes))] * 2,
+        out_shape=[shape, shape],
+        compiler_params=params(VMEM_SOME),
+    )(shares, shares, right, left)
+
+
+def final_kernel(regions, full, depth, me, back, own, right, left, tok, gain, routes, weights, moe_out, grad_out, comb_out, stack):
+    count = tok.shape[0]
     late = tok.shape[1] - EARLY
     high, low = combining(routes[...], weights[...], regions)
     moe, grad = [dot(high, rows, TN) + dot(low, rows, TN) for rows in decode(back[...], late, fold_matrix(regions))]
-    early = own[0].astype(F32) + left[...].astype(F32) + right[...].astype(F32)
+    early = own[0, :count].astype(F32) + right[:count].astype(F32) + left[:count].astype(F32)
     moe_out[:, :late] = moe.astype(BF)
     moe_out[:, late:] = early[:, :EARLY].astype(BF)
-    total = sums[...]
-    comb_out[...] = total[0:2]
-    row = lax.broadcasted_iota(jnp.int32, total.shape, 0)
-    columns = jnp.transpose(jnp.where(row == 3, inverse(squares[...], full), total))
-    inner, inv = columns[:, 2:3], columns[:, 3:4]
+    wide = tok[...].astype(F32)
+    stack[0] = own[0, count:, :count].astype(F32)
+    for away in range(1, depth):
+        source, slot = (left, away - 1) if away <= depth // 2 else (right, depth - away - 1)
+        stack[away] = source[count:, slot * 128 : slot * 128 + count].astype(F32)
+    total = 0.0
+    for z in range(depth):
+        total = total + stack[(z - me[0] + depth) % depth]
+    comb = [total[3 * k : 3 * k + 1] + total[3 * k + 1 : 3 * k + 2] + total[3 * k + 2 : 3 * k + 3] for k in range(3)]
+    comb_out[0:1] = comb[0]
+    comb_out[1:2] = comb[1]
+    inv = inverse(total[9:10] + total[10:11] + total[11:12], full)
+    row = lax.broadcasted_iota(jnp.int32, (8, count), 0)
+    columns = jnp.transpose(jnp.where(row == 0, comb[2], jnp.where(row == 1, inv, 0.0)))
+    inner, inv = columns[:, 0:1], columns[:, 1:2]
     scaled = gain[...] * jnp.concatenate([grad, early[:, EARLY:]], axis=1)
-    grad_out[...] = (inv * scaled - tok[...].astype(F32) * (inv * inv * inv * inner / full)).astype(BF)
-
-
-def final(back, early, tok, gain, squares, sums, routes, weights, regions, full):
+    grad_out[...] = (inv * scaled - wide * (inv * inv * inv * inner / full)).astype(BF)
+
+
+def final(me, back, shares, right, left, tok, gain, routes, weights, regions, full):
     count, width = tok.shape
+    depth, rows, lanes = shares.shape
     shapes = [
         jax.ShapeDtypeStruct((count, width), BF),
         jax.ShapeDtypeStruct((count, width), BF),
         jax.ShapeDtypeStruct((2, count), F32),
     ]
-    kernel = functools.partial(final_kernel, regions, full)
-    return once(kernel, shapes, back, *early, tok, gain, squares, sums, routes, weights)
+    operands = (back, shares, right, left, tok, gain, routes, weights)
+    specs = [whole(operand.shape) for operand in operands]
+    specs[1] = pl.BlockSpec((1, rows, lanes), lambda *_: (0, 0, 0))
+    return pl.pallas_call(
+        functools.partial(final_kernel, regions, full, depth),
+        grid_spec=pltpu.PrefetchScalarGridSpec(
+            num_scalar_prefetch=1,
+            grid=(1,),
+            in_specs=specs,
+            out_specs=[whole(shape.shape) for shape in shapes],
+            scratch_shapes=[pltpu.VMEM((depth, EXTRA, count), F32)],
+        ),
+        out_shape=shapes,
+        compiler_params=params(VMEM_SOME),
+    )(me, *operands)
 
 
 def swap(array, regions):
@@ -402,51 +494,29 @@
     return moved.reshape(array.shape)
 
 
-def add_over_local(array):
-    depth = lax.axis_size("local")
-    step = 1
-    while step < depth:
-        array = array + lax.ppermute(array, "local", [(z, z ^ step) for z in range(depth)])
-        step *= 2
-    return array
-
-
 def hop(array, step):
     depth = lax.axis_size("local")
     return lax.ppermute(array, "local", [(z, (z + step) % depth) for z in range(depth)])
 
 
-def ring_gather(own, squares):
+def ring_gather(own, packed):
     half = lax.axis_size("local") // 2
     low, high = own, own
     blocks = [own]
     for at in range(half - 1):
-        low, high = hop(low, 1), hop(high, -1)
-        if 1 << at < 2 * half:
-            other = lax.ppermute(squares, "local", [(z, z ^ (1 << at)) for z in range(2 * half)])
-            low, high, other = lax.optimization_barrier((low, high, other))
-            squares = squares + other
+        low, high = lax.optimization_barrier((hop(low, 1), hop(high, -1)))
+        if at == 0:
+            low, high, packed = lax.optimization_barrier((low, high, packed))
         blocks += [low, high]
-    at = half - 1
-    while 1 << at < 2 * half:
-        squares = squares + lax.ppermute(squares, "local", [(z, z ^ (1 << at)) for z in range(2 * half)])
-        at += 1
-    cut = own.shape[0] // 2
-    return blocks + [hop(low[:cut], 1), hop(high[cut:], -1)], squares
-
-
-def ring_scatter(shares):
-    depth = shares.shape[0]
-    half = depth // 2
-    cut = shares.shape[1] // 2
-    right, left = hop(shares[half, :cut], 1), hop(shares[half, cut:], -1)
-    add = lambda a, b: (a.astype(F32) + b.astype(F32)).astype(BF)
-    right = jnp.concatenate([add(shares[half - 1, :cut], right), shares[half - 1, cut:]], axis=0)
-    left = jnp.concatenate([shares[half + 1, :cut], add(shares[half + 1, cut:], left)], axis=0)
-    for j in range(half - 2, -1, -1):
+    cut = (own.shape[0] - EXTRA) // 2
+    return blocks + [hop(low[:cut], 1), hop(high[cut:], -1)], packed
+
+
+def ring_scatter(shares, right, left):
+    for at in range(shares.shape[0] // 2 - 1, -1, -1):
         right, left = hop(right, 1), hop(left, -1)
-        if j:
-            right, left = add(shares[j], right), add(shares[depth - j], left)
+        if at:
+            right, left = forward(shares, at, right, left)
     return right, left
 
 
@@ -457,19 +527,17 @@
     full = depth * tokens.shape[1]
     gain = norm_gain.reshape(1, -1)
     routes, weights = routes.T, combine.T
-    wide = tokens.astype(F32)
     packed, early = pack(tokens, gain, grad_out, routes, regions)
-    around, squares = ring_gather(early, jnp.sum(wide * wide, axis=1).reshape(1, -1))
+    around, packed = ring_gather(early, packed)
     arrived, _ = lax.optimization_barrier((swap(packed, regions), around[-3]))
     blocks = lax.all_gather(arrived, "local")
-    rows = swap(pack_early(around, squares, routes, regions, depth, full), regions)
+    rows = swap(pack_early(around, routes, regions, depth, full), regions)
     hidden = hidden_part(me, blocks, rows, w_gate, w_up, w_down, regions)
     partial, back_rows = back_part(me, *hidden, w_gate, w_up, w_down, regions, depth)
     summed = lax.psum_scatter(partial, "local", scatter_dimension=0)
-    shares, sums = combine_early(swap(back_rows, regions), routes, weights, regions, depth)
-    own = (shares, *ring_scatter(shares))
-    sums = add_over_local(sums)
-    moe, grad, comb = final(swap(summed, regions), own, tokens, gain, squares, sums, routes, weights, regions, full)
+    shares, right, left = combine_early(early, swap(back_rows, regions), routes, weights, regions, depth)
+    right, left = ring_scatter(shares, right, left)
+    moe, grad, comb = final(me, swap(summed, regions), shares, right, left, tokens, gain, routes, weights, regions, full)
     return moe, grad, comb.T
 
 

time: 261 us -> 251 us (0.962)
  blocking collectives: 55.5 us -> 0 us
  waiting for transfers between devices: 87.1 us -> 131 us
  Pallas kernels: 31.4 us -> 37.2 us
    all_to_all x1 -> x0, blocking collectives: 55.5 us -> none  [swap(): lax.all_to_all(split, 'region', split_axis=0, concat_axis=0, tiled=True)]
    all_to_all x3 -> x4, waiting for transfers between devices: 47.4 us -> 94.6 us  [swap(): lax.all_to_all(split, 'region', split_axis=0, concat_axis=0, tiled=True)]
    ppermute x6 -> x0, waiting for transfers between devices: 20.9 us -> none  [the longest x3 11.7 us: ring_gather(): lax.ppermute(squares, 'local', [(z, z ^ 1 << at) for z in range(2 * half)])]
    ppermute x16, waiting for transfers between devices: 18.8 us -> 36.3 us  [hop(): lax.ppermute(array, 'local', [(z, (z + step) % depth) for z in range(dept...]
    ppermute x6 -> x0, starting transfers between devices: 11.9 us -> none  [the longest x3 6.84 us: add_over_local(): lax.ppermute(array, 'local', [(z, z ^ step) for z in range(depth)])]
    all_to_all x3 -> x4, starting transfers between devices: 21.1 us -> 32.8 us  [swap(): lax.all_to_all(split, 'region', split_axis=0, concat_axis=0, tiled=True)]
    unnamed x20 -> x16, local copies, waits for them, and re-layouts: 8.16 us -> 4.52 us
    pallas_call x4 -> x3, Pallas kernels: 6.89 us -> 8.64 us  [once(): pl.pallas_call(kernel, grid=(1,), in_specs=[whole(operand.shape) for oper...]
  transfers between devices with their start and end apart: 27 -> 22, of which waited for: 13 -> 10; matrix products, arithmetic and copies ran while one was open for 1% -> 0% of each run, Pallas kernels for 2% -> 3%
where the time goes in v4:
time: 251 us; the launch traced here: 250 us
  waiting for transfers between devices  131 us (52%)
  starting transfers between devices  60.7 us (24%)
  Pallas kernels  37.2 us (15%)
  between operations  14.2 us (6%)
  local copies, waits for them, and re-layouts  6.56 us (3%)
    all_to_all x4, waiting for transfers between devices, swap(): lax.all_to_all(split, 'region', split_axis=0, concat_axis=0, tiled=True)  94.6 us
    ppermute x16, waiting for transfers between devices, hop(): lax.ppermute(array, 'local', [(z, (z + step) % depth) for z in range(dept...  36.3 us
    all_to_all x4, starting transfers between devices, swap(): lax.all_to_all(split, 'region', split_axis=0, concat_axis=0, tiled=True)  32.8 us
    ppermute x16, starting transfers between devices, hop(): lax.ppermute(array, 'local', [(z, (z + step) % depth) for z in range(dept...  27.8 us
    pallas_call x1, Pallas kernels, back_part(): pl.pallas_call(functools.partial(back_kernel, regions), grid_spec=pltpu.P...  13.5 us
    pallas_call x1, Pallas kernels, hidden_part(): pl.pallas_call(functools.partial(hidden_kernel, regions), grid_spec=pltpu...  13.4 us
    pallas_call x3, Pallas kernels, once(): pl.pallas_call(kernel, grid=(1,), in_specs=[whole(operand.shape) for oper...  8.64 us
  transfers between devices with their start and end apart: 22, of which 10 were waited for; matrix products, arithmetic and copies ran while one was open for 0% of the time, Pallas kernels for 3%

profile of v4, /device:TPU:2, one launch (start us, length us, event | category | flops | bytes accessed | tf_op | source)
XLA Modules:
  0.0 249.6 jit_solution(12977582615068467917)
XLA Ops:
  7.2 1.3 reshape.34.gain
  8.4 2.5 %shard_map.103 = (bf16[256,1280]{1,0:T(8,128)(2,1)}, bf16[144,768]{1,0:T(8,128)(2,1)}) custom-call(bf16[128,896]{1,0:T(8,128)(2,1)} %tok.3, f32[1,896]{1,0:T(1,128)} %reshape.34.gain, bf16[128,896]{1,0:T(8,128)(2,1)} %grad.1, s32[2,128]{1,0:T(2,128)} %bitcast.15), custom_call_target="tpu_custom_call" | custom-call | tf_op jit(solution)/shard_map/pallas_call | solution.py:111
  11.0 1.9 collective-permute-start
  12.9 3.9 %collective-permute-start.1 = (bf16[144,768]{1,0:T(8,128)(2,1)}, bf16[144,768]{1,0:T(8,128)(2,1)S(1)}, u32[]{:S(2)}, u32[]{:S(2)}) collective-permute-start(bf16[144,768]{1,0:T(8,128)(2,1)} %get-tuple-element.33.refs_0_), channel_id=1, source_target_pairs={{0,7},{1,0},{2,1},{3,2},{4,3},{5,4},{6,5},{7,6},{8,15},{9,8},{10,9... | collective-permute-start | bytes 663560 | tf_op jit(solution)/shard_map/ppermute | solution.py:499
  16.8 5.6 %collective-permute-done.refs_1_ = bf16[144,768]{1,0:T(8,128)(2,1)S(1)} collective-permute-done((bf16[144,768]{1,0:T(8,128)(2,1)}, bf16[144,768]{1,0:T(8,128)(2,1)S(1)}, u32[]{:S(2)}, u32[]{:S(2)}) %collective-permute-start) | collective-permute-done | bytes 221216 | tf_op jit(solution)/shard_map/ppermute | solution.py:499
  22.5 7.6 %all-to-all-start.1 = ((bf16[32,8,1280]{2,1,0:T(8,128)(2,1)}), bf16[32,8,1280]{2,1,0:T(8,128)(2,1)S(1)}, u32[]{:S(2)}, u32[]{:S(2)}) async-start(bf16[32,8,1280]{2,1,0:T(8,128)(2,1)} %bitcast.25), calls=%async_computation.1 | async-start | bytes 1310720 | tf_op jit(solution)/shard_map/all_to_all | solution.py:493
  30.1 0.0 all-gather.3.cloned.1.call-start
  30.2 0.1 collective-permute-start.2
  30.2 3.2 %collective-permute-start.3 = (bf16[144,768]{1,0:T(8,128)(2,1)S(1)}, bf16[144,768]{1,0:T(8,128)(2,1)S(1)}, u32[]{:S(2)}, u32[]{:S(2)}) collective-permute-start(bf16[144,768]{1,0:T(8,128)(2,1)S(1)} %collective-permute-done.1.refs_2_), channel_id=1, source_target_pairs={{0,7},{1,0},{2,1},{3,2},{4,3},{5,4},{6,5},{7,6},{8,15},{9,8},{10,9... | collective-permute-start | bytes 663560 | tf_op jit(solution)/shard_map/ppermute | solution.py:499
  33.5 5.5 %collective-permute-done.2.refs_3_ = bf16[144,768]{1,0:T(8,128)(2,1)S(1)} collective-permute-done((bf16[144,768]{1,0:T(8,128)(2,1)S(1)}, bf16[144,768]{1,0:T(8,128)(2,1)S(1)}, u32[]{:S(2)}, u32[]{:S(2)}) %collective-permute-start.2) | collective-permute-done | bytes 221216 | tf_op jit(solution)/shard_map/ppermute | solution.py:499
  38.9 2.5 collective-permute-start.4
  41.4 0.8 collective-permute-start.5
  42.2 4.6 %collective-permute-done.4.refs_5_ = bf16[144,768]{1,0:T(8,128)(2,1)S(1)} collective-permute-done((bf16[144,768]{1,0:T(8,128)(2,1)S(1)}, bf16[144,768]{1,0:T(8,128)(2,1)S(1)}, u32[]{:S(2)}, u32[]{:S(2)}) %collective-permute-start.4) | collective-permute-done | bytes 221216 | tf_op jit(solution)/shard_map/ppermute | solution.py:499
  46.8 1.0 collective-permute-done.5.refs_6_
  47.8 0.9 copy-done.7
  48.6 0.0 all-gather.3.cloned.1.call-update
  48.7 2.1 collective-permute-start.7
  50.7 0.1 collective-permute-start.6
  50.8 5.8 %collective-permute-done.6.refs_7_ = bf16[64,768]{1,0:T(8,128)(2,1)S(1)} collective-permute-done((bf16[64,768]{1,0:T(8,128)(2,1)S(1)}, bf16[64,768]{1,0:T(8,128)(2,1)S(1)}, u32[]{:S(2)}, u32[]{:S(2)}) %collective-permute-start.6) | collective-permute-done | bytes 98336 | tf_op jit(solution)/shard_map/ppermute | solution.py:499
  56.6 0.9 copy-done.2
  57.6 0.7 copy-done.4
  58.3 1.7 shard_map.104
  60.0 2.0 copy-done
  62.0 7.4 %all-to-all-start = ((bf16[32,8,7808]{2,1,0:T(8,128)(2,1)}), bf16[32,8,7808]{2,1,0:T(8,128)(2,1)}, u32[]{:S(2)}, u32[]{:S(2)}) async-start(bf16[32,8,7808]{2,1,0:T(8,128)(2,1)} %bitcast.13), calls=%async_computation | async-start | bytes 7995392 | tf_op jit(solution)/shard_map/all_to_all | solution.py:493
  69.5 0.0 reduce-scatter.2.cloned.1.call-start
  69.5 47.6 %all-to-all-done = bf16[32,8,7808]{2,1,0:T(8,128)(2,1)} async-done(((bf16[32,8,7808]{2,1,0:T(8,128)(2,1)}), bf16[32,8,7808]{2,1,0:T(8,128)(2,1)}, u32[]{:S(2)}, u32[]{:S(2)}) %all-to-all-start) | async-done | bytes 3997728 | tf_op jit(solution)/shard_map/all_to_all | solution.py:493
  117.1 13.4 %shard_map.105 = (bf16[320,256]{1,0:T(8,128)(2,1)}, bf16[320,256]{1,0:T(8,128)(2,1)}, bf16[320,256]{1,0:T(8,128)(2,1)}, bf16[256,128]{1,0:T(8,128)(2,1)}) custom-call(s32[1]{0:T(128)} %bitcast.me, bf16[256,7808]{1,0:T(8,128)(2,1)} %bitcast.3.scales.main.rest, bf16[8,256,1280]{2,1,0:T(8,128)(2,1)} %bitcast.21, bf16[256,7808]{1,0:T(8,128)(2,1)} %bitcast.3.scales.main.rest, ...), custom_call_target="tpu_custom_call" | custom-call | tf_op jit(solution)/shard_map/pallas_call | solution.py:279
  130.6 13.5 %shard_map.106 = (bf16[8,256,1280]{2,1,0:T(8,128)(2,1)}, bf16[256,7808]{1,0:T(8,128)(2,1)}) custom-call(s32[1]{0:T(128)} %bitcast.me, bf16[320,256]{1,0:T(8,128)(2,1)} %get-tuple-element.45.hid, bf16[320,256]{1,0:T(8,128)(2,1)} %get-tuple-element.46.gate_g, bf16[320,256]{1,0:T(8,128)(2,1)} %get-tuple-element.47.up_g, ...), custom_call_target="tpu_custom_call" | custom-call | tf_op jit(solution)/shard_map/pallas_call | solution.py:338
  144.1 9.3 %all-to-all-start.3 = ((bf16[32,8,7808]{2,1,0:T(8,128)(2,1)}), bf16[32,8,7808]{2,1,0:T(8,128)(2,1)}, u32[]{:S(2)}, u32[]{:S(2)}) async-start(bf16[32,8,7808]{2,1,0:T(8,128)(2,1)} %bitcast.22), calls=%async_computation.4 | async-start | bytes 7995392 | tf_op jit(solution)/shard_map/all_to_all | solution.py:493
  153.4 0.7 slice.11.squares
  154.2 46.9 %all-to-all-done.3 = bf16[32,8,7808]{2,1,0:T(8,128)(2,1)} async-done(((bf16[32,8,7808]{2,1,0:T(8,128)(2,1)}), bf16[32,8,7808]{2,1,0:T(8,128)(2,1)}, u32[]{:S(2)}, u32[]{:S(2)}) %all-to-all-start.3) | async-done | bytes 3997728 | tf_op jit(solution)/shard_map/all_to_all | solution.py:493
  201.1 4.4 %shard_map.107 = (bf16[8,144,768]{2,1,0:T(8,128)(2,1)S(1)}, bf16[80,768]{1,0:T(8,128)(2,1)S(1)}, bf16[80,768]{1,0:T(8,128)(2,1)S(1)}) custom-call(bf16[16,768]{1,0:T(8,128)(2,1)S(1)} %slice.11.squares, bf16[256,7808]{1,0:T(8,128)(2,1)} %bitcast.10.back, s32[2,128]{1,0:T(2,128)S(1)} %bitcast.17, f32[2,128]{1,0:T(2,128)S(1)} %bitcast.19), custom_call_target="tpu_custom_call" | custom-call | tf_op jit(solution)/shard_map/pallas_call | solution.py:111
  205.5 0.1 collective-permute-start.8
  205.6 3.2 %collective-permute-start.9 = (bf16[80,768]{1,0:T(8,128)(2,1)S(1)}, bf16[80,768]{1,0:T(8,128)(2,1)S(1)}, u32[]{:S(2)}, u32[]{:S(2)}) collective-permute-start(bf16[80,768]{1,0:T(8,128)(2,1)S(1)} %get-tuple-element.53), channel_id=1, source_target_pairs={{0,7},{1,0},{2,1},{3,2},{4,3},{5,4},{6,5},{7,6},{8,15},{9,8},{10,9... | collective-permute-start | bytes 368648 | tf_op jit(solution)/shard_map/ppermute | solution.py:499
  208.8 3.7 %collective-permute-done.8.right = bf16[80,768]{1,0:T(8,128)(2,1)S(1)} collective-permute-done((bf16[80,768]{1,0:T(8,128)(2,1)S(1)}, bf16[80,768]{1,0:T(8,128)(2,1)S(1)}, u32[]{:S(2)}, u32[]{:S(2)}) %collective-permute-start.8) | collective-permute-done | bytes 122912 | tf_op jit(solution)/shard_map/ppermute | solution.py:499
  212.5 0.1 shard_map.108
  212.6 0.1 collective-permute-start.10
  212.7 3.2 %collective-permute-start.11 = (bf16[144,768]{1,0:T(8,128)(2,1)S(1)}, bf16[144,768]{1,0:T(8,128)(2,1)S(1)}, u32[]{:S(2)}, u32[]{:S(2)}) collective-permute-start(bf16[144,768]{1,0:T(8,128)(2,1)S(1)} %get-tuple-element.55), channel_id=1, source_target_pairs={{0,7},{1,0},{2,1},{3,2},{4,3},{5,4},{6,5},{7,6},{8,15},{9,8},{10,9... | collective-permute-start | bytes 663560 | tf_op jit(solution)/shard_map/ppermute | solution.py:499
  215.9 8.4 %all-to-all-start.2 = ((bf16[32,8,1280]{2,1,0:T(8,128)(2,1)}), bf16[32,8,1280]{2,1,0:T(8,128)(2,1)S(1)}, u32[]{:S(2)}, u32[]{:S(2)}) async-start(bf16[32,8,1280]{2,1,0:T(8,128)(2,1)} %bitcast.24), calls=%async_computation.3 | async-start | bytes 1310720 | tf_op jit(solution)/shard_map/all_to_all | solution.py:493
  224.4 0.1 shard_map.109
  224.5 0.1 collective-permute-start.12
  224.6 3.2 %collective-permute-start.13 = (bf16[144,768]{1,0:T(8,128)(2,1)S(1)}, bf16[144,768]{1,0:T(8,128)(2,1)S(1)}, u32[]{:S(2)}, u32[]{:S(2)}) collective-permute-start(bf16[144,768]{1,0:T(8,128)(2,1)S(1)} %get-tuple-element.57), channel_id=1, source_target_pairs={{0,7},{1,0},{2,1},{3,2},{4,3},{5,4},{6,5},{7,6},{8,15},{9,8},{10,9... | collective-permute-start | bytes 663560 | tf_op jit(solution)/shard_map/ppermute | solution.py:499
  227.8 5.5 %collective-permute-done.12.right = bf16[144,768]{1,0:T(8,128)(2,1)S(1)} collective-permute-done((bf16[144,768]{1,0:T(8,128)(2,1)S(1)}, bf16[144,768]{1,0:T(8,128)(2,1)S(1)}, u32[]{:S(2)}, u32[]{:S(2)}) %collective-permute-start.12) | collective-permute-done | bytes 221216 | tf_op jit(solution)/shard_map/ppermute | solution.py:499
  233.2 0.1 shard_map.110
  233.4 1.5 collective-permute-start.14
  234.9 1.8 collective-permute-start.15
  236.7 4.6 %collective-permute-done.14.right = bf16[144,768]{1,0:T(8,128)(2,1)S(1)} collective-permute-done((bf16[144,768]{1,0:T(8,128)(2,1)S(1)}, bf16[144,768]{1,0:T(8,128)(2,1)S(1)}, u32[]{:S(2)}, u32[]{:S(2)}) %collective-permute-start.14) | collective-permute-done | bytes 221216 | tf_op jit(solution)/shard_map/ppermute | solution.py:499
  241.3 1.4 shard_map.111
  (27 shorter events, 0.1 us)
Async XLA Ops:
  11.0 11.5 %collective-permute-start = (bf16[144,768]{1,0:T(8,128)(2,1)}, bf16[144,768]{1,0:T(8,128)(2,1)S(1)}, u32[]{:S(2)}, u32[]{:S(2)}) collective-permute-start(bf16[144,768]{1,0:T(8,128)(2,1)} %get-tuple-element.33.refs_0_), channel_id=1, source_target_pairs={{0,1},{1,2},{2,3},{3,4},{4,5},{5,6},{6,7},{7,0},{8,9},{9,10},{10,1... | collective-permute-start | bytes 663560 | tf_op jit(solution)/shard_map/ppermute | solution.py:499
  12.9 9.6 %collective-permute-start.1 = (bf16[144,768]{1,0:T(8,128)(2,1)}, bf16[144,768]{1,0:T(8,128)(2,1)S(1)}, u32[]{:S(2)}, u32[]{:S(2)}) collective-permute-start(bf16[144,768]{1,0:T(8,128)(2,1)} %get-tuple-element.33.refs_0_), channel_id=1, source_target_pairs={{0,7},{1,0},{2,1},{3,2},{4,3},{5,4},{6,5},{7,6},{8,15},{9,8},{10,9... | collective-permute-start | bytes 663560 | tf_op jit(solution)/shard_map/ppermute | solution.py:499
  22.5 25.3 %all-to-all-start.1 = ((bf16[32,8,1280]{2,1,0:T(8,128)(2,1)}), bf16[32,8,1280]{2,1,0:T(8,128)(2,1)S(1)}, u32[]{:S(2)}, u32[]{:S(2)}) async-start(bf16[32,8,1280]{2,1,0:T(8,128)(2,1)} %bitcast.25), calls=%async_computation.1 | async-start | bytes 1310720 | tf_op jit(solution)/shard_map/all_to_all | solution.py:493
  30.1 87.0 %all-gather.3.cloned.1.call-start = ((), (), s32[]{:S(2)}) async-start(), calls=%async_computation.6 | async-start | bytes 5898240 | tf_op jit(solution)/shard_map/all_gather | solution.py:533
  30.2 8.8 %collective-permute-start.2 = (bf16[144,768]{1,0:T(8,128)(2,1)S(1)}, bf16[144,768]{1,0:T(8,128)(2,1)S(1)}, u32[]{:S(2)}, u32[]{:S(2)}) collective-permute-start(bf16[144,768]{1,0:T(8,128)(2,1)S(1)} %collective-permute-done.refs_1_), channel_id=1, source_target_pairs={{0,1},{1,2},{2,3},{3,4},{4,5},{5,6},{6,7},{7,0},{8,9},{9,10},{10,1... | collective-permute-start | bytes 663560 | tf_op jit(solution)/shard_map/ppermute | solution.py:499
  30.2 8.7 %collective-permute-start.3 = (bf16[144,768]{1,0:T(8,128)(2,1)S(1)}, bf16[144,768]{1,0:T(8,128)(2,1)S(1)}, u32[]{:S(2)}, u32[]{:S(2)}) collective-permute-start(bf16[144,768]{1,0:T(8,128)(2,1)S(1)} %collective-permute-done.1.refs_2_), channel_id=1, source_target_pairs={{0,7},{1,0},{2,1},{3,2},{4,3},{5,4},{6,5},{7,6},{8,15},{9,8},{10,9... | collective-permute-start | bytes 663560 | tf_op jit(solution)/shard_map/ppermute | solution.py:499
  38.9 7.9 %collective-permute-start.4 = (bf16[144,768]{1,0:T(8,128)(2,1)S(1)}, bf16[144,768]{1,0:T(8,128)(2,1)S(1)}, u32[]{:S(2)}, u32[]{:S(2)}) collective-permute-start(bf16[144,768]{1,0:T(8,128)(2,1)S(1)} %collective-permute-done.2.refs_3_), channel_id=1, source_target_pairs={{0,1},{1,2},{2,3},{3,4},{4,5},{5,6},{6,7},{7,0},{8,9},{9,10},{10,1... | collective-permute-start | bytes 663560 | tf_op jit(solution)/shard_map/ppermute | solution.py:499
  41.4 6.4 %collective-permute-start.5 = (bf16[144,768]{1,0:T(8,128)(2,1)S(1)}, bf16[144,768]{1,0:T(8,128)(2,1)S(1)}, u32[]{:S(2)}, u32[]{:S(2)}) collective-permute-start(bf16[144,768]{1,0:T(8,128)(2,1)S(1)} %collective-permute-done.3.refs_4_), channel_id=1, source_target_pairs={{0,7},{1,0},{2,1},{3,2},{4,3},{5,4},{6,5},{7,6},{8,15},{9,8},{10,9... | collective-permute-start | bytes 663560 | tf_op jit(solution)/shard_map/ppermute | solution.py:499
  47.8 0.9 copy-start.7
  48.7 8.0 %collective-permute-start.7 = (bf16[80,768]{1,0:T(8,128)(2,1)S(1)}, bf16[80,768]{1,0:T(8,128)(2,1)S(1)}, u32[]{:S(2)}, u32[]{:S(2)}) collective-permute-start(bf16[80,768]{1,0:T(8,128)(2,1)S(1)} %slice.10), channel_id=1, source_target_pairs={{0,7},{1,0},{2,1},{3,2},{4,3},{5,4},{6,5},{7,6},{8,15},{9,8},{10,9... | collective-permute-start | bytes 368648 | tf_op jit(solution)/shard_map/ppermute | solution.py:499
  50.7 5.9 %collective-permute-start.6 = (bf16[64,768]{1,0:T(8,128)(2,1)S(1)}, bf16[64,768]{1,0:T(8,128)(2,1)S(1)}, u32[]{:S(2)}, u32[]{:S(2)}) collective-permute-start(bf16[64,768]{1,0:T(8,128)(2,1)S(1)} %slice.9), channel_id=1, source_target_pairs={{0,1},{1,2},{2,3},{3,4},{4,5},{5,6},{6,7},{7,0},{8,9},{9,10},{10,1... | collective-permute-start | bytes 294920 | tf_op jit(solution)/shard_map/ppermute | solution.py:499
  56.6 0.9 copy-start.2
  57.6 0.7 copy-start.4
  60.0 2.0 copy-start
  62.0 55.1 %all-to-all-start = ((bf16[32,8,7808]{2,1,0:T(8,128)(2,1)}), bf16[32,8,7808]{2,1,0:T(8,128)(2,1)}, u32[]{:S(2)}, u32[]{:S(2)}) async-start(bf16[32,8,7808]{2,1,0:T(8,128)(2,1)} %bitcast.13), calls=%async_computation | async-start | bytes 7995392 | tf_op jit(solution)/shard_map/all_to_all | solution.py:493
  69.5 146.5 %reduce-scatter.2.cloned.1.call-start = ((), (), s32[]{:S(2)}) async-start(), calls=%async_computation.5 | async-start | bytes 5898240 | tf_op jit(solution)/shard_map/reduce_scatter | solution.py:537
  144.1 57.0 %copy-start.5 = (s32[128,2]{0,1:T(2,128)S(1)}, s32[128,2]{0,1:T(2,128)}, u32[]{:S(2)}) copy-start(s32[128,2]{0,1:T(2,128)} %param.13) | copy-start | bytes 3076
  144.1 57.0 %copy-start.6 = (f32[128,2]{0,1:T(2,128)S(1)}, f32[128,2]{0,1:T(2,128)}, u32[]{:S(2)}) copy-start(f32[128,2]{0,1:T(2,128)} %param.14) | copy-start | bytes 3076
  144.1 57.0 %all-to-all-start.3 = ((bf16[32,8,7808]{2,1,0:T(8,128)(2,1)}), bf16[32,8,7808]{2,1,0:T(8,128)(2,1)}, u32[]{:S(2)}, u32[]{:S(2)}) async-start(bf16[32,8,7808]{2,1,0:T(8,128)(2,1)} %bitcast.22), calls=%async_computation.4 | async-start | bytes 7995392 | tf_op jit(solution)/shard_map/all_to_all | solution.py:493
  205.5 7.1 %collective-permute-start.8 = (bf16[80,768]{1,0:T(8,128)(2,1)S(1)}, bf16[80,768]{1,0:T(8,128)(2,1)S(1)}, u32[]{:S(2)}, u32[]{:S(2)}) collective-permute-start(bf16[80,768]{1,0:T(8,128)(2,1)S(1)} %get-tuple-element.52), channel_id=1, source_target_pairs={{0,1},{1,2},{2,3},{3,4},{4,5},{5,6},{6,7},{7,0},{8,9},{9,10},{10,1... | collective-permute-start | bytes 368648 | tf_op jit(solution)/shard_map/ppermute | solution.py:499
  205.6 7.0 %collective-permute-start.9 = (bf16[80,768]{1,0:T(8,128)(2,1)S(1)}, bf16[80,768]{1,0:T(8,128)(2,1)S(1)}, u32[]{:S(2)}, u32[]{:S(2)}) collective-permute-start(bf16[80,768]{1,0:T(8,128)(2,1)S(1)} %get-tuple-element.53), channel_id=1, source_target_pairs={{0,7},{1,0},{2,1},{3,2},{4,3},{5,4},{6,5},{7,6},{8,15},{9,8},{10,9... | collective-permute-start | bytes 368648 | tf_op jit(solution)/shard_map/ppermute | solution.py:499
  212.6 11.7 %collective-permute-start.10 = (bf16[144,768]{1,0:T(8,128)(2,1)S(1)}, bf16[144,768]{1,0:T(8,128)(2,1)S(1)}, u32[]{:S(2)}, u32[]{:S(2)}) collective-permute-start(bf16[144,768]{1,0:T(8,128)(2,1)S(1)} %get-tuple-element.54), channel_id=1, source_target_pairs={{0,1},{1,2},{2,3},{3,4},{4,5},{5,6},{6,7},{7,0},{8,9},{9,10},{10,1... | collective-permute-start | bytes 663560 | tf_op jit(solution)/shard_map/ppermute | solution.py:499
  212.7 11.7 %collective-permute-start.11 = (bf16[144,768]{1,0:T(8,128)(2,1)S(1)}, bf16[144,768]{1,0:T(8,128)(2,1)S(1)}, u32[]{:S(2)}, u32[]{:S(2)}) collective-permute-start(bf16[144,768]{1,0:T(8,128)(2,1)S(1)} %get-tuple-element.55), channel_id=1, source_target_pairs={{0,7},{1,0},{2,1},{3,2},{4,3},{5,4},{6,5},{7,6},{8,15},{9,8},{10,9... | collective-permute-start | bytes 663560 | tf_op jit(solution)/shard_map/ppermute | solution.py:499
  215.9 25.4 %all-to-all-start.2 = ((bf16[32,8,1280]{2,1,0:T(8,128)(2,1)}), bf16[32,8,1280]{2,1,0:T(8,128)(2,1)S(1)}, u32[]{:S(2)}, u32[]{:S(2)}) async-start(bf16[32,8,1280]{2,1,0:T(8,128)(2,1)} %bitcast.24), calls=%async_computation.3 | async-start | bytes 1310720 | tf_op jit(solution)/shard_map/all_to_all | solution.py:493
  224.3 17.0 %copy-start.1 = (bf16[128,896]{1,0:T(8,128)(2,1)S(1)}, bf16[128,896]{1,0:T(8,128)(2,1)}, u32[]{:S(2)}) copy-start(bf16[128,896]{1,0:T(8,128)(2,1)} %tok.3) | copy-start | bytes 688132
  224.3 17.0 %copy-start.3 = (f32[1,896]{1,0:T(1,128)S(1)}, f32[1,896]{1,0:T(1,128)}, u32[]{:S(2)}) copy-start(f32[1,896]{1,0:T(1,128)} %reshape.34.gain) | copy-start | bytes 10756
  224.5 8.8 %collective-permute-start.12 = (bf16[144,768]{1,0:T(8,128)(2,1)S(1)}, bf16[144,768]{1,0:T(8,128)(2,1)S(1)}, u32[]{:S(2)}, u32[]{:S(2)}) collective-permute-start(bf16[144,768]{1,0:T(8,128)(2,1)S(1)} %get-tuple-element.56), channel_id=1, source_target_pairs={{0,1},{1,2},{2,3},{3,4},{4,5},{5,6},{6,7},{7,0},{8,9},{9,10},{10,1... | collective-permute-start | bytes 663560 | tf_op jit(solution)/shard_map/ppermute | solution.py:499
  224.6 8.7 %collective-permute-start.13 = (bf16[144,768]{1,0:T(8,128)(2,1)S(1)}, bf16[144,768]{1,0:T(8,128)(2,1)S(1)}, u32[]{:S(2)}, u32[]{:S(2)}) collective-permute-start(bf16[144,768]{1,0:T(8,128)(2,1)S(1)} %get-tuple-element.57), channel_id=1, source_target_pairs={{0,7},{1,0},{2,1},{3,2},{4,3},{5,4},{6,5},{7,6},{8,15},{9,8},{10,9... | collective-permute-start | bytes 663560 | tf_op jit(solution)/shard_map/ppermute | solution.py:499
  233.4 7.9 %collective-permute-start.14 = (bf16[144,768]{1,0:T(8,128)(2,1)S(1)}, bf16[144,768]{1,0:T(8,128)(2,1)S(1)}, u32[]{:S(2)}, u32[]{:S(2)}) collective-permute-start(bf16[144,768]{1,0:T(8,128)(2,1)S(1)} %get-tuple-element.58), channel_id=1, source_target_pairs={{0,1},{1,2},{2,3},{3,4},{4,5},{5,6},{6,7},{7,0},{8,9},{9,10},{10,1... | collective-permute-start | bytes 663560 | tf_op jit(solution)/shard_map/ppermute | solution.py:499
  234.9 6.4 %collective-permute-start.15 = (bf16[144,768]{1,0:T(8,128)(2,1)S(1)}, bf16[144,768]{1,0:T(8,128)(2,1)S(1)}, u32[]{:S(2)}, u32[]{:S(2)}) collective-permute-start(bf16[144,768]{1,0:T(8,128)(2,1)S(1)} %get-tuple-element.59), channel_id=1, source_target_pairs={{0,7},{1,0},{2,1},{3,2},{4,3},{5,4},{6,5},{7,6},{8,15},{9,8},{10,9... | collective-permute-start | bytes 663560 | tf_op jit(solution)/shard_map/ppermute | solution.py:499
Sparse Core Ops, SparseCore 0:
  48.8 63.7 all-gather.2
  144.2 67.3 reduce-scatter.1

commit v5 on v4

--- a/solution.py
+++ b/solution.py
@@ -155,7 +155,7 @@
     late = out.shape[1] * 2 // 5
     count = tok.shape[0]
     wide = tok[...].astype(F32)
-    scaled = (wide * gain[...]).astype(BF)
+    scaled = (wide * gain[...].reshape(1, -1)).astype(BF)
     rows = dot(pick, jnp.concatenate([scaled[:, :late], grad[:, :late]], axis=1)).astype(BF)
     cut = 8 * regions
     out[...] = encode(rows[:cut], rows[cut:], fold_matrix(regions))
@@ -199,7 +199,7 @@
         out[:, z * lanes : (z + 1) * lanes] = rows[:cut]
         rests.append(rows[cut:])
     for half in range(depth // 4):
-        stacked = jnp.concatenate([rests[part * (depth // 4) + half] for part in range(4)], axis=0)
+        stacked = jnp.concatenate(rests[4 * half : 4 * half + 4], axis=0)
         at_lane = (depth + half) * lanes
         out[:, at_lane : at_lane + lanes] = dot(fold_matrix(regions), stacked, TN).astype(BF)
     inv = inverse(squares, full)
@@ -218,135 +218,155 @@
     return once(functools.partial(pack_early_kernel, regions, depth, full), shape, routes, *blocks)
 
 
-def relative_specs(width, units, depth):
-    return [
-        pl.BlockSpec((1, width, units), lambda z, me: (0, (z + me[0]) % depth, 0)),
-        pl.BlockSpec((1, width, units), lambda z, me: (0, (z + me[0]) % depth, 0)),
-        pl.BlockSpec((1, units, width), lambda z, me: (0, 0, (z + me[0]) % depth)),
-    ]
-
-
-def hidden_kernel(
-    regions, me, scales, block, main, rest, gate_w, up_w, down_w, hid_out, gate_out, up_out, scal_out, acc_g, acc_u, acc_h, fold
+def anywhere():
+    return pl.BlockSpec(memory_space=pl.ANY)
+
+
+def expert_kernel(
+    regions,
+    depth,
+    me,
+    blocks,
+    rows,
+    gate_hbm,
+    up_hbm,
+    down_hbm,
+    late_out,
+    early_out,
+    gate_w,
+    up_w,
+    down_w,
+    acc_g,
+    acc_u,
+    acc_h,
+    hid,
+    gate_g,
+    up_g,
+    scal,
+    fold,
+    scales,
+    sem,
+    weight_sems,
 ):
-    step = pl.program_id(0)
-    width = gate_w.shape[1]
+    width = gate_w.shape[1] // depth
     few = 2 * regions
-    quarter = pl.num_programs(0) // 4
-
-    @pl.when(step == 0)
-    def _():
-        fold[...] = fold_matrix(regions)
-        acc_g[...] = jnp.zeros_like(acc_g)
-        acc_u[...] = jnp.zeros_like(acc_u)
-        acc_h[...] = jnp.zeros_like(acc_h)
-
-    late_in, late_grad = decode(block[0], width - EARLY, fold[...])
-    pick = fold[pl.ds(pl.multiple_of((step // quarter) * few, few), few), :]
-    early = jnp.concatenate([main[...], dot(pick, rest[...]).astype(BF)], axis=0)
-    rows_in = jnp.concatenate([late_in, early[:, :EARLY]], axis=1)
-    rows_grad = jnp.concatenate([late_grad, early[:, EARLY:]], axis=1)
-    acc_g[...] += dot(rows_in, gate_w[0])
-    acc_u[...] += dot(rows_in, up_w[0])
-    acc_h[...] += dot(rows_grad, down_w[0], NT)
-
-    @pl.when(step == pl.num_programs(0) - 1)
-    def _():
-        cut = 8 * regions
-        first = fold[0:few, :]
-        inv = jnp.concatenate([from_lanes(scales[...], 0), from_lanes(dot(first, scales[...]), 3)], axis=0)
-        gate_raw, up_raw, grad_hidden = acc_g[...], acc_u[...], acc_h[...]
-        gate_pre, up_pre = gate_raw * inv, up_raw * inv
-        sig = jax.nn.sigmoid(gate_pre)
-        act = gate_pre * sig
-        hidden = (act * up_pre).astype(BF)
-        grad_gate = (grad_hidden * up_pre * sig * (1.0 + gate_pre * (1.0 - sig))).astype(BF)
-        grad_up = (grad_hidden * act).astype(BF)
-        hid_out[...] = hidden
-        gate_out[...] = grad_gate
-        up_out[...] = grad_up
-        comb = jnp.sum(hidden.astype(F32) * grad_hidden, axis=1, keepdims=True)
-        inner = jnp.sum(grad_gate.astype(F32) * gate_raw + grad_up.astype(F32) * up_raw, axis=1, keepdims=True)
-        here = in_lanes(triple(comb[:cut]) + triple(inner[:cut]), cut)
-        there = in_lanes([None] * 6 + triple(comb[cut:]) + triple(inner[cut:]), few)
-        scal_out[...] = here + dot(first, there, TN).astype(BF)
-
-
-def hidden_part(me, blocks, rows, gate_w, up_w, down_w, regions):
+    cut, lanes = blocks.shape[1:]
+    first_block = me[0]
+    copy = pltpu.make_async_copy(rows.at[:, rows.shape[1] - 128 :], scales, sem)
+    copy.start()
+
+    def lanes_of(step):
+        return pl.ds(pl.multiple_of((step + first_block) % depth * width, 128), width)
+
+    def weight_copies(step):
+        at = lanes_of(step)
+        return [
+            pltpu.make_async_copy(gate_hbm.at[:, at, :], gate_w.at[:, at, :], weight_sems.at[0, step]),
+            pltpu.make_async_copy(up_hbm.at[:, at, :], up_w.at[:, at, :], weight_sems.at[1, step]),
+            pltpu.make_async_copy(down_hbm.at[:, :, at], down_w.at[:, :, at], weight_sems.at[2, step]),
+        ]
+
+    for step in range(depth):
+        for one in weight_copies(step):
+            one.start()
+    fold[...] = fold_matrix(regions)
+    acc_g[...] = jnp.zeros_like(acc_g)
+    acc_u[...] = jnp.zeros_like(acc_u)
+    acc_h[...] = jnp.zeros_like(acc_h)
+
+    def body(block, main, rest):
+        step = pl.program_id(0)
+        at = lanes_of(step)
+        for one in weight_copies(step):
+            one.wait()
+        late_in, late_grad = decode(block[0], width - EARLY, fold[...])
+        pick = fold[pl.ds(pl.multiple_of((step % 4) * few, few), few), :]
+        early = jnp.concatenate([main[...], dot(pick, rest[...]).astype(BF)], axis=0)
+        rows_in = jnp.concatenate([late_in, early[:, :EARLY]], axis=1)
+        rows_grad = jnp.concatenate([late_grad, early[:, EARLY:]], axis=1)
+        acc_g[...] += dot(rows_in, gate_w[0, at, :])
+        acc_u[...] += dot(rows_in, up_w[0, at, :])
+        acc_h[...] += dot(rows_grad, down_w[0, :, at], NT)
+
+    pltpu.emit_pipeline(
+        body,
+        grid=(depth,),
+        in_specs=[
+            pl.BlockSpec((1, cut, lanes), lambda z: ((z + first_block) % depth, 0, 0)),
+            pl.BlockSpec((cut, 2 * EARLY), lambda z: (0, z)),
+            pl.BlockSpec((cut, 2 * EARLY), lambda z: (0, depth + z // 4)),
+        ],
+    )(blocks, rows, rows)
+
+    copy.wait()
+    first = fold[0:few, :]
+    inv = jnp.concatenate([from_lanes(scales[...], 0), from_lanes(dot(first, scales[...]), 3)], axis=0)
+    gate_raw, up_raw, grad_hidden = acc_g[...], acc_u[...], acc_h[...]
+    gate_pre, up_pre = gate_raw * inv, up_raw * inv
+    sig = jax.nn.sigmoid(gate_pre)
+    act = gate_pre * sig
+    hidden = (act * up_pre).astype(BF)
+    grad_gate = (grad_hidden * up_pre * sig * (1.0 + gate_pre * (1.0 - sig))).astype(BF)
+    grad_up = (grad_hidden * act).astype(BF)
+    hid[...] = hidden
+    gate_g[...] = grad_gate
+    up_g[...] = grad_up
+    comb = jnp.sum(hidden.astype(F32) * grad_hidden, axis=1, keepdims=True)
+    inner = jnp.sum(grad_gate.astype(F32) * gate_raw + grad_up.astype(F32) * up_raw, axis=1, keepdims=True)
+    here = in_lanes(triple(comb[:cut]) + triple(inner[:cut]), cut)
+    there = in_lanes([None] * 6 + triple(comb[cut:]) + triple(inner[cut:]), few)
+    scal[...] = here + dot(first, there, TN).astype(BF)
+    late = width - EARLY
+    late_lanes = late_out.shape[2]
+
+    def back(late_block, main, rest):
+        step = pl.program_id(0)
+        at = lanes_of(step)
+        moe = dot(hid[...], down_w[0, :, at]).astype(BF)
+        grad = (dot(gate_g[...], gate_w[0, at, :], NT) + dot(up_g[...], up_w[0, at, :], NT)).astype(BF)
+        both = jnp.concatenate([moe[:, :late], grad[:, :late]], axis=1)
+        late_block[0] = encode(both[:cut], both[cut:], fold[...])
+        both = jnp.concatenate([moe[:, late:], grad[:, late:]], axis=1)
+        main[...] = both[:cut]
+        pick = fold[pl.ds(pl.multiple_of((step % 4) * few, few), few), :]
+        low = dot(pick, both[cut:], TN).astype(BF)
+
+        @pl.when(step % 4 == 0)
+        def _():
+            rest[...] = low
+
+        @pl.when(step % 4 > 0)
+        def _():
+            rest[...] = rest[...] + low
+
+    pltpu.emit_pipeline(
+        back,
+        grid=(depth,),
+        out_specs=[
+            pl.BlockSpec((1, cut, late_lanes), lambda z: ((z + first_block) % depth, 0, 0)),
+            pl.BlockSpec((cut, 2 * EARLY), lambda z: (0, z)),
+            pl.BlockSpec((cut, 2 * EARLY), lambda z: (0, depth + z // 4)),
+        ],
+    )(late_out, early_out, early_out)
+    pltpu.sync_copy(scal, early_out.at[:, early_out.shape[1] - 128 :])
+
+
+def expert_part(me, blocks, rows, gate_w, up_w, down_w, regions):
     depth, cut, lanes = blocks.shape
-    width, units = gate_w.shape[1] // depth, gate_w.shape[2]
+    units = gate_w.shape[2]
     total = 10 * regions
     return pl.pallas_call(
-        functools.partial(hidden_kernel, regions),
-        grid_spec=pltpu.PrefetchScalarGridSpec(
-            num_scalar_prefetch=1,
-            grid=(depth,),
-            in_specs=[
-                pl.BlockSpec((cut, 128), lambda z, me: (0, 2 * EARLY * depth * 5 // 512)),
-                pl.BlockSpec((1, cut, lanes), lambda z, me: ((z + me[0]) % depth, 0, 0)),
-                pl.BlockSpec((cut, 2 * EARLY), lambda z, me: (0, z)),
-                pl.BlockSpec((cut, 2 * EARLY), lambda z, me: (0, depth + z % (depth // 4))),
-            ]
-            + relative_specs(width, units, depth),
-            out_specs=[whole((total, units))] * 3 + [whole((cut, 128))],
-            scratch_shapes=[pltpu.VMEM((total, units), F32)] * 3 + [pltpu.VMEM((cut, cut), BF)],
-        ),
-        out_shape=[jax.ShapeDtypeStruct((total, units), BF)] * 3 + [jax.ShapeDtypeStruct((cut, 128), BF)],
-        compiler_params=params(),
-    )(me, rows, blocks, rows, rows, gate_w, up_w, down_w)
-
-
-def back_kernel(regions, me, hid, gate_g, up_g, scal, gate_w, up_w, down_w, late_out, early_out, fold):
-    depth = pl.num_programs(0)
-    step = pl.program_id(0)
-    late = gate_w.shape[1] - EARLY
-    lanes = 2 * EARLY
-    few = 2 * regions
-    cut = 8 * regions
-    quarter = depth // 4
-
-    @pl.when(step == 0)
-    def _():
-        fold[...] = fold_matrix(regions)
-        early_out[:, -128:] = scal[...]
-
-    moe = dot(hid[...], down_w[0]).astype(BF)
-    grad = (dot(gate_g[...], gate_w[0], NT) + dot(up_g[...], up_w[0], NT)).astype(BF)
-    both = jnp.concatenate([moe[:, :late], grad[:, :late]], axis=1)
-    late_out[0] = encode(both[:cut], both[cut:], fold[...])
-    both = jnp.concatenate([moe[:, late:], grad[:, late:]], axis=1)
-    early_out[:, pl.ds(pl.multiple_of(step * lanes, 128), lanes)] = both[:cut]
-    spot = pl.ds(pl.multiple_of((depth + step % quarter) * lanes, 128), lanes)
-    pick = fold[pl.ds(pl.multiple_of((step // quarter) * few, few), few), :]
-    low = dot(pick, both[cut:], TN).astype(BF)
-
-    @pl.when(step < quarter)
-    def _():
-        early_out[:, spot] = low
-
-    @pl.when(step >= quarter)
-    def _():
-        early_out[:, spot] = early_out[:, spot] + low
-
-
-def back_part(me, hid, gate_g, up_g, scal, gate_w, up_w, down_w, regions, depth):
-    width, units = gate_w.shape[1] // depth, gate_w.shape[2]
-    total = 10 * regions
-    cut = 8 * regions
-    lanes = packed_lanes(width - EARLY)
-    shape = early_shape(regions, depth)
-    return pl.pallas_call(
-        functools.partial(back_kernel, regions),
-        grid_spec=pltpu.PrefetchScalarGridSpec(
-            num_scalar_prefetch=1,
-            grid=(depth,),
-            in_specs=[whole((total, units))] * 3 + [whole((cut, 128))] + relative_specs(width, units, depth),
-            out_specs=[pl.BlockSpec((1, cut, lanes), lambda z, me: ((z + me[0]) % depth, 0, 0)), whole(shape)],
-            scratch_shapes=[pltpu.VMEM((cut, cut), BF)],
-        ),
-        out_shape=[jax.ShapeDtypeStruct((depth, cut, lanes), BF), jax.ShapeDtypeStruct(shape, BF)],
-        compiler_params=params(),
-    )(me, hid, gate_g, up_g, scal, gate_w, up_w, down_w)
+        functools.partial(expert_kernel, regions, depth),
+        in_specs=[pl.BlockSpec(memory_space=pltpu.SMEM)] + [anywhere()] * 5,
+        out_specs=[anywhere()] * 2,
+        out_shape=[jax.ShapeDtypeStruct((depth, cut, lanes), BF), jax.ShapeDtypeStruct(rows.shape, BF)],
+        scratch_shapes=[pltpu.VMEM(w.shape, BF) for w in (gate_w, up_w, down_w)]
+        + [pltpu.VMEM((total, units), F32)] * 3
+        + [pltpu.VMEM((total, units), BF)] * 3
+        + [pltpu.VMEM((cut, 128), BF), pltpu.VMEM((cut, cut), BF), pltpu.VMEM((cut, 128), BF)]
+        + [pltpu.SemaphoreType.DMA(()), pltpu.SemaphoreType.DMA((3, depth))],
+        compiler_params=params(VMEM_MOST),
+    )(me, blocks, rows, gate_w, up_w, down_w)
 
 
 def scalars(here, routes, weights, regions):
@@ -383,8 +403,8 @@
     fold = fold_matrix(regions)
     rests = [dot(fold, back[:, (depth + half) * lanes : (depth + half + 1) * lanes]).astype(BF) for half in range(quarter)]
     for z in range(depth):
-        part = z // quarter
-        rest = rests[z % quarter][part * few : (part + 1) * few]
+        part = z % 4
+        rest = rests[z // 4][part * few : (part + 1) * few]
         rows = jnp.concatenate([back[:, z * lanes : (z + 1) * lanes], rest], axis=0)
         share = (dot(high, rows, TN) + dot(low, rows, TN)).astype(BF)
         out[z, :count] = share
@@ -459,7 +479,7 @@
     row = lax.broadcasted_iota(jnp.int32, (8, count), 0)
     columns = jnp.transpose(jnp.where(row == 0, comb[2], jnp.where(row == 1, inv, 0.0)))
     inner, inv = columns[:, 0:1], columns[:, 1:2]
-    scaled = gain[...] * jnp.concatenate([grad, early[:, EARLY:]], axis=1)
+    scaled = gain[...].reshape(1, -1) * jnp.concatenate([grad, early[:, EARLY:]], axis=1)
     grad_out[...] = (inv * scaled - wide * (inv * inv * inv * inner / full)).astype(BF)
 
 
@@ -499,17 +519,15 @@
     return lax.ppermute(array, "local", [(z, (z + step) % depth) for z in range(depth)])
 
 
-def ring_gather(own, packed):
+def ring_gather(own):
     half = lax.axis_size("local") // 2
     low, high = own, own
     blocks = [own]
-    for at in range(half - 1):
+    for _ in range(half - 1):
         low, high = lax.optimization_barrier((hop(low, 1), hop(high, -1)))
-        if at == 0:
-            low, high, packed = lax.optimization_barrier((low, high, packed))
         blocks += [low, high]
     cut = (own.shape[0] - EXTRA) // 2
-    return blocks + [hop(low[:cut], 1), hop(high[cut:], -1)], packed
+    return blocks + [hop(low[:cut], 1), hop(high[cut:], -1)]
 
 
 def ring_scatter(shares, right, left):
@@ -525,15 +543,15 @@
     depth = lax.axis_size("local")
     me = lax.axis_index("local").astype(jnp.int32).reshape(1)
     full = depth * tokens.shape[1]
-    gain = norm_gain.reshape(1, -1)
+    gain = norm_gain
     routes, weights = routes.T, combine.T
     packed, early = pack(tokens, gain, grad_out, routes, regions)
-    around, packed = ring_gather(early, packed)
-    arrived, _ = lax.optimization_barrier((swap(packed, regions), around[-3]))
+    around = ring_gather(early)
+    arrived, _ = lax.optimization_barrier((swap(packed, regions), around[4]))
     blocks = lax.all_gather(arrived, "local")
-    rows = swap(pack_early(around, routes, regions, depth, full), regions)
-    hidden = hidden_part(me, blocks, rows, w_gate, w_up, w_down, regions)
-    partial, back_rows = back_part(me, *hidden, w_gate, w_up, w_down, regions, depth)
+    early_rows = pack_early(around, routes, regions, depth, full)
+    rows = swap(early_rows, regions)
+    partial, back_rows = expert_part(me, blocks, rows, w_gate, w_up, w_down, regions)
     summed = lax.psum_scatter(partial, "local", scatter_dimension=0)
     shares, right, left = combine_early(early, swap(back_rows, regions), routes, weights, regions, depth)
     right, left = ring_scatter(shares, right, left)

time: 251 us -> 249 us (level)
  Pallas kernels: 37.2 us -> 33.7 us
    pallas_call x2 -> x1, Pallas kernels: 26.9 us -> 23.3 us  [expert_part(): pl.pallas_call(functools.partial(expert_kernel, regions, depth), in_specs...]
where the time goes in v5:
time: 249 us; the launch traced here: 248 us
  waiting for transfers between devices  132 us (53%)
  starting transfers between devices  62.8 us (25%)
  Pallas kernels  33.7 us (14%)
  between operations  14.2 us (6%)
  local copies, waits for them, and re-layouts  5.19 us (2%)
    all_to_all x4, waiting for transfers between devices, swap(): lax.all_to_all(split, 'region', split_axis=0, concat_axis=0, tiled=True)  94.6 us
    ppermute x16, waiting for transfers between devices, hop(): lax.ppermute(array, 'local', [(z, (z + step) % depth) for z in range(dept...  37.7 us
    all_to_all x4, starting transfers between devices, swap(): lax.all_to_all(split, 'region', split_axis=0, concat_axis=0, tiled=True)  33.6 us
    ppermute x16, starting transfers between devices, hop(): lax.ppermute(array, 'local', [(z, (z + step) % depth) for z in range(dept...  29.2 us
    pallas_call x1, Pallas kernels, expert_part(): pl.pallas_call(functools.partial(expert_kernel, regions, depth), in_specs...  23.3 us
    pallas_call x3, Pallas kernels, once(): pl.pallas_call(kernel, grid=(1,), in_specs=[whole(operand.shape) for oper...  8.63 us
  transfers between devices with their start and end apart: 22, of which 10 were waited for; matrix products, arithmetic and copies ran while one was open for 0% of the time, Pallas kernels for 3%

profile of v5, /device:TPU:2, one launch (start us, length us, event | category | flops | bytes accessed | tf_op | source)
XLA Modules:
  0.0 248.2 jit_solution(8815753606816727872)
XLA Ops:
  7.2 2.6 %shard_map.103 = (bf16[256,1280]{1,0:T(8,128)(2,1)}, bf16[144,768]{1,0:T(8,128)(2,1)}) custom-call(bf16[128,896]{1,0:T(8,128)(2,1)} %tok.3, f32[896]{0:T(1024)} %gain.3, bf16[128,896]{1,0:T(8,128)(2,1)} %grad.1, s32[2,128]{1,0:T(2,128)} %bitcast.15), custom_call_target="tpu_custom_call" | custom-call | tf_op jit(solution)/shard_map/pallas_call | solution.py:111
  9.7 7.6 %all-to-all-start = ((bf16[32,8,1280]{2,1,0:T(8,128)(2,1)}), bf16[32,8,1280]{2,1,0:T(8,128)(2,1)S(1)}, u32[]{:S(2)}, u32[]{:S(2)}) async-start(bf16[32,8,1280]{2,1,0:T(8,128)(2,1)} %bitcast.25), calls=%async_computation | async-start | bytes 1310720 | tf_op jit(solution)/shard_map/all_to_all | solution.py:513
  17.4 0.0 all-gather.3.cloned.1.call-start
  17.4 5.9 %collective-permute-start.1 = (bf16[144,768]{1,0:T(8,128)(2,1)}, bf16[144,768]{1,0:T(8,128)(2,1)S(1)}, u32[]{:S(2)}, u32[]{:S(2)}) collective-permute-start(bf16[144,768]{1,0:T(8,128)(2,1)} %get-tuple-element.27.refs_0_), channel_id=1, source_target_pairs={{0,7},{1,0},{2,1},{3,2},{4,3},{5,4},{6,5},{7,6},{8,15},{9,8},{10,9... | collective-permute-start | bytes 663560 | tf_op jit(solution)/shard_map/ppermute | solution.py:519
  23.4 5.3 %collective-permute-done.1.refs_2_ = bf16[144,768]{1,0:T(8,128)(2,1)S(1)} collective-permute-done((bf16[144,768]{1,0:T(8,128)(2,1)}, bf16[144,768]{1,0:T(8,128)(2,1)S(1)}, u32[]{:S(2)}, u32[]{:S(2)}) %collective-permute-start.1) | collective-permute-done | bytes 221216 | tf_op jit(solution)/shard_map/ppermute | solution.py:519
  28.7 3.3 %collective-permute-done.refs_1_ = bf16[144,768]{1,0:T(8,128)(2,1)S(1)} collective-permute-done((bf16[144,768]{1,0:T(8,128)(2,1)}, bf16[144,768]{1,0:T(8,128)(2,1)S(1)}, u32[]{:S(2)}, u32[]{:S(2)}) %collective-permute-start) | collective-permute-done | bytes 221216 | tf_op jit(solution)/shard_map/ppermute | solution.py:519
  32.0 3.2 %collective-permute-start.3 = (bf16[144,768]{1,0:T(8,128)(2,1)S(1)}, bf16[144,768]{1,0:T(8,128)(2,1)S(1)}, u32[]{:S(2)}, u32[]{:S(2)}) collective-permute-start(bf16[144,768]{1,0:T(8,128)(2,1)S(1)} %collective-permute-done.1.refs_2_), channel_id=1, source_target_pairs={{0,7},{1,0},{2,1},{3,2},{4,3},{5,4},{6,5},{7,6},{8,15},{9,8},{10,9... | collective-permute-start | bytes 663560 | tf_op jit(solution)/shard_map/ppermute | solution.py:519
  35.2 4.3 %collective-permute-done.2.refs_3_ = bf16[144,768]{1,0:T(8,128)(2,1)S(1)} collective-permute-done((bf16[144,768]{1,0:T(8,128)(2,1)S(1)}, bf16[144,768]{1,0:T(8,128)(2,1)S(1)}, u32[]{:S(2)}, u32[]{:S(2)}) %collective-permute-start.2) | collective-permute-done | bytes 221216 | tf_op jit(solution)/shard_map/ppermute | solution.py:519
  39.5 0.8 copy-done.7
  40.4 0.0 all-gather.3.cloned.1.call-update
  40.4 0.1 collective-permute-start.4
  40.5 3.2 %collective-permute-start.5 = (bf16[144,768]{1,0:T(8,128)(2,1)S(1)}, bf16[144,768]{1,0:T(8,128)(2,1)S(1)}, u32[]{:S(2)}, u32[]{:S(2)}) collective-permute-start(bf16[144,768]{1,0:T(8,128)(2,1)S(1)} %collective-permute-done.3.refs_4_), channel_id=1, source_target_pairs={{0,7},{1,0},{2,1},{3,2},{4,3},{5,4},{6,5},{7,6},{8,15},{9,8},{10,9... | collective-permute-start | bytes 663560 | tf_op jit(solution)/shard_map/ppermute | solution.py:519
  43.7 3.9 %collective-permute-done.4.refs_5_ = bf16[144,768]{1,0:T(8,128)(2,1)S(1)} collective-permute-done((bf16[144,768]{1,0:T(8,128)(2,1)S(1)}, bf16[144,768]{1,0:T(8,128)(2,1)S(1)}, u32[]{:S(2)}, u32[]{:S(2)}) %collective-permute-start.4) | collective-permute-done | bytes 221216 | tf_op jit(solution)/shard_map/ppermute | solution.py:519
  47.6 3.3 %collective-permute-start.7 = (bf16[80,768]{1,0:T(8,128)(2,1)S(1)}, bf16[80,768]{1,0:T(8,128)(2,1)S(1)}, u32[]{:S(2)}, u32[]{:S(2)}) collective-permute-start(bf16[80,768]{1,0:T(8,128)(2,1)S(1)} %slice.10), channel_id=1, source_target_pairs={{0,7},{1,0},{2,1},{3,2},{4,3},{5,4},{6,5},{7,6},{8,15},{9,8},{10,9... | collective-permute-start | bytes 368648 | tf_op jit(solution)/shard_map/ppermute | solution.py:519
  50.9 0.1 collective-permute-start.6
  51.0 7.9 %collective-permute-done.6.refs_7_ = bf16[64,768]{1,0:T(8,128)(2,1)S(1)} collective-permute-done((bf16[64,768]{1,0:T(8,128)(2,1)S(1)}, bf16[64,768]{1,0:T(8,128)(2,1)S(1)}, u32[]{:S(2)}, u32[]{:S(2)}) %collective-permute-start.6) | collective-permute-done | bytes 98336 | tf_op jit(solution)/shard_map/ppermute | solution.py:519
  58.9 0.9 copy-done.2
  59.8 0.7 copy-done.4
  60.5 1.7 shard_map.104
  62.2 2.0 copy-done
  64.2 7.4 %all-to-all-start.1 = ((bf16[32,8,7808]{2,1,0:T(8,128)(2,1)}), bf16[32,8,7808]{2,1,0:T(8,128)(2,1)}, u32[]{:S(2)}, u32[]{:S(2)}) async-start(bf16[32,8,7808]{2,1,0:T(8,128)(2,1)} %bitcast.13), calls=%async_computation.1 | async-start | bytes 7995392 | tf_op jit(solution)/shard_map/all_to_all | solution.py:513
  71.6 0.0 reduce-scatter.2.cloned.1.call-start
  71.7 47.6 %all-to-all-done.1 = bf16[32,8,7808]{2,1,0:T(8,128)(2,1)} async-done(((bf16[32,8,7808]{2,1,0:T(8,128)(2,1)}), bf16[32,8,7808]{2,1,0:T(8,128)(2,1)}, u32[]{:S(2)}, u32[]{:S(2)}) %all-to-all-start.1) | async-done | bytes 3997728 | tf_op jit(solution)/shard_map/all_to_all | solution.py:513
  119.3 23.3 %shard_map.105 = (bf16[8,256,1280]{2,1,0:T(8,128)(2,1)}, bf16[256,7808]{1,0:T(8,128)(2,1)}) custom-call(s32[1]{0:T(128)} %bitcast.me, bf16[8,256,1280]{2,1,0:T(8,128)(2,1)} %bitcast.21, bf16[256,7808]{1,0:T(8,128)(2,1)} %bitcast.6.rows, bf16[1,7168,256]{2,1,0:T(8,128)(2,1)} %gate_hbm.1, bf16[1,7168,256]{2,1,0:T(8,128)(2,1)} %up_hbm.1, ...), custom_call_target="tpu_custom_call" | custom-call | tf_op jit(solution)/shard_map/pallas_call | solution.py:358
  142.6 0.0 reduce-scatter.2.cloned.1.call-update
  142.7 0.0 copy-start.5
  142.7 0.0 copy-start.6
  142.7 9.3 %all-to-all-start.3 = ((bf16[32,8,7808]{2,1,0:T(8,128)(2,1)}), bf16[32,8,7808]{2,1,0:T(8,128)(2,1)}, u32[]{:S(2)}, u32[]{:S(2)}) async-start(bf16[32,8,7808]{2,1,0:T(8,128)(2,1)} %bitcast.22), calls=%async_computation.4 | async-start | bytes 7995392 | tf_op jit(solution)/shard_map/all_to_all | solution.py:513
  152.0 0.7 slice.11.squares
  152.7 46.9 %all-to-all-done.3 = bf16[32,8,7808]{2,1,0:T(8,128)(2,1)} async-done(((bf16[32,8,7808]{2,1,0:T(8,128)(2,1)}), bf16[32,8,7808]{2,1,0:T(8,128)(2,1)}, u32[]{:S(2)}, u32[]{:S(2)}) %all-to-all-start.3) | async-done | bytes 3997728 | tf_op jit(solution)/shard_map/all_to_all | solution.py:513
  199.7 4.3 %shard_map.106 = (bf16[8,144,768]{2,1,0:T(8,128)(2,1)S(1)}, bf16[80,768]{1,0:T(8,128)(2,1)S(1)}, bf16[80,768]{1,0:T(8,128)(2,1)S(1)}) custom-call(bf16[16,768]{1,0:T(8,128)(2,1)S(1)} %slice.11.squares, bf16[256,7808]{1,0:T(8,128)(2,1)} %bitcast.10.back, s32[2,128]{1,0:T(2,128)S(1)} %bitcast.17, f32[2,128]{1,0:T(2,128)S(1)} %bitcast.19), custom_call_target="tpu_custom_call" | custom-call | tf_op jit(solution)/shard_map/pallas_call | solution.py:111
  204.0 0.1 collective-permute-start.8
  204.1 3.2 %collective-permute-start.9 = (bf16[80,768]{1,0:T(8,128)(2,1)S(1)}, bf16[80,768]{1,0:T(8,128)(2,1)S(1)}, u32[]{:S(2)}, u32[]{:S(2)}) collective-permute-start(bf16[80,768]{1,0:T(8,128)(2,1)S(1)} %get-tuple-element.39), channel_id=1, source_target_pairs={{0,7},{1,0},{2,1},{3,2},{4,3},{5,4},{6,5},{7,6},{8,15},{9,8},{10,9... | collective-permute-start | bytes 368648 | tf_op jit(solution)/shard_map/ppermute | solution.py:519
  207.3 2.9 %collective-permute-done.8.right = bf16[80,768]{1,0:T(8,128)(2,1)S(1)} collective-permute-done((bf16[80,768]{1,0:T(8,128)(2,1)S(1)}, bf16[80,768]{1,0:T(8,128)(2,1)S(1)}, u32[]{:S(2)}, u32[]{:S(2)}) %collective-permute-start.8) | collective-permute-done | bytes 122912 | tf_op jit(solution)/shard_map/ppermute | solution.py:519
  210.2 0.1 shard_map.107
  210.2 0.1 collective-permute-start.10
  210.3 3.3 %collective-permute-start.11 = (bf16[144,768]{1,0:T(8,128)(2,1)S(1)}, bf16[144,768]{1,0:T(8,128)(2,1)S(1)}, u32[]{:S(2)}, u32[]{:S(2)}) collective-permute-start(bf16[144,768]{1,0:T(8,128)(2,1)S(1)} %get-tuple-element.41), channel_id=1, source_target_pairs={{0,7},{1,0},{2,1},{3,2},{4,3},{5,4},{6,5},{7,6},{8,15},{9,8},{10,9... | collective-permute-start | bytes 663560 | tf_op jit(solution)/shard_map/ppermute | solution.py:519
  213.6 9.3 %all-to-all-start.2 = ((bf16[32,8,1280]{2,1,0:T(8,128)(2,1)}), bf16[32,8,1280]{2,1,0:T(8,128)(2,1)S(1)}, u32[]{:S(2)}, u32[]{:S(2)}) async-start(bf16[32,8,1280]{2,1,0:T(8,128)(2,1)} %bitcast.24), calls=%async_computation.3 | async-start | bytes 1310720 | tf_op jit(solution)/shard_map/all_to_all | solution.py:513
  222.9 0.0 copy-start.1
  223.0 0.1 shard_map.108
  223.1 0.1 collective-permute-start.12
  223.2 3.2 %collective-permute-start.13 = (bf16[144,768]{1,0:T(8,128)(2,1)S(1)}, bf16[144,768]{1,0:T(8,128)(2,1)S(1)}, u32[]{:S(2)}, u32[]{:S(2)}) collective-permute-start(bf16[144,768]{1,0:T(8,128)(2,1)S(1)} %get-tuple-element.43), channel_id=1, source_target_pairs={{0,7},{1,0},{2,1},{3,2},{4,3},{5,4},{6,5},{7,6},{8,15},{9,8},{10,9... | collective-permute-start | bytes 663560 | tf_op jit(solution)/shard_map/ppermute | solution.py:519
  226.4 5.5 %collective-permute-done.12.right = bf16[144,768]{1,0:T(8,128)(2,1)S(1)} collective-permute-done((bf16[144,768]{1,0:T(8,128)(2,1)S(1)}, bf16[144,768]{1,0:T(8,128)(2,1)S(1)}, u32[]{:S(2)}, u32[]{:S(2)}) %collective-permute-start.12) | collective-permute-done | bytes 221216 | tf_op jit(solution)/shard_map/ppermute | solution.py:519
  231.8 0.1 shard_map.109
  231.9 0.1 collective-permute-start.14
  232.0 3.2 %collective-permute-start.15 = (bf16[144,768]{1,0:T(8,128)(2,1)S(1)}, bf16[144,768]{1,0:T(8,128)(2,1)S(1)}, u32[]{:S(2)}, u32[]{:S(2)}) collective-permute-start(bf16[144,768]{1,0:T(8,128)(2,1)S(1)} %get-tuple-element.45), channel_id=1, source_target_pairs={{0,7},{1,0},{2,1},{3,2},{4,3},{5,4},{6,5},{7,6},{8,15},{9,8},{10,9... | collective-permute-start | bytes 663560 | tf_op jit(solution)/shard_map/ppermute | solution.py:519
  235.2 4.6 %collective-permute-done.14.right = bf16[144,768]{1,0:T(8,128)(2,1)S(1)} collective-permute-done((bf16[144,768]{1,0:T(8,128)(2,1)S(1)}, bf16[144,768]{1,0:T(8,128)(2,1)S(1)}, u32[]{:S(2)}, u32[]{:S(2)}) %collective-permute-start.14) | collective-permute-done | bytes 221216 | tf_op jit(solution)/shard_map/ppermute | solution.py:519
  239.9 1.4 shard_map.110
  (25 shorter events, 0.1 us)
Async XLA Ops:
  9.7 29.8 %all-to-all-start = ((bf16[32,8,1280]{2,1,0:T(8,128)(2,1)}), bf16[32,8,1280]{2,1,0:T(8,128)(2,1)S(1)}, u32[]{:S(2)}, u32[]{:S(2)}) async-start(bf16[32,8,1280]{2,1,0:T(8,128)(2,1)} %bitcast.25), calls=%async_computation | async-start | bytes 1310720 | tf_op jit(solution)/shard_map/all_to_all | solution.py:513
  17.4 101.9 %all-gather.3.cloned.1.call-start = ((), (), s32[]{:S(2)}) async-start(), calls=%async_computation.6 | async-start | bytes 5898240 | tf_op jit(solution)/shard_map/all_gather | solution.py:551
  17.4 11.3 %collective-permute-start.1 = (bf16[144,768]{1,0:T(8,128)(2,1)}, bf16[144,768]{1,0:T(8,128)(2,1)S(1)}, u32[]{:S(2)}, u32[]{:S(2)}) collective-permute-start(bf16[144,768]{1,0:T(8,128)(2,1)} %get-tuple-element.27.refs_0_), channel_id=1, source_target_pairs={{0,7},{1,0},{2,1},{3,2},{4,3},{5,4},{6,5},{7,6},{8,15},{9,8},{10,9... | collective-permute-start | bytes 663560 | tf_op jit(solution)/shard_map/ppermute | solution.py:519
  23.4 8.6 %collective-permute-start = (bf16[144,768]{1,0:T(8,128)(2,1)}, bf16[144,768]{1,0:T(8,128)(2,1)S(1)}, u32[]{:S(2)}, u32[]{:S(2)}) collective-permute-start(bf16[144,768]{1,0:T(8,128)(2,1)} %get-tuple-element.27.refs_0_), channel_id=1, source_target_pairs={{0,1},{1,2},{2,3},{3,4},{4,5},{5,6},{6,7},{7,0},{8,9},{9,10},{10,1... | collective-permute-start | bytes 663560 | tf_op jit(solution)/shard_map/ppermute | solution.py:519
  32.0 7.5 %collective-permute-start.2 = (bf16[144,768]{1,0:T(8,128)(2,1)S(1)}, bf16[144,768]{1,0:T(8,128)(2,1)S(1)}, u32[]{:S(2)}, u32[]{:S(2)}) collective-permute-start(bf16[144,768]{1,0:T(8,128)(2,1)S(1)} %collective-permute-done.refs_1_), channel_id=1, source_target_pairs={{0,1},{1,2},{2,3},{3,4},{4,5},{5,6},{6,7},{7,0},{8,9},{9,10},{10,1... | collective-permute-start | bytes 663560 | tf_op jit(solution)/shard_map/ppermute | solution.py:519
  32.0 7.5 %collective-permute-start.3 = (bf16[144,768]{1,0:T(8,128)(2,1)S(1)}, bf16[144,768]{1,0:T(8,128)(2,1)S(1)}, u32[]{:S(2)}, u32[]{:S(2)}) collective-permute-start(bf16[144,768]{1,0:T(8,128)(2,1)S(1)} %collective-permute-done.1.refs_2_), channel_id=1, source_target_pairs={{0,7},{1,0},{2,1},{3,2},{4,3},{5,4},{6,5},{7,6},{8,15},{9,8},{10,9... | collective-permute-start | bytes 663560 | tf_op jit(solution)/shard_map/ppermute | solution.py:519
  39.5 0.8 copy-start.7
  40.4 7.2 %collective-permute-start.4 = (bf16[144,768]{1,0:T(8,128)(2,1)S(1)}, bf16[144,768]{1,0:T(8,128)(2,1)S(1)}, u32[]{:S(2)}, u32[]{:S(2)}) collective-permute-start(bf16[144,768]{1,0:T(8,128)(2,1)S(1)} %collective-permute-done.2.refs_3_), channel_id=1, source_target_pairs={{0,1},{1,2},{2,3},{3,4},{4,5},{5,6},{6,7},{7,0},{8,9},{9,10},{10,1... | collective-permute-start | bytes 663560 | tf_op jit(solution)/shard_map/ppermute | solution.py:519
  40.5 7.1 %collective-permute-start.5 = (bf16[144,768]{1,0:T(8,128)(2,1)S(1)}, bf16[144,768]{1,0:T(8,128)(2,1)S(1)}, u32[]{:S(2)}, u32[]{:S(2)}) collective-permute-start(bf16[144,768]{1,0:T(8,128)(2,1)S(1)} %collective-permute-done.3.refs_4_), channel_id=1, source_target_pairs={{0,7},{1,0},{2,1},{3,2},{4,3},{5,4},{6,5},{7,6},{8,15},{9,8},{10,9... | collective-permute-start | bytes 663560 | tf_op jit(solution)/shard_map/ppermute | solution.py:519
  47.6 11.3 %collective-permute-start.7 = (bf16[80,768]{1,0:T(8,128)(2,1)S(1)}, bf16[80,768]{1,0:T(8,128)(2,1)S(1)}, u32[]{:S(2)}, u32[]{:S(2)}) collective-permute-start(bf16[80,768]{1,0:T(8,128)(2,1)S(1)} %slice.10), channel_id=1, source_target_pairs={{0,7},{1,0},{2,1},{3,2},{4,3},{5,4},{6,5},{7,6},{8,15},{9,8},{10,9... | collective-permute-start | bytes 368648 | tf_op jit(solution)/shard_map/ppermute | solution.py:519
  50.9 7.9 %collective-permute-start.6 = (bf16[64,768]{1,0:T(8,128)(2,1)S(1)}, bf16[64,768]{1,0:T(8,128)(2,1)S(1)}, u32[]{:S(2)}, u32[]{:S(2)}) collective-permute-start(bf16[64,768]{1,0:T(8,128)(2,1)S(1)} %slice.9), channel_id=1, source_target_pairs={{0,1},{1,2},{2,3},{3,4},{4,5},{5,6},{6,7},{7,0},{8,9},{9,10},{10,1... | collective-permute-start | bytes 294920 | tf_op jit(solution)/shard_map/ppermute | solution.py:519
  58.9 0.9 copy-start.2
  59.8 0.7 copy-start.4
  62.2 2.0 copy-start
  64.2 55.1 %all-to-all-start.1 = ((bf16[32,8,7808]{2,1,0:T(8,128)(2,1)}), bf16[32,8,7808]{2,1,0:T(8,128)(2,1)}, u32[]{:S(2)}, u32[]{:S(2)}) async-start(bf16[32,8,7808]{2,1,0:T(8,128)(2,1)} %bitcast.13), calls=%async_computation.1 | async-start | bytes 7995392 | tf_op jit(solution)/shard_map/all_to_all | solution.py:513
  71.6 142.0 %reduce-scatter.2.cloned.1.call-start = ((), (), s32[]{:S(2)}) async-start(), calls=%async_computation.5 | async-start | bytes 5898240 | tf_op jit(solution)/shard_map/reduce_scatter | solution.py:555
  142.7 57.0 %copy-start.5 = (s32[128,2]{0,1:T(2,128)S(1)}, s32[128,2]{0,1:T(2,128)}, u32[]{:S(2)}) copy-start(s32[128,2]{0,1:T(2,128)} %param.13) | copy-start | bytes 3076
  142.7 57.0 %copy-start.6 = (f32[128,2]{0,1:T(2,128)S(1)}, f32[128,2]{0,1:T(2,128)}, u32[]{:S(2)}) copy-start(f32[128,2]{0,1:T(2,128)} %param.14) | copy-start | bytes 3076
  142.7 57.0 %all-to-all-start.3 = ((bf16[32,8,7808]{2,1,0:T(8,128)(2,1)}), bf16[32,8,7808]{2,1,0:T(8,128)(2,1)}, u32[]{:S(2)}, u32[]{:S(2)}) async-start(bf16[32,8,7808]{2,1,0:T(8,128)(2,1)} %bitcast.22), calls=%async_computation.4 | async-start | bytes 7995392 | tf_op jit(solution)/shard_map/all_to_all | solution.py:513
  204.0 6.2 %collective-permute-start.8 = (bf16[80,768]{1,0:T(8,128)(2,1)S(1)}, bf16[80,768]{1,0:T(8,128)(2,1)S(1)}, u32[]{:S(2)}, u32[]{:S(2)}) collective-permute-start(bf16[80,768]{1,0:T(8,128)(2,1)S(1)} %get-tuple-element.38), channel_id=1, source_target_pairs={{0,1},{1,2},{2,3},{3,4},{4,5},{5,6},{6,7},{7,0},{8,9},{9,10},{10,1... | collective-permute-start | bytes 368648 | tf_op jit(solution)/shard_map/ppermute | solution.py:519
  204.1 6.1 %collective-permute-start.9 = (bf16[80,768]{1,0:T(8,128)(2,1)S(1)}, bf16[80,768]{1,0:T(8,128)(2,1)S(1)}, u32[]{:S(2)}, u32[]{:S(2)}) collective-permute-start(bf16[80,768]{1,0:T(8,128)(2,1)S(1)} %get-tuple-element.39), channel_id=1, source_target_pairs={{0,7},{1,0},{2,1},{3,2},{4,3},{5,4},{6,5},{7,6},{8,15},{9,8},{10,9... | collective-permute-start | bytes 368648 | tf_op jit(solution)/shard_map/ppermute | solution.py:519
  210.2 12.7 %collective-permute-start.10 = (bf16[144,768]{1,0:T(8,128)(2,1)S(1)}, bf16[144,768]{1,0:T(8,128)(2,1)S(1)}, u32[]{:S(2)}, u32[]{:S(2)}) collective-permute-start(bf16[144,768]{1,0:T(8,128)(2,1)S(1)} %get-tuple-element.40), channel_id=1, source_target_pairs={{0,1},{1,2},{2,3},{3,4},{4,5},{5,6},{6,7},{7,0},{8,9},{9,10},{10,1... | collective-permute-start | bytes 663560 | tf_op jit(solution)/shard_map/ppermute | solution.py:519
  210.3 12.6 %collective-permute-start.11 = (bf16[144,768]{1,0:T(8,128)(2,1)S(1)}, bf16[144,768]{1,0:T(8,128)(2,1)S(1)}, u32[]{:S(2)}, u32[]{:S(2)}) collective-permute-start(bf16[144,768]{1,0:T(8,128)(2,1)S(1)} %get-tuple-element.41), channel_id=1, source_target_pairs={{0,7},{1,0},{2,1},{3,2},{4,3},{5,4},{6,5},{7,6},{8,15},{9,8},{10,9... | collective-permute-start | bytes 663560 | tf_op jit(solution)/shard_map/ppermute | solution.py:519
  213.6 26.2 %all-to-all-start.2 = ((bf16[32,8,1280]{2,1,0:T(8,128)(2,1)}), bf16[32,8,1280]{2,1,0:T(8,128)(2,1)S(1)}, u32[]{:S(2)}, u32[]{:S(2)}) async-start(bf16[32,8,1280]{2,1,0:T(8,128)(2,1)} %bitcast.24), calls=%async_computation.3 | async-start | bytes 1310720 | tf_op jit(solution)/shard_map/all_to_all | solution.py:513
  222.9 17.0 %copy-start.1 = (bf16[128,896]{1,0:T(8,128)(2,1)S(1)}, bf16[128,896]{1,0:T(8,128)(2,1)}, u32[]{:S(2)}) copy-start(bf16[128,896]{1,0:T(8,128)(2,1)} %tok.3) | copy-start | bytes 688132
  222.9 17.0 %copy-start.3 = (f32[896]{0:T(1024)S(1)}, f32[896]{0:T(1024)}, u32[]{:S(2)}) copy-start(f32[896]{0:T(1024)} %gain.3) | copy-start | bytes 10756
  223.1 8.8 %collective-permute-start.12 = (bf16[144,768]{1,0:T(8,128)(2,1)S(1)}, bf16[144,768]{1,0:T(8,128)(2,1)S(1)}, u32[]{:S(2)}, u32[]{:S(2)}) collective-permute-start(bf16[144,768]{1,0:T(8,128)(2,1)S(1)} %get-tuple-element.42), channel_id=1, source_target_pairs={{0,1},{1,2},{2,3},{3,4},{4,5},{5,6},{6,7},{7,0},{8,9},{9,10},{10,1... | collective-permute-start | bytes 663560 | tf_op jit(solution)/shard_map/ppermute | solution.py:519
  223.2 8.7 %collective-permute-start.13 = (bf16[144,768]{1,0:T(8,128)(2,1)S(1)}, bf16[144,768]{1,0:T(8,128)(2,1)S(1)}, u32[]{:S(2)}, u32[]{:S(2)}) collective-permute-start(bf16[144,768]{1,0:T(8,128)(2,1)S(1)} %get-tuple-element.43), channel_id=1, source_target_pairs={{0,7},{1,0},{2,1},{3,2},{4,3},{5,4},{6,5},{7,6},{8,15},{9,8},{10,9... | collective-permute-start | bytes 663560 | tf_op jit(solution)/shard_map/ppermute | solution.py:519
  231.9 7.9 %collective-permute-start.14 = (bf16[144,768]{1,0:T(8,128)(2,1)S(1)}, bf16[144,768]{1,0:T(8,128)(2,1)S(1)}, u32[]{:S(2)}, u32[]{:S(2)}) collective-permute-start(bf16[144,768]{1,0:T(8,128)(2,1)S(1)} %get-tuple-element.44), channel_id=1, source_target_pairs={{0,1},{1,2},{2,3},{3,4},{4,5},{5,6},{6,7},{7,0},{8,9},{9,10},{10,1... | collective-permute-start | bytes 663560 | tf_op jit(solution)/shard_map/ppermute | solution.py:519
  232.0 7.9 %collective-permute-start.15 = (bf16[144,768]{1,0:T(8,128)(2,1)S(1)}, bf16[144,768]{1,0:T(8,128)(2,1)S(1)}, u32[]{:S(2)}, u32[]{:S(2)}) collective-permute-start(bf16[144,768]{1,0:T(8,128)(2,1)S(1)} %get-tuple-element.45), channel_id=1, source_target_pairs={{0,7},{1,0},{2,1},{3,2},{4,3},{5,4},{6,5},{7,6},{8,15},{9,8},{10,9... | collective-permute-start | bytes 663560 | tf_op jit(solution)/shard_map/ppermute | solution.py:519
Sparse Core Ops, SparseCore 0:
  40.5 64.1 all-gather.2
  142.8 64.3 reduce-scatter.1

commit v6 on v5

--- a/solution.py
+++ b/solution.py
@@ -14,15 +14,20 @@
 VMEM_MOST = 63 * 1024 * 1024
 VMEM_SOME = 40 * 1024 * 1024
 EXTRA = 16
-EARLY = 384
-
-
-def fold_lanes(width):
-    return 128 * -(-width // 256)
-
-
-def packed_lanes(width):
-    return 2 * width + fold_lanes(width)
+EARLY = (384, 256)
+EARLY_LANES = sum(EARLY)
+
+
+def late_widths(width):
+    return [width - early for early in EARLY]
+
+
+def fold_lanes(widths):
+    return max(128 * -(-width // 256) for width in widths)
+
+
+def packed_lanes(widths):
+    return sum(widths) + fold_lanes(widths)
 
 
 def dot(a, b, dims=(((1,), (0,)), ((), ())), precision=None):
@@ -44,32 +49,34 @@
     return (j == 4 * (i % (2 * regions)) + i // (2 * regions)).astype(BF)
 
 
-def encode(main, rest, fold):
-    width = main.shape[1] // 2
-    lanes = fold_lanes(width)
-    pad = 2 * lanes - width
+def encode(main, rest, fold, widths):
+    lanes = fold_lanes(widths)
     parts = []
-    for side in range(2):
-        parts.append(rest[:, side * width : side * width + lanes])
-        tail = rest[:, side * width + lanes : (side + 1) * width]
+    start = 0
+    for width in widths:
+        parts.append(rest[:, start : start + lanes])
+        tail = rest[:, start + lanes : start + width]
+        pad = 2 * lanes - width
         if pad:
             tail = jnp.concatenate([tail, jnp.zeros((rest.shape[0], pad), rest.dtype)], axis=1)
         parts.append(tail)
+        start += width
     stacked = jnp.concatenate(parts, axis=0)
     return jnp.concatenate([main, dot(fold, stacked, TN).astype(BF)], axis=1)
 
 
-def decode(block, width, fold):
-    lanes = fold_lanes(width)
-    rows = block.shape[0]
-    rest = dot(fold, block[:, 2 * width :]).astype(BF)
-    few = rows // 4
+def decode(block, widths, fold):
+    lanes = fold_lanes(widths)
+    few = block.shape[0] // 4
+    rest = dot(fold, block[:, sum(widths) :]).astype(BF)
     sides = []
-    for side in range(2):
+    start = 0
+    for side, width in enumerate(widths):
         head = rest[(2 * side) * few : (2 * side + 1) * few]
         tail = rest[(2 * side + 1) * few : (2 * side + 2) * few, : width - lanes]
         low = jnp.concatenate([head, tail], axis=1)
-        sides.append(jnp.concatenate([block[:, side * width : (side + 1) * width], low], axis=0))
+        sides.append(jnp.concatenate([block[:, start : start + width], low], axis=0))
+        start += width
     return sides
 
 
@@ -152,14 +159,14 @@
 def pack_kernel(regions, tok, gain, grad, routes, out, early):
     at = placed(routes[...], regions)
     pick = (at[0] | at[1]).astype(F32).astype(BF)
-    late = out.shape[1] * 2 // 5
+    late = late_widths(tok.shape[1])
     count = tok.shape[0]
     wide = tok[...].astype(F32)
     scaled = (wide * gain[...].reshape(1, -1)).astype(BF)
-    rows = dot(pick, jnp.concatenate([scaled[:, :late], grad[:, :late]], axis=1)).astype(BF)
+    rows = dot(pick, jnp.concatenate([scaled[:, : late[0]], grad[:, : late[1]]], axis=1)).astype(BF)
     cut = 8 * regions
-    out[...] = encode(rows[:cut], rows[cut:], fold_matrix(regions))
-    early[:count] = jnp.concatenate([scaled[:, late:], grad[:, late:]], axis=1)
+    out[...] = encode(rows[:cut], rows[cut:], fold_matrix(regions), late)
+    early[:count] = jnp.concatenate([scaled[:, late[0] :], grad[:, late[1] :]], axis=1)
     squares = jnp.broadcast_to(jnp.sum(wide * wide, axis=1, keepdims=True), (count, 128))
     early[count:] = in_rows(triple(jnp.transpose(squares)[0:1]), early.shape[1])
 
@@ -167,8 +174,8 @@
 def pack(tok, gain, grad, routes, regions):
     count, width = tok.shape
     shapes = [
-        jax.ShapeDtypeStruct((8 * regions, packed_lanes(width - EARLY)), BF),
-        jax.ShapeDtypeStruct((count + EXTRA, 2 * EARLY), BF),
+        jax.ShapeDtypeStruct((8 * regions, packed_lanes(late_widths(width))), BF),
+        jax.ShapeDtypeStruct((count + EXTRA, EARLY_LANES), BF),
     ]
     return once(functools.partial(pack_kernel, regions), shapes, tok, gain, grad, routes, limit=VMEM_MOST)
 
@@ -210,7 +217,7 @@
 
 
 def early_shape(regions, depth):
-    return (8 * regions, 2 * EARLY * depth * 5 // 4 + 128)
+    return (8 * regions, EARLY_LANES * depth * 5 // 4 + 128)
 
 
 def pack_early(blocks, routes, regions, depth, full):
@@ -251,6 +258,7 @@
     width = gate_w.shape[1] // depth
     few = 2 * regions
     cut, lanes = blocks.shape[1:]
+    late = late_widths(width)
     first_block = me[0]
     copy = pltpu.make_async_copy(rows.at[:, rows.shape[1] - 128 :], scales, sem)
     copy.start()
@@ -279,11 +287,11 @@
         at = lanes_of(step)
         for one in weight_copies(step):
             one.wait()
-        late_in, late_grad = decode(block[0], width - EARLY, fold[...])
+        late_in, late_grad = decode(block[0], late, fold[...])
         pick = fold[pl.ds(pl.multiple_of((step % 4) * few, few), few), :]
         early = jnp.concatenate([main[...], dot(pick, rest[...]).astype(BF)], axis=0)
-        rows_in = jnp.concatenate([late_in, early[:, :EARLY]], axis=1)
-        rows_grad = jnp.concatenate([late_grad, early[:, EARLY:]], axis=1)
+        rows_in = jnp.concatenate([late_in, early[:, : EARLY[0]]], axis=1)
+        rows_grad = jnp.concatenate([late_grad, early[:, EARLY[0] :]], axis=1)
         acc_g[...] += dot(rows_in, gate_w[0, at, :])
         acc_u[...] += dot(rows_in, up_w[0, at, :])
         acc_h[...] += dot(rows_grad, down_w[0, :, at], NT)
@@ -293,8 +301,8 @@
         grid=(depth,),
         in_specs=[
             pl.BlockSpec((1, cut, lanes), lambda z: ((z + first_block) % depth, 0, 0)),
-            pl.BlockSpec((cut, 2 * EARLY), lambda z: (0, z)),
-            pl.BlockSpec((cut, 2 * EARLY), lambda z: (0, depth + z // 4)),
+            pl.BlockSpec((cut, EARLY_LANES), lambda z: (0, z)),
+            pl.BlockSpec((cut, EARLY_LANES), lambda z: (0, depth + z // 4)),
         ],
     )(blocks, rows, rows)
 
@@ -316,7 +324,6 @@
     here = in_lanes(triple(comb[:cut]) + triple(inner[:cut]), cut)
     there = in_lanes([None] * 6 + triple(comb[cut:]) + triple(inner[cut:]), few)
     scal[...] = here + dot(first, there, TN).astype(BF)
-    late = width - EARLY
     late_lanes = late_out.shape[2]
 
     def back(late_block, main, rest):
@@ -324,9 +331,9 @@
         at = lanes_of(step)
         moe = dot(hid[...], down_w[0, :, at]).astype(BF)
         grad = (dot(gate_g[...], gate_w[0, at, :], NT) + dot(up_g[...], up_w[0, at, :], NT)).astype(BF)
-        both = jnp.concatenate([moe[:, :late], grad[:, :late]], axis=1)
-        late_block[0] = encode(both[:cut], both[cut:], fold[...])
-        both = jnp.concatenate([moe[:, late:], grad[:, late:]], axis=1)
+        both = jnp.concatenate([moe[:, : late[0]], grad[:, : late[1]]], axis=1)
+        late_block[0] = encode(both[:cut], both[cut:], fold[...], late)
+        both = jnp.concatenate([moe[:, late[0] :], grad[:, late[1] :]], axis=1)
         main[...] = both[:cut]
         pick = fold[pl.ds(pl.multiple_of((step % 4) * few, few), few), :]
         low = dot(pick, both[cut:], TN).astype(BF)
@@ -344,8 +351,8 @@
         grid=(depth,),
         out_specs=[
             pl.BlockSpec((1, cut, late_lanes), lambda z: ((z + first_block) % depth, 0, 0)),
-            pl.BlockSpec((cut, 2 * EARLY), lambda z: (0, z)),
-            pl.BlockSpec((cut, 2 * EARLY), lambda z: (0, depth + z // 4)),
+            pl.BlockSpec((cut, EARLY_LANES), lambda z: (0, z)),
+            pl.BlockSpec((cut, EARLY_LANES), lambda z: (0, depth + z // 4)),
         ],
     )(late_out, early_out, early_out)
     pltpu.sync_copy(scal, early_out.at[:, early_out.shape[1] - 128 :])
@@ -417,13 +424,13 @@
 def combine_early(early, back, routes, weights, regions, depth):
     count = routes.shape[1]
     squares = early[count:]
-    lanes = 2 * EARLY
+    lanes = EARLY_LANES
     shapes = [
         jax.ShapeDtypeStruct((depth, count + EXTRA, lanes), BF),
         jax.ShapeDtypeStruct((count // 2 + EXTRA, lanes), BF),
         jax.ShapeDtypeStruct((count // 2 + EXTRA, lanes), BF),
     ]
-    return once(functools.partial(combine_early_kernel, regions), shapes, squares, back, routes, weights)
+    return once(functools.partial(combine_early_kernel, regions), shapes, squares, back, routes, weights, limit=VMEM_MOST)
 
 
 def forward_kernel(for_right, for_left, right, left, right_out, left_out):
@@ -458,12 +465,12 @@
 
 def final_kernel(regions, full, depth, me, back, own, right, left, tok, gain, routes, weights, moe_out, grad_out, comb_out, stack):
     count = tok.shape[0]
-    late = tok.shape[1] - EARLY
+    late = late_widths(tok.shape[1])
     high, low = combining(routes[...], weights[...], regions)
     moe, grad = [dot(high, rows, TN) + dot(low, rows, TN) for rows in decode(back[...], late, fold_matrix(regions))]
     early = own[0, :count].astype(F32) + right[:count].astype(F32) + left[:count].astype(F32)
-    moe_out[:, :late] = moe.astype(BF)
-    moe_out[:, late:] = early[:, :EARLY].astype(BF)
+    moe_out[:, : late[0]] = moe.astype(BF)
+    moe_out[:, late[0] :] = early[:, : EARLY[0]].astype(BF)
     wide = tok[...].astype(F32)
     stack[0] = own[0, count:, :count].astype(F32)
     for away in range(1, depth):
@@ -479,7 +486,7 @@
     row = lax.broadcasted_iota(jnp.int32, (8, count), 0)
     columns = jnp.transpose(jnp.where(row == 0, comb[2], jnp.where(row == 1, inv, 0.0)))
     inner, inv = columns[:, 0:1], columns[:, 1:2]
-    scaled = gain[...].reshape(1, -1) * jnp.concatenate([grad, early[:, EARLY:]], axis=1)
+    scaled = gain[...].reshape(1, -1) * jnp.concatenate([grad, early[:, EARLY[0] :]], axis=1)
     grad_out[...] = (inv * scaled - wide * (inv * inv * inv * inner / full)).astype(BF)
 
 
@@ -530,12 +537,14 @@
     return blocks + [hop(low[:cut], 1), hop(high[cut:], -1)]
 
 
-def ring_scatter(shares, right, left):
+def ring_scatter(shares, right, left, summed):
     for at in range(shares.shape[0] // 2 - 1, -1, -1):
         right, left = hop(right, 1), hop(left, -1)
+        if at == shares.shape[0] // 2 - 2:
+            summed, _, _ = lax.optimization_barrier((summed, right, left))
         if at:
             right, left = forward(shares, at, right, left)
-    return right, left
+    return right, left, summed
 
 
 def on_device(tokens, norm_gain, w_gate, w_up, w_down, routes, combine, grad_out):
@@ -554,7 +563,7 @@
     partial, back_rows = expert_part(me, blocks, rows, w_gate, w_up, w_down, regions)
     summed = lax.psum_scatter(partial, "local", scatter_dimension=0)
     shares, right, left = combine_early(early, swap(back_rows, regions), routes, weights, regions, depth)
-    right, left = ring_scatter(shares, right, left)
+    right, left, summed = ring_scatter(shares, right, left, summed)
     moe, grad, comb = final(me, swap(summed, regions), shares, right, left, tokens, gain, routes, weights, regions, full)
     return moe, grad, comb.T
 

time: 249 us -> 249 us (level)
  starting transfers between devices: 62.8 us -> 59.3 us
  Pallas kernels: 33.7 us -> 37 us
    all_to_all x4, waiting for transfers between devices: 94.6 us -> 77.9 us  [swap(): lax.all_to_all(split, 'region', split_axis=0, concat_axis=0, tiled=True)]
    ppermute x16, waiting for transfers between devices: 37.7 us -> 45.5 us  [hop(): lax.ppermute(array, 'local', [(z, (z + step) % depth) for z in range(dept...]
    all_gather x1, waiting for transfers between devices: 0.01 us -> 4.82 us  [on_device(): blocks = lax.all_gather(arrived, 'local')]
    reduce_scatter x1, waiting for transfers between devices: 0.01 us -> 4.3 us  [on_device(): summed = lax.psum_scatter(partial, 'local', scatter_dimension=0)]
    all_to_all x4, starting transfers between devices: 33.6 us -> 30 us  [swap(): lax.all_to_all(split, 'region', split_axis=0, concat_axis=0, tiled=True)]
    pallas_call x3, Pallas kernels: 8.63 us -> 11.2 us  [once(): pl.pallas_call(kernel, grid=(1,), in_specs=[whole(operand.shape) for oper...]
  transfers between devices with their start and end apart: 22 -> 22, of which waited for: 10 -> 13; matrix products, arithmetic and copies ran while one was open for 0% -> 1% of each run, Pallas kernels for 3% -> 4%
where the time goes in v6:
time: 249 us; the launch traced here: 248 us
  waiting for transfers between devices  133 us (53%)
  starting transfers between devices  59.3 us (24%)
  Pallas kernels  37 us (15%)
  between operations  14.2 us (6%)
  local copies, waits for them, and re-layouts  5.25 us (2%)
    all_to_all x4, waiting for transfers between devices, swap(): lax.all_to_all(split, 'region', split_axis=0, concat_axis=0, tiled=True)  77.9 us
    ppermute x16, waiting for transfers between devices, hop(): lax.ppermute(array, 'local', [(z, (z + step) % depth) for z in range(dept...  45.5 us
    all_to_all x4, starting transfers between devices, swap(): lax.all_to_all(split, 'region', split_axis=0, concat_axis=0, tiled=True)  30 us
    ppermute x16, starting transfers between devices, hop(): lax.ppermute(array, 'local', [(z, (z + step) % depth) for z in range(dept...  29.2 us
    pallas_call x1, Pallas kernels, expert_part(): pl.pallas_call(functools.partial(expert_kernel, regions, depth), in_specs...  24 us
    pallas_call x3, Pallas kernels, once(): pl.pallas_call(kernel, grid=(1,), in_specs=[whole(operand.shape) for oper...  11.2 us
  transfers between devices with their start and end apart: 22, of which 13 were waited for; matrix products, arithmetic and copies ran while one was open for 1% of the time, Pallas kernels for 4%

profile of v6, /device:TPU:2, one launch (start us, length us, event | category | flops | bytes accessed | tf_op | source)
XLA Modules:
  0.0 248.3 jit_solution(671704175010256521)
XLA Ops:
  7.2 2.7 %shard_map.103 = (bf16[256,1536]{1,0:T(8,128)(2,1)}, bf16[144,640]{1,0:T(8,128)(2,1)}) custom-call(bf16[128,896]{1,0:T(8,128)(2,1)} %tok.3, f32[896]{0:T(1024)} %gain.3, bf16[128,896]{1,0:T(8,128)(2,1)} %grad.1, s32[2,128]{1,0:T(2,128)} %bitcast.15), custom_call_target="tpu_custom_call" | custom-call | tf_op jit(solution)/shard_map/pallas_call | solution.py:118
  9.8 7.6 %all-to-all-start = ((bf16[32,8,1536]{2,1,0:T(8,128)(2,1)}), bf16[32,8,1536]{2,1,0:T(8,128)(2,1)S(1)}, u32[]{:S(2)}, u32[]{:S(2)}) async-start(bf16[32,8,1536]{2,1,0:T(8,128)(2,1)} %bitcast.24), calls=%async_computation | async-start | bytes 1572864 | tf_op jit(solution)/shard_map/all_to_all | solution.py:520
  17.5 0.0 all-gather.3.cloned.1.call-start
  17.5 5.9 %collective-permute-start.1 = (bf16[144,640]{1,0:T(8,128)(2,1)}, bf16[144,640]{1,0:T(8,128)(2,1)S(1)}, u32[]{:S(2)}, u32[]{:S(2)}) collective-permute-start(bf16[144,640]{1,0:T(8,128)(2,1)} %get-tuple-element.28.refs_0_), channel_id=1, source_target_pairs={{0,7},{1,0},{2,1},{3,2},{4,3},{5,4},{6,5},{7,6},{8,15},{9,8},{10,9... | collective-permute-start | bytes 552968 | tf_op jit(solution)/shard_map/ppermute | solution.py:526
  23.4 4.5 %collective-permute-done.1.refs_2_ = bf16[144,640]{1,0:T(8,128)(2,1)S(1)} collective-permute-done((bf16[144,640]{1,0:T(8,128)(2,1)}, bf16[144,640]{1,0:T(8,128)(2,1)S(1)}, u32[]{:S(2)}, u32[]{:S(2)}) %collective-permute-start.1) | collective-permute-done | bytes 184352 | tf_op jit(solution)/shard_map/ppermute | solution.py:526
  28.0 3.3 %collective-permute-done.refs_1_ = bf16[144,640]{1,0:T(8,128)(2,1)S(1)} collective-permute-done((bf16[144,640]{1,0:T(8,128)(2,1)}, bf16[144,640]{1,0:T(8,128)(2,1)S(1)}, u32[]{:S(2)}, u32[]{:S(2)}) %collective-permute-start) | collective-permute-done | bytes 184352 | tf_op jit(solution)/shard_map/ppermute | solution.py:526
  31.3 3.2 %collective-permute-start.3 = (bf16[144,640]{1,0:T(8,128)(2,1)S(1)}, bf16[144,640]{1,0:T(8,128)(2,1)S(1)}, u32[]{:S(2)}, u32[]{:S(2)}) collective-permute-start(bf16[144,640]{1,0:T(8,128)(2,1)S(1)} %collective-permute-done.1.refs_2_), channel_id=1, source_target_pairs={{0,7},{1,0},{2,1},{3,2},{4,3},{5,4},{6,5},{7,6},{8,15},{9,8},{10,9... | collective-permute-start | bytes 552968 | tf_op jit(solution)/shard_map/ppermute | solution.py:526
  34.5 3.5 %collective-permute-done.2.refs_3_ = bf16[144,640]{1,0:T(8,128)(2,1)S(1)} collective-permute-done((bf16[144,640]{1,0:T(8,128)(2,1)S(1)}, bf16[144,640]{1,0:T(8,128)(2,1)S(1)}, u32[]{:S(2)}, u32[]{:S(2)}) %collective-permute-start.2) | collective-permute-done | bytes 184352 | tf_op jit(solution)/shard_map/ppermute | solution.py:526
  38.0 0.9 copy-done.8
  38.9 0.0 all-gather.3.cloned.1.call-update
  39.0 0.1 collective-permute-start.4
  39.0 3.3 %collective-permute-start.5 = (bf16[144,640]{1,0:T(8,128)(2,1)S(1)}, bf16[144,640]{1,0:T(8,128)(2,1)S(1)}, u32[]{:S(2)}, u32[]{:S(2)}) collective-permute-start(bf16[144,640]{1,0:T(8,128)(2,1)S(1)} %collective-permute-done.3.refs_4_), channel_id=1, source_target_pairs={{0,7},{1,0},{2,1},{3,2},{4,3},{5,4},{6,5},{7,6},{8,15},{9,8},{10,9... | collective-permute-start | bytes 552968 | tf_op jit(solution)/shard_map/ppermute | solution.py:526
  42.4 3.4 %collective-permute-done.4.refs_5_ = bf16[144,640]{1,0:T(8,128)(2,1)S(1)} collective-permute-done((bf16[144,640]{1,0:T(8,128)(2,1)S(1)}, bf16[144,640]{1,0:T(8,128)(2,1)S(1)}, u32[]{:S(2)}, u32[]{:S(2)}) %collective-permute-start.4) | collective-permute-done | bytes 184352 | tf_op jit(solution)/shard_map/ppermute | solution.py:526
  45.8 3.4 %collective-permute-start.7 = (bf16[80,640]{1,0:T(8,128)(2,1)S(1)}, bf16[80,640]{1,0:T(8,128)(2,1)S(1)}, u32[]{:S(2)}, u32[]{:S(2)}) collective-permute-start(bf16[80,640]{1,0:T(8,128)(2,1)S(1)} %slice.10), channel_id=1, source_target_pairs={{0,7},{1,0},{2,1},{3,2},{4,3},{5,4},{6,5},{7,6},{8,15},{9,8},{10,9... | collective-permute-start | bytes 307208 | tf_op jit(solution)/shard_map/ppermute | solution.py:526
  49.2 0.1 collective-permute-start.6
  49.3 7.2 %collective-permute-done.6.refs_7_ = bf16[64,640]{1,0:T(8,128)(2,1)S(1)} collective-permute-done((bf16[64,640]{1,0:T(8,128)(2,1)S(1)}, bf16[64,640]{1,0:T(8,128)(2,1)S(1)}, u32[]{:S(2)}, u32[]{:S(2)}) %collective-permute-start.6) | collective-permute-done | bytes 81952 | tf_op jit(solution)/shard_map/ppermute | solution.py:526
  56.5 0.9 copy-done.3
  57.4 0.7 copy-done.5
  58.1 3.3 %shard_map.104 = bf16[256,6528]{1,0:T(8,128)(2,1)} custom-call(s32[2,128]{1,0:T(2,128)S(1)} %bitcast.17, bf16[144,640]{1,0:T(8,128)(2,1)S(1)} %copy-done.3, bf16[144,640]{1,0:T(8,128)(2,1)S(1)} %collective-permute-done.refs_1_, bf16[144,640]{1,0:T(8,128)(2,1)S(1)} %collective-permute-done.1.refs_2_, bf16[144,640]{1,0:T(8,128)(2,1)S(1)} %collective-permute-done.2.refs_3_, ...), custom_call_target="tpu_custom_call" | custom-call | tf_op jit(solution)/shard_map/pallas_call | solution.py:118
  61.3 7.4 %all-to-all-start.1 = ((bf16[32,8,6528]{2,1,0:T(8,128)(2,1)}), bf16[32,8,6528]{2,1,0:T(8,128)(2,1)}, u32[]{:S(2)}, u32[]{:S(2)}) async-start(bf16[32,8,6528]{2,1,0:T(8,128)(2,1)} %bitcast.5), calls=%async_computation.1 | async-start | bytes 6684672 | tf_op jit(solution)/shard_map/all_to_all | solution.py:520
  68.8 0.0 reduce-scatter.2.cloned.1.call-start
  68.8 39.6 %all-to-all-done.1 = bf16[32,8,6528]{2,1,0:T(8,128)(2,1)} async-done(((bf16[32,8,6528]{2,1,0:T(8,128)(2,1)}), bf16[32,8,6528]{2,1,0:T(8,128)(2,1)}, u32[]{:S(2)}, u32[]{:S(2)}) %all-to-all-start.1) | async-done | bytes 3342368 | tf_op jit(solution)/shard_map/all_to_all | solution.py:520
  108.4 4.8 %all-gather.3.cloned.1.call-done = bf16[2048,1536]{1,0:T(8,128)(2,1)} async-done(((bf16[256,1536]{1,0:T(8,128)(2,1)}), bf16[2048,1536]{1,0:T(8,128)(2,1)}) %all-gather.3.cloned.1.call-update) | async-done | bytes 6291472 | tf_op jit(solution)/shard_map/all_gather | solution.py:560
  113.2 24.0 %shard_map.105 = (bf16[8,256,1536]{2,1,0:T(8,128)(2,1)}, bf16[256,6528]{1,0:T(8,128)(2,1)}) custom-call(s32[1]{0:T(128)} %bitcast.me, bf16[8,256,1536]{2,1,0:T(8,128)(2,1)} %bitcast.21, bf16[256,6528]{1,0:T(8,128)(2,1)} %bitcast.6.rows, bf16[1,7168,256]{2,1,0:T(8,128)(2,1)} %gate_hbm.1, bf16[1,7168,256]{2,1,0:T(8,128)(2,1)} %up_hbm.1, ...), custom_call_target="tpu_custom_call" | custom-call | tf_op jit(solution)/shard_map/pallas_call | solution.py:365
  137.2 0.0 reduce-scatter.2.cloned.1.call-update
  137.2 7.5 %all-to-all-start.2 = ((bf16[32,8,6528]{2,1,0:T(8,128)(2,1)}), bf16[32,8,6528]{2,1,0:T(8,128)(2,1)}, u32[]{:S(2)}, u32[]{:S(2)}) async-start(bf16[32,8,6528]{2,1,0:T(8,128)(2,1)} %bitcast.8), calls=%async_computation.3 | async-start | bytes 6684672 | tf_op jit(solution)/shard_map/all_to_all | solution.py:520
  144.7 1.3 slice.11.squares
  146.0 38.3 %all-to-all-done.2 = bf16[32,8,6528]{2,1,0:T(8,128)(2,1)} async-done(((bf16[32,8,6528]{2,1,0:T(8,128)(2,1)}), bf16[32,8,6528]{2,1,0:T(8,128)(2,1)}, u32[]{:S(2)}, u32[]{:S(2)}) %all-to-all-start.2) | async-done | bytes 3342368 | tf_op jit(solution)/shard_map/all_to_all | solution.py:520
  184.3 5.3 %shard_map.106 = (bf16[8,144,640]{2,1,0:T(8,128)(2,1)}, bf16[80,640]{1,0:T(8,128)(2,1)}, bf16[80,640]{1,0:T(8,128)(2,1)}) custom-call(bf16[16,640]{1,0:T(8,128)(2,1)} %slice.11.squares, bf16[256,6528]{1,0:T(8,128)(2,1)} %bitcast.9.back, s32[2,128]{1,0:T(2,128)} %bitcast.16, f32[2,128]{1,0:T(2,128)} %bitcast.19), custom_call_target="tpu_custom_call" | custom-call | tf_op jit(solution)/shard_map/pallas_call | solution.py:118
  189.6 3.3 %collective-permute-start.9 = (bf16[80,640]{1,0:T(8,128)(2,1)}, bf16[80,640]{1,0:T(8,128)(2,1)S(1)}, u32[]{:S(2)}, u32[]{:S(2)}) collective-permute-start(bf16[80,640]{1,0:T(8,128)(2,1)} %get-tuple-element.40), channel_id=1, source_target_pairs={{0,7},{1,0},{2,1},{3,2},{4,3},{5,4},{6,5},{7,6},{8,15},{9,8},{10,9... | collective-permute-start | bytes 307208 | tf_op jit(solution)/shard_map/ppermute | solution.py:526
  192.9 6.0 %collective-permute-done.8.right = bf16[80,640]{1,0:T(8,128)(2,1)S(1)} collective-permute-done((bf16[80,640]{1,0:T(8,128)(2,1)}, bf16[80,640]{1,0:T(8,128)(2,1)S(1)}, u32[]{:S(2)}, u32[]{:S(2)}) %collective-permute-start.8) | collective-permute-done | bytes 102432 | tf_op jit(solution)/shard_map/ppermute | solution.py:526
  198.9 1.4 copy-done
  200.2 0.1 shard_map.107
  200.3 0.1 collective-permute-start.10
  200.4 3.2 %collective-permute-start.11 = (bf16[144,640]{1,0:T(8,128)(2,1)S(1)}, bf16[144,640]{1,0:T(8,128)(2,1)S(1)}, u32[]{:S(2)}, u32[]{:S(2)}) collective-permute-start(bf16[144,640]{1,0:T(8,128)(2,1)S(1)} %get-tuple-element.42), channel_id=1, source_target_pairs={{0,7},{1,0},{2,1},{3,2},{4,3},{5,4},{6,5},{7,6},{8,15},{9,8},{10,9... | collective-permute-start | bytes 552968 | tf_op jit(solution)/shard_map/ppermute | solution.py:526
  203.6 9.1 %collective-permute-done.10.right = bf16[144,640]{1,0:T(8,128)(2,1)S(1)} collective-permute-done((bf16[144,640]{1,0:T(8,128)(2,1)S(1)}, bf16[144,640]{1,0:T(8,128)(2,1)S(1)}, u32[]{:S(2)}, u32[]{:S(2)}) %collective-permute-start.10) | collective-permute-done | bytes 184352 | tf_op jit(solution)/shard_map/ppermute | solution.py:526
  212.7 4.3 %reduce-scatter.2.cloned.1.call-done = bf16[1,256,1536]{2,1,0:T(8,128)(2,1)} async-done(((bf16[8,256,1536]{2,1,0:T(8,128)(2,1)}), bf16[1,256,1536]{2,1,0:T(8,128)(2,1)}) %reduce-scatter.2.cloned.1.call-update) | async-done | bytes 786448 | tf_op jit(solution)/shard_map/reduce_scatter | solution.py:564
  217.0 7.4 %all-to-all-start.3 = ((bf16[32,8,1536]{2,1,0:T(8,128)(2,1)}), bf16[32,8,1536]{2,1,0:T(8,128)(2,1)S(1)}, u32[]{:S(2)}, u32[]{:S(2)}) async-start(bf16[32,8,1536]{2,1,0:T(8,128)(2,1)} %bitcast.23), calls=%async_computation.4 | async-start | bytes 1572864 | tf_op jit(solution)/shard_map/all_to_all | solution.py:520
  224.5 0.0 copy-start.2
  224.5 0.1 shard_map.108
  224.6 0.1 collective-permute-start.12
  224.7 3.2 %collective-permute-start.13 = (bf16[144,640]{1,0:T(8,128)(2,1)S(1)}, bf16[144,640]{1,0:T(8,128)(2,1)S(1)}, u32[]{:S(2)}, u32[]{:S(2)}) collective-permute-start(bf16[144,640]{1,0:T(8,128)(2,1)S(1)} %get-tuple-element.45), channel_id=1, source_target_pairs={{0,7},{1,0},{2,1},{3,2},{4,3},{5,4},{6,5},{7,6},{8,15},{9,8},{10,9... | collective-permute-start | bytes 552968 | tf_op jit(solution)/shard_map/ppermute | solution.py:526
  227.9 4.7 %collective-permute-done.12.right = bf16[144,640]{1,0:T(8,128)(2,1)S(1)} collective-permute-done((bf16[144,640]{1,0:T(8,128)(2,1)S(1)}, bf16[144,640]{1,0:T(8,128)(2,1)S(1)}, u32[]{:S(2)}, u32[]{:S(2)}) %collective-permute-start.12) | collective-permute-done | bytes 184352 | tf_op jit(solution)/shard_map/ppermute | solution.py:526
  232.6 0.1 shard_map.109
  232.7 1.0 collective-permute-start.14
  233.6 2.4 collective-permute-start.15
  236.0 3.8 %collective-permute-done.14.right = bf16[144,640]{1,0:T(8,128)(2,1)S(1)} collective-permute-done((bf16[144,640]{1,0:T(8,128)(2,1)S(1)}, bf16[144,640]{1,0:T(8,128)(2,1)S(1)}, u32[]{:S(2)}, u32[]{:S(2)}) %collective-permute-start.14) | collective-permute-done | bytes 184352 | tf_op jit(solution)/shard_map/ppermute | solution.py:526
  239.9 1.5 shard_map.110
  (27 shorter events, 0.1 us)
Async XLA Ops:
  9.8 28.2 %all-to-all-start = ((bf16[32,8,1536]{2,1,0:T(8,128)(2,1)}), bf16[32,8,1536]{2,1,0:T(8,128)(2,1)S(1)}, u32[]{:S(2)}, u32[]{:S(2)}) async-start(bf16[32,8,1536]{2,1,0:T(8,128)(2,1)} %bitcast.24), calls=%async_computation | async-start | bytes 1572864 | tf_op jit(solution)/shard_map/all_to_all | solution.py:520
  17.5 95.8 %all-gather.3.cloned.1.call-start = ((), (), s32[]{:S(2)}) async-start(), calls=%async_computation.6 | async-start | bytes 7077888 | tf_op jit(solution)/shard_map/all_gather | solution.py:560
  17.5 10.5 %collective-permute-start.1 = (bf16[144,640]{1,0:T(8,128)(2,1)}, bf16[144,640]{1,0:T(8,128)(2,1)S(1)}, u32[]{:S(2)}, u32[]{:S(2)}) collective-permute-start(bf16[144,640]{1,0:T(8,128)(2,1)} %get-tuple-element.28.refs_0_), channel_id=1, source_target_pairs={{0,7},{1,0},{2,1},{3,2},{4,3},{5,4},{6,5},{7,6},{8,15},{9,8},{10,9... | collective-permute-start | bytes 552968 | tf_op jit(solution)/shard_map/ppermute | solution.py:526
  23.4 7.8 %collective-permute-start = (bf16[144,640]{1,0:T(8,128)(2,1)}, bf16[144,640]{1,0:T(8,128)(2,1)S(1)}, u32[]{:S(2)}, u32[]{:S(2)}) collective-permute-start(bf16[144,640]{1,0:T(8,128)(2,1)} %get-tuple-element.28.refs_0_), channel_id=1, source_target_pairs={{0,1},{1,2},{2,3},{3,4},{4,5},{5,6},{6,7},{7,0},{8,9},{9,10},{10,1... | collective-permute-start | bytes 552968 | tf_op jit(solution)/shard_map/ppermute | solution.py:526
  31.3 6.8 %collective-permute-start.2 = (bf16[144,640]{1,0:T(8,128)(2,1)S(1)}, bf16[144,640]{1,0:T(8,128)(2,1)S(1)}, u32[]{:S(2)}, u32[]{:S(2)}) collective-permute-start(bf16[144,640]{1,0:T(8,128)(2,1)S(1)} %collective-permute-done.refs_1_), channel_id=1, source_target_pairs={{0,1},{1,2},{2,3},{3,4},{4,5},{5,6},{6,7},{7,0},{8,9},{9,10},{10,1... | collective-permute-start | bytes 552968 | tf_op jit(solution)/shard_map/ppermute | solution.py:526
  31.3 6.8 %collective-permute-start.3 = (bf16[144,640]{1,0:T(8,128)(2,1)S(1)}, bf16[144,640]{1,0:T(8,128)(2,1)S(1)}, u32[]{:S(2)}, u32[]{:S(2)}) collective-permute-start(bf16[144,640]{1,0:T(8,128)(2,1)S(1)} %collective-permute-done.1.refs_2_), channel_id=1, source_target_pairs={{0,7},{1,0},{2,1},{3,2},{4,3},{5,4},{6,5},{7,6},{8,15},{9,8},{10,9... | collective-permute-start | bytes 552968 | tf_op jit(solution)/shard_map/ppermute | solution.py:526
  38.0 0.9 copy-start.8
  39.0 6.8 %collective-permute-start.4 = (bf16[144,640]{1,0:T(8,128)(2,1)S(1)}, bf16[144,640]{1,0:T(8,128)(2,1)S(1)}, u32[]{:S(2)}, u32[]{:S(2)}) collective-permute-start(bf16[144,640]{1,0:T(8,128)(2,1)S(1)} %collective-permute-done.2.refs_3_), channel_id=1, source_target_pairs={{0,1},{1,2},{2,3},{3,4},{4,5},{5,6},{6,7},{7,0},{8,9},{9,10},{10,1... | collective-permute-start | bytes 552968 | tf_op jit(solution)/shard_map/ppermute | solution.py:526
  39.0 6.7 %collective-permute-start.5 = (bf16[144,640]{1,0:T(8,128)(2,1)S(1)}, bf16[144,640]{1,0:T(8,128)(2,1)S(1)}, u32[]{:S(2)}, u32[]{:S(2)}) collective-permute-start(bf16[144,640]{1,0:T(8,128)(2,1)S(1)} %collective-permute-done.3.refs_4_), channel_id=1, source_target_pairs={{0,7},{1,0},{2,1},{3,2},{4,3},{5,4},{6,5},{7,6},{8,15},{9,8},{10,9... | collective-permute-start | bytes 552968 | tf_op jit(solution)/shard_map/ppermute | solution.py:526
  45.8 10.7 %collective-permute-start.7 = (bf16[80,640]{1,0:T(8,128)(2,1)S(1)}, bf16[80,640]{1,0:T(8,128)(2,1)S(1)}, u32[]{:S(2)}, u32[]{:S(2)}) collective-permute-start(bf16[80,640]{1,0:T(8,128)(2,1)S(1)} %slice.10), channel_id=1, source_target_pairs={{0,7},{1,0},{2,1},{3,2},{4,3},{5,4},{6,5},{7,6},{8,15},{9,8},{10,9... | collective-permute-start | bytes 307208 | tf_op jit(solution)/shard_map/ppermute | solution.py:526
  49.2 7.3 %collective-permute-start.6 = (bf16[64,640]{1,0:T(8,128)(2,1)S(1)}, bf16[64,640]{1,0:T(8,128)(2,1)S(1)}, u32[]{:S(2)}, u32[]{:S(2)}) collective-permute-start(bf16[64,640]{1,0:T(8,128)(2,1)S(1)} %slice.9), channel_id=1, source_target_pairs={{0,1},{1,2},{2,3},{3,4},{4,5},{5,6},{6,7},{7,0},{8,9},{9,10},{10,1... | collective-permute-start | bytes 245768 | tf_op jit(solution)/shard_map/ppermute | solution.py:526
  56.5 0.9 copy-start.3
  57.4 0.7 copy-start.5
  61.3 47.1 %all-to-all-start.1 = ((bf16[32,8,6528]{2,1,0:T(8,128)(2,1)}), bf16[32,8,6528]{2,1,0:T(8,128)(2,1)}, u32[]{:S(2)}, u32[]{:S(2)}) async-start(bf16[32,8,6528]{2,1,0:T(8,128)(2,1)} %bitcast.5), calls=%async_computation.1 | async-start | bytes 6684672 | tf_op jit(solution)/shard_map/all_to_all | solution.py:520
  68.8 148.3 %reduce-scatter.2.cloned.1.call-start = ((), (), s32[]{:S(2)}) async-start(), calls=%async_computation.5 | async-start | bytes 7077888 | tf_op jit(solution)/shard_map/reduce_scatter | solution.py:564
  137.2 47.1 %all-to-all-start.2 = ((bf16[32,8,6528]{2,1,0:T(8,128)(2,1)}), bf16[32,8,6528]{2,1,0:T(8,128)(2,1)}, u32[]{:S(2)}, u32[]{:S(2)}) async-start(bf16[32,8,6528]{2,1,0:T(8,128)(2,1)} %bitcast.8), calls=%async_computation.3 | async-start | bytes 6684672 | tf_op jit(solution)/shard_map/all_to_all | solution.py:520
  189.6 9.2 %collective-permute-start.8 = (bf16[80,640]{1,0:T(8,128)(2,1)}, bf16[80,640]{1,0:T(8,128)(2,1)S(1)}, u32[]{:S(2)}, u32[]{:S(2)}) collective-permute-start(bf16[80,640]{1,0:T(8,128)(2,1)} %get-tuple-element.39), channel_id=1, source_target_pairs={{0,1},{1,2},{2,3},{3,4},{4,5},{5,6},{6,7},{7,0},{8,9},{9,10},{10,1... | collective-permute-start | bytes 307208 | tf_op jit(solution)/shard_map/ppermute | solution.py:526
  189.6 9.2 %collective-permute-start.9 = (bf16[80,640]{1,0:T(8,128)(2,1)}, bf16[80,640]{1,0:T(8,128)(2,1)S(1)}, u32[]{:S(2)}, u32[]{:S(2)}) collective-permute-start(bf16[80,640]{1,0:T(8,128)(2,1)} %get-tuple-element.40), channel_id=1, source_target_pairs={{0,7},{1,0},{2,1},{3,2},{4,3},{5,4},{6,5},{7,6},{8,15},{9,8},{10,9... | collective-permute-start | bytes 307208 | tf_op jit(solution)/shard_map/ppermute | solution.py:526
  198.9 1.4 copy-start
  200.2 24.2 %copy-start.1 = (bf16[8,144,640]{2,1,0:T(8,128)(2,1)S(1)}, bf16[8,144,640]{2,1,0:T(8,128)(2,1)}, u32[]{:S(2)}) copy-start(bf16[8,144,640]{2,1,0:T(8,128)(2,1)} %get-tuple-element.38.for_right.for_left.own) | copy-start | bytes 4423684
  200.3 12.4 %collective-permute-start.10 = (bf16[144,640]{1,0:T(8,128)(2,1)S(1)}, bf16[144,640]{1,0:T(8,128)(2,1)S(1)}, u32[]{:S(2)}, u32[]{:S(2)}) collective-permute-start(bf16[144,640]{1,0:T(8,128)(2,1)S(1)} %get-tuple-element.41), channel_id=1, source_target_pairs={{0,1},{1,2},{2,3},{3,4},{4,5},{5,6},{6,7},{7,0},{8,9},{9,10},{10,1... | collective-permute-start | bytes 552968 | tf_op jit(solution)/shard_map/ppermute | solution.py:526
  200.4 12.3 %collective-permute-start.11 = (bf16[144,640]{1,0:T(8,128)(2,1)S(1)}, bf16[144,640]{1,0:T(8,128)(2,1)S(1)}, u32[]{:S(2)}, u32[]{:S(2)}) collective-permute-start(bf16[144,640]{1,0:T(8,128)(2,1)S(1)} %get-tuple-element.42), channel_id=1, source_target_pairs={{0,7},{1,0},{2,1},{3,2},{4,3},{5,4},{6,5},{7,6},{8,15},{9,8},{10,9... | collective-permute-start | bytes 552968 | tf_op jit(solution)/shard_map/ppermute | solution.py:526
  217.0 22.8 %all-to-all-start.3 = ((bf16[32,8,1536]{2,1,0:T(8,128)(2,1)}), bf16[32,8,1536]{2,1,0:T(8,128)(2,1)S(1)}, u32[]{:S(2)}, u32[]{:S(2)}) async-start(bf16[32,8,1536]{2,1,0:T(8,128)(2,1)} %bitcast.23), calls=%async_computation.4 | async-start | bytes 1572864 | tf_op jit(solution)/shard_map/all_to_all | solution.py:520
  224.5 15.4 %copy-start.2 = (bf16[128,896]{1,0:T(8,128)(2,1)S(1)}, bf16[128,896]{1,0:T(8,128)(2,1)}, u32[]{:S(2)}) copy-start(bf16[128,896]{1,0:T(8,128)(2,1)} %tok.3) | copy-start | bytes 688132
  224.5 15.4 %copy-start.4 = (f32[896]{0:T(1024)S(1)}, f32[896]{0:T(1024)}, u32[]{:S(2)}) copy-start(f32[896]{0:T(1024)} %gain.3) | copy-start | bytes 10756
  224.5 15.4 %copy-start.6 = (s32[128,2]{0,1:T(2,128)S(1)}, s32[128,2]{0,1:T(2,128)}, u32[]{:S(2)}) copy-start(s32[128,2]{0,1:T(2,128)} %param.13) | copy-start | bytes 3076
  224.5 15.4 %copy-start.7 = (f32[128,2]{0,1:T(2,128)S(1)}, f32[128,2]{0,1:T(2,128)}, u32[]{:S(2)}) copy-start(f32[128,2]{0,1:T(2,128)} %param.14) | copy-start | bytes 3076
  224.6 8.0 %collective-permute-start.12 = (bf16[144,640]{1,0:T(8,128)(2,1)S(1)}, bf16[144,640]{1,0:T(8,128)(2,1)S(1)}, u32[]{:S(2)}, u32[]{:S(2)}) collective-permute-start(bf16[144,640]{1,0:T(8,128)(2,1)S(1)} %get-tuple-element.44), channel_id=1, source_target_pairs={{0,1},{1,2},{2,3},{3,4},{4,5},{5,6},{6,7},{7,0},{8,9},{9,10},{10,1... | collective-permute-start | bytes 552968 | tf_op jit(solution)/shard_map/ppermute | solution.py:526
  224.7 7.9 %collective-permute-start.13 = (bf16[144,640]{1,0:T(8,128)(2,1)S(1)}, bf16[144,640]{1,0:T(8,128)(2,1)S(1)}, u32[]{:S(2)}, u32[]{:S(2)}) collective-permute-start(bf16[144,640]{1,0:T(8,128)(2,1)S(1)} %get-tuple-element.45), channel_id=1, source_target_pairs={{0,7},{1,0},{2,1},{3,2},{4,3},{5,4},{6,5},{7,6},{8,15},{9,8},{10,9... | collective-permute-start | bytes 552968 | tf_op jit(solution)/shard_map/ppermute | solution.py:526
  232.7 7.2 %collective-permute-start.14 = (bf16[144,640]{1,0:T(8,128)(2,1)S(1)}, bf16[144,640]{1,0:T(8,128)(2,1)S(1)}, u32[]{:S(2)}, u32[]{:S(2)}) collective-permute-start(bf16[144,640]{1,0:T(8,128)(2,1)S(1)} %get-tuple-element.46), channel_id=1, source_target_pairs={{0,1},{1,2},{2,3},{3,4},{4,5},{5,6},{6,7},{7,0},{8,9},{9,10},{10,1... | collective-permute-start | bytes 552968 | tf_op jit(solution)/shard_map/ppermute | solution.py:526
  233.6 6.2 %collective-permute-start.15 = (bf16[144,640]{1,0:T(8,128)(2,1)S(1)}, bf16[144,640]{1,0:T(8,128)(2,1)S(1)}, u32[]{:S(2)}, u32[]{:S(2)}) collective-permute-start(bf16[144,640]{1,0:T(8,128)(2,1)S(1)} %get-tuple-element.47), channel_id=1, source_target_pairs={{0,7},{1,0},{2,1},{3,2},{4,3},{5,4},{6,5},{7,6},{8,15},{9,8},{10,9... | collective-permute-start | bytes 552968 | tf_op jit(solution)/shard_map/ppermute | solution.py:526
Sparse Core Ops, SparseCore 0:
  39.1 74.0 all-gather.2
  137.3 79.6 reduce-scatter.1

commit v7 on v6

--- a/solution.py
+++ b/solution.py
@@ -15,11 +15,11 @@
 VMEM_SOME = 40 * 1024 * 1024
 EXTRA = 16
 EARLY = (384, 256)
-EARLY_LANES = sum(EARLY)
-
-
-def late_widths(width):
-    return [width - early for early in EARLY]
+BACK = (384, 384)
+
+
+def late_widths(width, early):
+    return [width - lanes for lanes in early]
 
 
 def fold_lanes(widths):
@@ -159,7 +159,7 @@
 def pack_kernel(regions, tok, gain, grad, routes, out, early):
     at = placed(routes[...], regions)
     pick = (at[0] | at[1]).astype(F32).astype(BF)
-    late = late_widths(tok.shape[1])
+    late = late_widths(tok.shape[1], EARLY)
     count = tok.shape[0]
     wide = tok[...].astype(F32)
     scaled = (wide * gain[...].reshape(1, -1)).astype(BF)
@@ -174,8 +174,8 @@
 def pack(tok, gain, grad, routes, regions):
     count, width = tok.shape
     shapes = [
-        jax.ShapeDtypeStruct((8 * regions, packed_lanes(late_widths(width))), BF),
-        jax.ShapeDtypeStruct((count + EXTRA, EARLY_LANES), BF),
+        jax.ShapeDtypeStruct((8 * regions, packed_lanes(late_widths(width, EARLY))), BF),
+        jax.ShapeDtypeStruct((count + EXTRA, sum(EARLY)), BF),
     ]
     return once(functools.partial(pack_kernel, regions), shapes, tok, gain, grad, routes, limit=VMEM_MOST)
 
@@ -216,12 +216,12 @@
     out[:, -128:] = in_lanes(columns, cut)
 
 
-def early_shape(regions, depth):
-    return (8 * regions, EARLY_LANES * depth * 5 // 4 + 128)
+def early_shape(regions, depth, early):
+    return (8 * regions, sum(early) * depth * 5 // 4 + 128)
 
 
 def pack_early(blocks, routes, regions, depth, full):
-    shape = jax.ShapeDtypeStruct(early_shape(regions, depth), BF)
+    shape = jax.ShapeDtypeStruct(early_shape(regions, depth, EARLY), BF)
     return once(functools.partial(pack_early_kernel, regions, depth, full), shape, routes, *blocks)
 
 
@@ -258,7 +258,8 @@
     width = gate_w.shape[1] // depth
     few = 2 * regions
     cut, lanes = blocks.shape[1:]
-    late = late_widths(width)
+    late = late_widths(width, EARLY)
+    late_back = late_widths(width, BACK)
     first_block = me[0]
     copy = pltpu.make_async_copy(rows.at[:, rows.shape[1] - 128 :], scales, sem)
     copy.start()
@@ -301,8 +302,8 @@
         grid=(depth,),
         in_specs=[
             pl.BlockSpec((1, cut, lanes), lambda z: ((z + first_block) % depth, 0, 0)),
-            pl.BlockSpec((cut, EARLY_LANES), lambda z: (0, z)),
-            pl.BlockSpec((cut, EARLY_LANES), lambda z: (0, depth + z // 4)),
+            pl.BlockSpec((cut, sum(EARLY)), lambda z: (0, z)),
+            pl.BlockSpec((cut, sum(EARLY)), lambda z: (0, depth + z // 4)),
         ],
     )(blocks, rows, rows)
 
@@ -331,9 +332,9 @@
         at = lanes_of(step)
         moe = dot(hid[...], down_w[0, :, at]).astype(BF)
         grad = (dot(gate_g[...], gate_w[0, at, :], NT) + dot(up_g[...], up_w[0, at, :], NT)).astype(BF)
-        both = jnp.concatenate([moe[:, : late[0]], grad[:, : late[1]]], axis=1)
-        late_block[0] = encode(both[:cut], both[cut:], fold[...], late)
-        both = jnp.concatenate([moe[:, late[0] :], grad[:, late[1] :]], axis=1)
+        both = jnp.concatenate([moe[:, : late_back[0]], grad[:, : late_back[1]]], axis=1)
+        late_block[0] = encode(both[:cut], both[cut:], fold[...], late_back)
+        both = jnp.concatenate([moe[:, late_back[0] :], grad[:, late_back[1] :]], axis=1)
         main[...] = both[:cut]
         pick = fold[pl.ds(pl.multiple_of((step % 4) * few, few), few), :]
         low = dot(pick, both[cut:], TN).astype(BF)
@@ -351,8 +352,8 @@
         grid=(depth,),
         out_specs=[
             pl.BlockSpec((1, cut, late_lanes), lambda z: ((z + first_block) % depth, 0, 0)),
-            pl.BlockSpec((cut, EARLY_LANES), lambda z: (0, z)),
-            pl.BlockSpec((cut, EARLY_LANES), lambda z: (0, depth + z // 4)),
+            pl.BlockSpec((cut, sum(BACK)), lambda z: (0, z)),
+            pl.BlockSpec((cut, sum(BACK)), lambda z: (0, depth + z // 4)),
         ],
     )(late_out, early_out, early_out)
     pltpu.sync_copy(scal, early_out.at[:, early_out.shape[1] - 128 :])
@@ -361,12 +362,13 @@
 def expert_part(me, blocks, rows, gate_w, up_w, down_w, regions):
     depth, cut, lanes = blocks.shape
     units = gate_w.shape[2]
+    back_lanes = packed_lanes(late_widths(gate_w.shape[1] // depth, BACK))
     total = 10 * regions
     return pl.pallas_call(
         functools.partial(expert_kernel, regions, depth),
         in_specs=[pl.BlockSpec(memory_space=pltpu.SMEM)] + [anywhere()] * 5,
         out_specs=[anywhere()] * 2,
-        out_shape=[jax.ShapeDtypeStruct((depth, cut, lanes), BF), jax.ShapeDtypeStruct(rows.shape, BF)],
+        out_shape=[jax.ShapeDtypeStruct((depth, cut, back_lanes), BF), jax.ShapeDtypeStruct(early_shape(regions, depth, BACK), BF)],
         scratch_shapes=[pltpu.VMEM(w.shape, BF) for w in (gate_w, up_w, down_w)]
         + [pltpu.VMEM((total, units), F32)] * 3
         + [pltpu.VMEM((total, units), BF)] * 3
@@ -424,13 +426,13 @@
 def combine_early(early, back, routes, weights, regions, depth):
     count = routes.shape[1]
     squares = early[count:]
-    lanes = EARLY_LANES
+    lanes = sum(BACK)
     shapes = [
         jax.ShapeDtypeStruct((depth, count + EXTRA, lanes), BF),
         jax.ShapeDtypeStruct((count // 2 + EXTRA, lanes), BF),
         jax.ShapeDtypeStruct((count // 2 + EXTRA, lanes), BF),
     ]
-    return once(functools.partial(combine_early_kernel, regions), shapes, squares, back, routes, weights, limit=VMEM_MOST)
+    return once(functools.partial(combine_early_kernel, regions), shapes, squares, back, routes, weights)
 
 
 def forward_kernel(for_right, for_left, right, left, right_out, left_out):
@@ -465,12 +467,12 @@
 
 def final_kernel(regions, full, depth, me, back, own, right, left, tok, gain, routes, weights, moe_out, grad_out, comb_out, stack):
     count = tok.shape[0]
-    late = late_widths(tok.shape[1])
+    late = late_widths(tok.shape[1], BACK)
     high, low = combining(routes[...], weights[...], regions)
     moe, grad = [dot(high, rows, TN) + dot(low, rows, TN) for rows in decode(back[...], late, fold_matrix(regions))]
     early = own[0, :count].astype(F32) + right[:count].astype(F32) + left[:count].astype(F32)
     moe_out[:, : late[0]] = moe.astype(BF)
-    moe_out[:, late[0] :] = early[:, : EARLY[0]].astype(BF)
+    moe_out[:, late[0] :] = early[:, : BACK[0]].astype(BF)
     wide = tok[...].astype(F32)
     stack[0] = own[0, count:, :count].astype(F32)
     for away in range(1, depth):
@@ -486,7 +488,7 @@
     row = lax.broadcasted_iota(jnp.int32, (8, count), 0)
     columns = jnp.transpose(jnp.where(row == 0, comb[2], jnp.where(row == 1, inv, 0.0)))
     inner, inv = columns[:, 0:1], columns[:, 1:2]
-    scaled = gain[...].reshape(1, -1) * jnp.concatenate([grad, early[:, EARLY[0] :]], axis=1)
+    scaled = gain[...].reshape(1, -1) * jnp.concatenate([grad, early[:, BACK[0] :]], axis=1)
     grad_out[...] = (inv * scaled - wide * (inv * inv * inv * inner / full)).astype(BF)
 
 
@@ -540,7 +542,7 @@
 def ring_scatter(shares, right, left, summed):
     for at in range(shares.shape[0] // 2 - 1, -1, -1):
         right, left = hop(right, 1), hop(left, -1)
-        if at == shares.shape[0] // 2 - 2:
+        if at == shares.shape[0] // 2 - 1:
             summed, _, _ = lax.optimization_barrier((summed, right, left))
         if at:
             right, left = forward(shares, at, right, left)

time: 249 us -> 241 us (0.968)
  waiting for transfers between devices: 133 us -> 126 us
    ppermute x16, waiting for transfers between devices: 45.5 us -> 35.1 us  [hop(): lax.ppermute(array, 'local', [(z, (z + step) % depth) for z in range(dept...]
    all_to_all x4, waiting for transfers between devices: 77.9 us -> 86.3 us  [swap(): lax.all_to_all(split, 'region', split_axis=0, concat_axis=0, tiled=True)]
    reduce_scatter x1, waiting for transfers between devices: 4.3 us -> 0.01 us  [on_device(): summed = lax.psum_scatter(partial, 'local', scatter_dimension=0)]
  transfers between devices with their start and end apart: 22 -> 22, of which waited for: 13 -> 11; matrix products, arithmetic and copies ran while one was open for 1% -> 0% of each run, Pallas kernels for 4% -> 3%
where the time goes in v7:
time: 241 us; the launch traced here: 240 us
  waiting for transfers between devices  126 us (52%)
  starting transfers between devices  61.2 us (25%)
  Pallas kernels  35.4 us (15%)
  between operations  14.2 us (6%)
  local copies, waits for them, and re-layouts  3.29 us (1%)
    all_to_all x4, waiting for transfers between devices, swap(): lax.all_to_all(split, 'region', split_axis=0, concat_axis=0, tiled=True)  86.3 us
    ppermute x16, waiting for transfers between devices, hop(): lax.ppermute(array, 'local', [(z, (z + step) % depth) for z in range(dept...  35.1 us
    all_to_all x4, starting transfers between devices, swap(): lax.all_to_all(split, 'region', split_axis=0, concat_axis=0, tiled=True)  31.9 us
    ppermute x16, starting transfers between devices, hop(): lax.ppermute(array, 'local', [(z, (z + step) % depth) for z in range(dept...  29.3 us
    pallas_call x1, Pallas kernels, expert_part(): pl.pallas_call(functools.partial(expert_kernel, regions, depth), in_specs...  23.4 us
    pallas_call x3, Pallas kernels, once(): pl.pallas_call(kernel, grid=(1,), in_specs=[whole(operand.shape) for oper...  10.3 us
  transfers between devices with their start and end apart: 22, of which 11 were waited for; matrix products, arithmetic and copies ran while one was open for 0% of the time, Pallas kernels for 3%

profile of v7, /device:TPU:2, one launch (start us, length us, event | category | flops | bytes accessed | tf_op | source)
XLA Modules:
  0.0 240.4 jit_solution(18149418867907752448)
XLA Ops:
  7.2 2.7 %shard_map.103 = (bf16[256,1536]{1,0:T(8,128)(2,1)}, bf16[144,640]{1,0:T(8,128)(2,1)}) custom-call(bf16[128,896]{1,0:T(8,128)(2,1)} %tok.3, f32[896]{0:T(1024)} %gain.3, bf16[128,896]{1,0:T(8,128)(2,1)} %grad.1, s32[2,128]{1,0:T(2,128)} %bitcast.15), custom_call_target="tpu_custom_call" | custom-call | tf_op jit(solution)/shard_map/pallas_call | solution.py:118
  9.8 7.6 %all-to-all-start = ((bf16[32,8,1536]{2,1,0:T(8,128)(2,1)}), bf16[32,8,1536]{2,1,0:T(8,128)(2,1)S(1)}, u32[]{:S(2)}, u32[]{:S(2)}) async-start(bf16[32,8,1536]{2,1,0:T(8,128)(2,1)} %bitcast.24), calls=%async_computation | async-start | bytes 1572864 | tf_op jit(solution)/shard_map/all_to_all | solution.py:522
  17.4 0.0 all-gather.3.cloned.1.call-start
  17.5 5.9 %collective-permute-start.1 = (bf16[144,640]{1,0:T(8,128)(2,1)}, bf16[144,640]{1,0:T(8,128)(2,1)S(1)}, u32[]{:S(2)}, u32[]{:S(2)}) collective-permute-start(bf16[144,640]{1,0:T(8,128)(2,1)} %get-tuple-element.28.refs_0_), channel_id=1, source_target_pairs={{0,7},{1,0},{2,1},{3,2},{4,3},{5,4},{6,5},{7,6},{8,15},{9,8},{10,9... | collective-permute-start | bytes 552968 | tf_op jit(solution)/shard_map/ppermute | solution.py:528
  23.4 4.5 %collective-permute-done.1.refs_2_ = bf16[144,640]{1,0:T(8,128)(2,1)S(1)} collective-permute-done((bf16[144,640]{1,0:T(8,128)(2,1)}, bf16[144,640]{1,0:T(8,128)(2,1)S(1)}, u32[]{:S(2)}, u32[]{:S(2)}) %collective-permute-start.1) | collective-permute-done | bytes 184352 | tf_op jit(solution)/shard_map/ppermute | solution.py:528
  28.0 3.3 %collective-permute-done.refs_1_ = bf16[144,640]{1,0:T(8,128)(2,1)S(1)} collective-permute-done((bf16[144,640]{1,0:T(8,128)(2,1)}, bf16[144,640]{1,0:T(8,128)(2,1)S(1)}, u32[]{:S(2)}, u32[]{:S(2)}) %collective-permute-start) | collective-permute-done | bytes 184352 | tf_op jit(solution)/shard_map/ppermute | solution.py:528
  31.3 3.2 %collective-permute-start.3 = (bf16[144,640]{1,0:T(8,128)(2,1)S(1)}, bf16[144,640]{1,0:T(8,128)(2,1)S(1)}, u32[]{:S(2)}, u32[]{:S(2)}) collective-permute-start(bf16[144,640]{1,0:T(8,128)(2,1)S(1)} %collective-permute-done.1.refs_2_), channel_id=1, source_target_pairs={{0,7},{1,0},{2,1},{3,2},{4,3},{5,4},{6,5},{7,6},{8,15},{9,8},{10,9... | collective-permute-start | bytes 552968 | tf_op jit(solution)/shard_map/ppermute | solution.py:528
  34.5 3.5 %collective-permute-done.2.refs_3_ = bf16[144,640]{1,0:T(8,128)(2,1)S(1)} collective-permute-done((bf16[144,640]{1,0:T(8,128)(2,1)S(1)}, bf16[144,640]{1,0:T(8,128)(2,1)S(1)}, u32[]{:S(2)}, u32[]{:S(2)}) %collective-permute-start.2) | collective-permute-done | bytes 184352 | tf_op jit(solution)/shard_map/ppermute | solution.py:528
  38.0 0.9 copy-done.6
  38.9 0.0 all-gather.3.cloned.1.call-update
  39.0 0.1 collective-permute-start.4
  39.1 3.3 %collective-permute-start.5 = (bf16[144,640]{1,0:T(8,128)(2,1)S(1)}, bf16[144,640]{1,0:T(8,128)(2,1)S(1)}, u32[]{:S(2)}, u32[]{:S(2)}) collective-permute-start(bf16[144,640]{1,0:T(8,128)(2,1)S(1)} %collective-permute-done.3.refs_4_), channel_id=1, source_target_pairs={{0,7},{1,0},{2,1},{3,2},{4,3},{5,4},{6,5},{7,6},{8,15},{9,8},{10,9... | collective-permute-start | bytes 552968 | tf_op jit(solution)/shard_map/ppermute | solution.py:528
  42.4 3.4 %collective-permute-done.4.refs_5_ = bf16[144,640]{1,0:T(8,128)(2,1)S(1)} collective-permute-done((bf16[144,640]{1,0:T(8,128)(2,1)S(1)}, bf16[144,640]{1,0:T(8,128)(2,1)S(1)}, u32[]{:S(2)}, u32[]{:S(2)}) %collective-permute-start.4) | collective-permute-done | bytes 184352 | tf_op jit(solution)/shard_map/ppermute | solution.py:528
  45.8 3.4 %collective-permute-start.7 = (bf16[80,640]{1,0:T(8,128)(2,1)S(1)}, bf16[80,640]{1,0:T(8,128)(2,1)S(1)}, u32[]{:S(2)}, u32[]{:S(2)}) collective-permute-start(bf16[80,640]{1,0:T(8,128)(2,1)S(1)} %slice.10), channel_id=1, source_target_pairs={{0,7},{1,0},{2,1},{3,2},{4,3},{5,4},{6,5},{7,6},{8,15},{9,8},{10,9... | collective-permute-start | bytes 307208 | tf_op jit(solution)/shard_map/ppermute | solution.py:528
  49.2 0.1 collective-permute-start.6
  49.3 7.2 %collective-permute-done.6.refs_7_ = bf16[64,640]{1,0:T(8,128)(2,1)S(1)} collective-permute-done((bf16[64,640]{1,0:T(8,128)(2,1)S(1)}, bf16[64,640]{1,0:T(8,128)(2,1)S(1)}, u32[]{:S(2)}, u32[]{:S(2)}) %collective-permute-start.6) | collective-permute-done | bytes 81952 | tf_op jit(solution)/shard_map/ppermute | solution.py:528
  56.5 0.9 copy-done.1
  57.4 0.7 copy-done.3
  58.1 3.3 %shard_map.104 = bf16[256,6528]{1,0:T(8,128)(2,1)} custom-call(s32[2,128]{1,0:T(2,128)S(1)} %bitcast.16, bf16[144,640]{1,0:T(8,128)(2,1)S(1)} %copy-done.1, bf16[144,640]{1,0:T(8,128)(2,1)S(1)} %collective-permute-done.refs_1_, bf16[144,640]{1,0:T(8,128)(2,1)S(1)} %collective-permute-done.1.refs_2_, bf16[144,640]{1,0:T(8,128)(2,1)S(1)} %collective-permute-done.2.refs_3_, ...), custom_call_target="tpu_custom_call" | custom-call | tf_op jit(solution)/shard_map/pallas_call | solution.py:118
  61.4 7.4 %all-to-all-start.1 = ((bf16[32,8,6528]{2,1,0:T(8,128)(2,1)}), bf16[32,8,6528]{2,1,0:T(8,128)(2,1)}, u32[]{:S(2)}, u32[]{:S(2)}) async-start(bf16[32,8,6528]{2,1,0:T(8,128)(2,1)} %bitcast.5), calls=%async_computation.1 | async-start | bytes 6684672 | tf_op jit(solution)/shard_map/all_to_all | solution.py:522
  68.8 0.0 reduce-scatter.2.cloned.1.call-start
  68.9 39.6 %all-to-all-done.1 = bf16[32,8,6528]{2,1,0:T(8,128)(2,1)} async-done(((bf16[32,8,6528]{2,1,0:T(8,128)(2,1)}), bf16[32,8,6528]{2,1,0:T(8,128)(2,1)}, u32[]{:S(2)}, u32[]{:S(2)}) %all-to-all-start.1) | async-done | bytes 3342368 | tf_op jit(solution)/shard_map/all_to_all | solution.py:522
  108.5 4.7 %all-gather.3.cloned.1.call-done = bf16[2048,1536]{1,0:T(8,128)(2,1)} async-done(((bf16[256,1536]{1,0:T(8,128)(2,1)}), bf16[2048,1536]{1,0:T(8,128)(2,1)}) %all-gather.3.cloned.1.call-update) | async-done | bytes 6291472 | tf_op jit(solution)/shard_map/all_gather | solution.py:562
  113.2 23.4 %shard_map.105 = (bf16[8,256,1280]{2,1,0:T(8,128)(2,1)}, bf16[256,7808]{1,0:T(8,128)(2,1)}) custom-call(s32[1]{0:T(128)} %bitcast.me, bf16[8,256,1536]{2,1,0:T(8,128)(2,1)} %bitcast.21, bf16[256,6528]{1,0:T(8,128)(2,1)} %bitcast.6.rows, bf16[1,7168,256]{2,1,0:T(8,128)(2,1)} %gate_hbm.1, bf16[1,7168,256]{2,1,0:T(8,128)(2,1)} %up_hbm.1, ...), custom_call_target="tpu_custom_call" | custom-call | tf_op jit(solution)/shard_map/pallas_call | solution.py:367
  136.6 0.0 reduce-scatter.2.cloned.1.call-update
  136.7 0.0 copy-start.5
  136.7 7.5 %all-to-all-start.2 = ((bf16[32,8,7808]{2,1,0:T(8,128)(2,1)}), bf16[32,8,7808]{2,1,0:T(8,128)(2,1)}, u32[]{:S(2)}, u32[]{:S(2)}) async-start(bf16[32,8,7808]{2,1,0:T(8,128)(2,1)} %bitcast.22), calls=%async_computation.3 | async-start | bytes 7995392 | tf_op jit(solution)/shard_map/all_to_all | solution.py:522
  144.2 0.7 slice.11.squares
  144.9 46.7 %all-to-all-done.2 = bf16[32,8,7808]{2,1,0:T(8,128)(2,1)} async-done(((bf16[32,8,7808]{2,1,0:T(8,128)(2,1)}), bf16[32,8,7808]{2,1,0:T(8,128)(2,1)}, u32[]{:S(2)}, u32[]{:S(2)}) %all-to-all-start.2) | async-done | bytes 3997728 | tf_op jit(solution)/shard_map/all_to_all | solution.py:522
  191.6 4.4 %shard_map.106 = (bf16[8,144,768]{2,1,0:T(8,128)(2,1)S(1)}, bf16[80,768]{1,0:T(8,128)(2,1)S(1)}, bf16[80,768]{1,0:T(8,128)(2,1)S(1)}) custom-call(bf16[16,640]{1,0:T(8,128)(2,1)S(1)} %slice.11.squares, bf16[256,7808]{1,0:T(8,128)(2,1)} %bitcast.9.back, s32[2,128]{1,0:T(2,128)S(1)} %bitcast.17, f32[2,128]{1,0:T(2,128)S(1)} %bitcast.19), custom_call_target="tpu_custom_call" | custom-call | tf_op jit(solution)/shard_map/pallas_call | solution.py:118
  196.0 0.1 collective-permute-start.8
  196.1 3.2 %collective-permute-start.9 = (bf16[80,768]{1,0:T(8,128)(2,1)S(1)}, bf16[80,768]{1,0:T(8,128)(2,1)S(1)}, u32[]{:S(2)}, u32[]{:S(2)}) collective-permute-start(bf16[80,768]{1,0:T(8,128)(2,1)S(1)} %get-tuple-element.39), channel_id=1, source_target_pairs={{0,7},{1,0},{2,1},{3,2},{4,3},{5,4},{6,5},{7,6},{8,15},{9,8},{10,9... | collective-permute-start | bytes 368648 | tf_op jit(solution)/shard_map/ppermute | solution.py:528
  199.3 3.0 %collective-permute-done.8.right = bf16[80,768]{1,0:T(8,128)(2,1)S(1)} collective-permute-done((bf16[80,768]{1,0:T(8,128)(2,1)S(1)}, bf16[80,768]{1,0:T(8,128)(2,1)S(1)}, u32[]{:S(2)}, u32[]{:S(2)}) %collective-permute-start.8) | collective-permute-done | bytes 122912 | tf_op jit(solution)/shard_map/ppermute | solution.py:528
  202.4 0.1 shard_map.107
  202.4 0.2 collective-permute-start.10
  202.6 3.1 %collective-permute-start.11 = (bf16[144,768]{1,0:T(8,128)(2,1)S(1)}, bf16[144,768]{1,0:T(8,128)(2,1)S(1)}, u32[]{:S(2)}, u32[]{:S(2)}) collective-permute-start(bf16[144,768]{1,0:T(8,128)(2,1)S(1)} %get-tuple-element.43), channel_id=1, source_target_pairs={{0,7},{1,0},{2,1},{3,2},{4,3},{5,4},{6,5},{7,6},{8,15},{9,8},{10,9... | collective-permute-start | bytes 663560 | tf_op jit(solution)/shard_map/ppermute | solution.py:528
  205.7 9.3 %all-to-all-start.3 = ((bf16[32,8,1280]{2,1,0:T(8,128)(2,1)}), bf16[32,8,1280]{2,1,0:T(8,128)(2,1)S(1)}, u32[]{:S(2)}, u32[]{:S(2)}) async-start(bf16[32,8,1280]{2,1,0:T(8,128)(2,1)} %bitcast.25), calls=%async_computation.4 | async-start | bytes 1310720 | tf_op jit(solution)/shard_map/all_to_all | solution.py:522
  215.1 0.0 copy-start
  215.1 0.0 copy-start.2
  215.1 0.1 shard_map.108
  215.2 0.1 collective-permute-start.12
  215.3 3.2 %collective-permute-start.13 = (bf16[144,768]{1,0:T(8,128)(2,1)S(1)}, bf16[144,768]{1,0:T(8,128)(2,1)S(1)}, u32[]{:S(2)}, u32[]{:S(2)}) collective-permute-start(bf16[144,768]{1,0:T(8,128)(2,1)S(1)} %get-tuple-element.45), channel_id=1, source_target_pairs={{0,7},{1,0},{2,1},{3,2},{4,3},{5,4},{6,5},{7,6},{8,15},{9,8},{10,9... | collective-permute-start | bytes 663560 | tf_op jit(solution)/shard_map/ppermute | solution.py:528
  218.6 5.5 %collective-permute-done.12.right = bf16[144,768]{1,0:T(8,128)(2,1)S(1)} collective-permute-done((bf16[144,768]{1,0:T(8,128)(2,1)S(1)}, bf16[144,768]{1,0:T(8,128)(2,1)S(1)}, u32[]{:S(2)}, u32[]{:S(2)}) %collective-permute-start.12) | collective-permute-done | bytes 221216 | tf_op jit(solution)/shard_map/ppermute | solution.py:528
  224.0 0.1 shard_map.109
  224.1 0.2 collective-permute-start.14
  224.3 3.1 %collective-permute-start.15 = (bf16[144,768]{1,0:T(8,128)(2,1)S(1)}, bf16[144,768]{1,0:T(8,128)(2,1)S(1)}, u32[]{:S(2)}, u32[]{:S(2)}) collective-permute-start(bf16[144,768]{1,0:T(8,128)(2,1)S(1)} %get-tuple-element.47), channel_id=1, source_target_pairs={{0,7},{1,0},{2,1},{3,2},{4,3},{5,4},{6,5},{7,6},{8,15},{9,8},{10,9... | collective-permute-start | bytes 663560 | tf_op jit(solution)/shard_map/ppermute | solution.py:528
  227.4 4.6 %collective-permute-done.14.right = bf16[144,768]{1,0:T(8,128)(2,1)S(1)} collective-permute-done((bf16[144,768]{1,0:T(8,128)(2,1)S(1)}, bf16[144,768]{1,0:T(8,128)(2,1)S(1)}, u32[]{:S(2)}, u32[]{:S(2)}) %collective-permute-start.14) | collective-permute-done | bytes 221216 | tf_op jit(solution)/shard_map/ppermute | solution.py:528
  232.1 1.4 shard_map.110
  (23 shorter events, 0.1 us)
Async XLA Ops:
  9.8 28.2 %all-to-all-start = ((bf16[32,8,1536]{2,1,0:T(8,128)(2,1)}), bf16[32,8,1536]{2,1,0:T(8,128)(2,1)S(1)}, u32[]{:S(2)}, u32[]{:S(2)}) async-start(bf16[32,8,1536]{2,1,0:T(8,128)(2,1)} %bitcast.24), calls=%async_computation | async-start | bytes 1572864 | tf_op jit(solution)/shard_map/all_to_all | solution.py:522
  17.4 95.8 %all-gather.3.cloned.1.call-start = ((), (), s32[]{:S(2)}) async-start(), calls=%async_computation.6 | async-start | bytes 7077888 | tf_op jit(solution)/shard_map/all_gather | solution.py:562
  17.5 10.5 %collective-permute-start.1 = (bf16[144,640]{1,0:T(8,128)(2,1)}, bf16[144,640]{1,0:T(8,128)(2,1)S(1)}, u32[]{:S(2)}, u32[]{:S(2)}) collective-permute-start(bf16[144,640]{1,0:T(8,128)(2,1)} %get-tuple-element.28.refs_0_), channel_id=1, source_target_pairs={{0,7},{1,0},{2,1},{3,2},{4,3},{5,4},{6,5},{7,6},{8,15},{9,8},{10,9... | collective-permute-start | bytes 552968 | tf_op jit(solution)/shard_map/ppermute | solution.py:528
  23.4 7.8 %collective-permute-start = (bf16[144,640]{1,0:T(8,128)(2,1)}, bf16[144,640]{1,0:T(8,128)(2,1)S(1)}, u32[]{:S(2)}, u32[]{:S(2)}) collective-permute-start(bf16[144,640]{1,0:T(8,128)(2,1)} %get-tuple-element.28.refs_0_), channel_id=1, source_target_pairs={{0,1},{1,2},{2,3},{3,4},{4,5},{5,6},{6,7},{7,0},{8,9},{9,10},{10,1... | collective-permute-start | bytes 552968 | tf_op jit(solution)/shard_map/ppermute | solution.py:528
  31.3 6.8 %collective-permute-start.2 = (bf16[144,640]{1,0:T(8,128)(2,1)S(1)}, bf16[144,640]{1,0:T(8,128)(2,1)S(1)}, u32[]{:S(2)}, u32[]{:S(2)}) collective-permute-start(bf16[144,640]{1,0:T(8,128)(2,1)S(1)} %collective-permute-done.refs_1_), channel_id=1, source_target_pairs={{0,1},{1,2},{2,3},{3,4},{4,5},{5,6},{6,7},{7,0},{8,9},{9,10},{10,1... | collective-permute-start | bytes 552968 | tf_op jit(solution)/shard_map/ppermute | solution.py:528
  31.3 6.8 %collective-permute-start.3 = (bf16[144,640]{1,0:T(8,128)(2,1)S(1)}, bf16[144,640]{1,0:T(8,128)(2,1)S(1)}, u32[]{:S(2)}, u32[]{:S(2)}) collective-permute-start(bf16[144,640]{1,0:T(8,128)(2,1)S(1)} %collective-permute-done.1.refs_2_), channel_id=1, source_target_pairs={{0,7},{1,0},{2,1},{3,2},{4,3},{5,4},{6,5},{7,6},{8,15},{9,8},{10,9... | collective-permute-start | bytes 552968 | tf_op jit(solution)/shard_map/ppermute | solution.py:528
  38.0 0.9 copy-start.6
  39.0 6.8 %collective-permute-start.4 = (bf16[144,640]{1,0:T(8,128)(2,1)S(1)}, bf16[144,640]{1,0:T(8,128)(2,1)S(1)}, u32[]{:S(2)}, u32[]{:S(2)}) collective-permute-start(bf16[144,640]{1,0:T(8,128)(2,1)S(1)} %collective-permute-done.2.refs_3_), channel_id=1, source_target_pairs={{0,1},{1,2},{2,3},{3,4},{4,5},{5,6},{6,7},{7,0},{8,9},{9,10},{10,1... | collective-permute-start | bytes 552968 | tf_op jit(solution)/shard_map/ppermute | solution.py:528
  39.1 6.7 %collective-permute-start.5 = (bf16[144,640]{1,0:T(8,128)(2,1)S(1)}, bf16[144,640]{1,0:T(8,128)(2,1)S(1)}, u32[]{:S(2)}, u32[]{:S(2)}) collective-permute-start(bf16[144,640]{1,0:T(8,128)(2,1)S(1)} %collective-permute-done.3.refs_4_), channel_id=1, source_target_pairs={{0,7},{1,0},{2,1},{3,2},{4,3},{5,4},{6,5},{7,6},{8,15},{9,8},{10,9... | collective-permute-start | bytes 552968 | tf_op jit(solution)/shard_map/ppermute | solution.py:528
  45.8 10.7 %collective-permute-start.7 = (bf16[80,640]{1,0:T(8,128)(2,1)S(1)}, bf16[80,640]{1,0:T(8,128)(2,1)S(1)}, u32[]{:S(2)}, u32[]{:S(2)}) collective-permute-start(bf16[80,640]{1,0:T(8,128)(2,1)S(1)} %slice.10), channel_id=1, source_target_pairs={{0,7},{1,0},{2,1},{3,2},{4,3},{5,4},{6,5},{7,6},{8,15},{9,8},{10,9... | collective-permute-start | bytes 307208 | tf_op jit(solution)/shard_map/ppermute | solution.py:528
  49.2 7.3 %collective-permute-start.6 = (bf16[64,640]{1,0:T(8,128)(2,1)S(1)}, bf16[64,640]{1,0:T(8,128)(2,1)S(1)}, u32[]{:S(2)}, u32[]{:S(2)}) collective-permute-start(bf16[64,640]{1,0:T(8,128)(2,1)S(1)} %slice.9), channel_id=1, source_target_pairs={{0,1},{1,2},{2,3},{3,4},{4,5},{5,6},{6,7},{7,0},{8,9},{9,10},{10,1... | collective-permute-start | bytes 245768 | tf_op jit(solution)/shard_map/ppermute | solution.py:528
  56.5 0.9 copy-start.1
  57.4 0.7 copy-start.3
  61.4 47.1 %all-to-all-start.1 = ((bf16[32,8,6528]{2,1,0:T(8,128)(2,1)}), bf16[32,8,6528]{2,1,0:T(8,128)(2,1)}, u32[]{:S(2)}, u32[]{:S(2)}) async-start(bf16[32,8,6528]{2,1,0:T(8,128)(2,1)} %bitcast.5), calls=%async_computation.1 | async-start | bytes 6684672 | tf_op jit(solution)/shard_map/all_to_all | solution.py:522
  68.8 136.9 %reduce-scatter.2.cloned.1.call-start = ((), (), s32[]{:S(2)}) async-start(), calls=%async_computation.5 | async-start | bytes 5898240 | tf_op jit(solution)/shard_map/reduce_scatter | solution.py:566
  136.6 55.0 %copy-start.4 = (s32[128,2]{0,1:T(2,128)S(1)}, s32[128,2]{0,1:T(2,128)}, u32[]{:S(2)}) copy-start(s32[128,2]{0,1:T(2,128)} %param.13) | copy-start | bytes 3076
  136.7 55.0 %copy-start.5 = (f32[128,2]{0,1:T(2,128)S(1)}, f32[128,2]{0,1:T(2,128)}, u32[]{:S(2)}) copy-start(f32[128,2]{0,1:T(2,128)} %param.14) | copy-start | bytes 3076
  136.7 55.0 %all-to-all-start.2 = ((bf16[32,8,7808]{2,1,0:T(8,128)(2,1)}), bf16[32,8,7808]{2,1,0:T(8,128)(2,1)}, u32[]{:S(2)}, u32[]{:S(2)}) async-start(bf16[32,8,7808]{2,1,0:T(8,128)(2,1)} %bitcast.22), calls=%async_computation.3 | async-start | bytes 7995392 | tf_op jit(solution)/shard_map/all_to_all | solution.py:522
  196.0 6.4 %collective-permute-start.8 = (bf16[80,768]{1,0:T(8,128)(2,1)S(1)}, bf16[80,768]{1,0:T(8,128)(2,1)S(1)}, u32[]{:S(2)}, u32[]{:S(2)}) collective-permute-start(bf16[80,768]{1,0:T(8,128)(2,1)S(1)} %get-tuple-element.38), channel_id=1, source_target_pairs={{0,1},{1,2},{2,3},{3,4},{4,5},{5,6},{6,7},{7,0},{8,9},{9,10},{10,1... | collective-permute-start | bytes 368648 | tf_op jit(solution)/shard_map/ppermute | solution.py:528
  196.1 6.3 %collective-permute-start.9 = (bf16[80,768]{1,0:T(8,128)(2,1)S(1)}, bf16[80,768]{1,0:T(8,128)(2,1)S(1)}, u32[]{:S(2)}, u32[]{:S(2)}) collective-permute-start(bf16[80,768]{1,0:T(8,128)(2,1)S(1)} %get-tuple-element.39), channel_id=1, source_target_pairs={{0,7},{1,0},{2,1},{3,2},{4,3},{5,4},{6,5},{7,6},{8,15},{9,8},{10,9... | collective-permute-start | bytes 368648 | tf_op jit(solution)/shard_map/ppermute | solution.py:528
  202.4 12.7 %collective-permute-start.10 = (bf16[144,768]{1,0:T(8,128)(2,1)S(1)}, bf16[144,768]{1,0:T(8,128)(2,1)S(1)}, u32[]{:S(2)}, u32[]{:S(2)}) collective-permute-start(bf16[144,768]{1,0:T(8,128)(2,1)S(1)} %get-tuple-element.42), channel_id=1, source_target_pairs={{0,1},{1,2},{2,3},{3,4},{4,5},{5,6},{6,7},{7,0},{8,9},{9,10},{10,1... | collective-permute-start | bytes 663560 | tf_op jit(solution)/shard_map/ppermute | solution.py:528
  202.6 12.5 %collective-permute-start.11 = (bf16[144,768]{1,0:T(8,128)(2,1)S(1)}, bf16[144,768]{1,0:T(8,128)(2,1)S(1)}, u32[]{:S(2)}, u32[]{:S(2)}) collective-permute-start(bf16[144,768]{1,0:T(8,128)(2,1)S(1)} %get-tuple-element.43), channel_id=1, source_target_pairs={{0,7},{1,0},{2,1},{3,2},{4,3},{5,4},{6,5},{7,6},{8,15},{9,8},{10,9... | collective-permute-start | bytes 663560 | tf_op jit(solution)/shard_map/ppermute | solution.py:528
  205.7 26.3 %all-to-all-start.3 = ((bf16[32,8,1280]{2,1,0:T(8,128)(2,1)}), bf16[32,8,1280]{2,1,0:T(8,128)(2,1)S(1)}, u32[]{:S(2)}, u32[]{:S(2)}) async-start(bf16[32,8,1280]{2,1,0:T(8,128)(2,1)} %bitcast.25), calls=%async_computation.4 | async-start | bytes 1310720 | tf_op jit(solution)/shard_map/all_to_all | solution.py:522
  215.1 17.0 %copy-start = (bf16[128,896]{1,0:T(8,128)(2,1)S(1)}, bf16[128,896]{1,0:T(8,128)(2,1)}, u32[]{:S(2)}) copy-start(bf16[128,896]{1,0:T(8,128)(2,1)} %tok.3) | copy-start | bytes 688132
  215.1 17.0 %copy-start.2 = (f32[896]{0:T(1024)S(1)}, f32[896]{0:T(1024)}, u32[]{:S(2)}) copy-start(f32[896]{0:T(1024)} %gain.3) | copy-start | bytes 10756
  215.2 8.8 %collective-permute-start.12 = (bf16[144,768]{1,0:T(8,128)(2,1)S(1)}, bf16[144,768]{1,0:T(8,128)(2,1)S(1)}, u32[]{:S(2)}, u32[]{:S(2)}) collective-permute-start(bf16[144,768]{1,0:T(8,128)(2,1)S(1)} %get-tuple-element.44), channel_id=1, source_target_pairs={{0,1},{1,2},{2,3},{3,4},{4,5},{5,6},{6,7},{7,0},{8,9},{9,10},{10,1... | collective-permute-start | bytes 663560 | tf_op jit(solution)/shard_map/ppermute | solution.py:528
  215.3 8.7 %collective-permute-start.13 = (bf16[144,768]{1,0:T(8,128)(2,1)S(1)}, bf16[144,768]{1,0:T(8,128)(2,1)S(1)}, u32[]{:S(2)}, u32[]{:S(2)}) collective-permute-start(bf16[144,768]{1,0:T(8,128)(2,1)S(1)} %get-tuple-element.45), channel_id=1, source_target_pairs={{0,7},{1,0},{2,1},{3,2},{4,3},{5,4},{6,5},{7,6},{8,15},{9,8},{10,9... | collective-permute-start | bytes 663560 | tf_op jit(solution)/shard_map/ppermute | solution.py:528
  224.1 7.9 %collective-permute-start.14 = (bf16[144,768]{1,0:T(8,128)(2,1)S(1)}, bf16[144,768]{1,0:T(8,128)(2,1)S(1)}, u32[]{:S(2)}, u32[]{:S(2)}) collective-permute-start(bf16[144,768]{1,0:T(8,128)(2,1)S(1)} %get-tuple-element.46), channel_id=1, source_target_pairs={{0,1},{1,2},{2,3},{3,4},{4,5},{5,6},{6,7},{7,0},{8,9},{9,10},{10,1... | collective-permute-start | bytes 663560 | tf_op jit(solution)/shard_map/ppermute | solution.py:528
  224.3 7.7 %collective-permute-start.15 = (bf16[144,768]{1,0:T(8,128)(2,1)S(1)}, bf16[144,768]{1,0:T(8,128)(2,1)S(1)}, u32[]{:S(2)}, u32[]{:S(2)}) collective-permute-start(bf16[144,768]{1,0:T(8,128)(2,1)S(1)} %get-tuple-element.47), channel_id=1, source_target_pairs={{0,7},{1,0},{2,1},{3,2},{4,3},{5,4},{6,5},{7,6},{8,15},{9,8},{10,9... | collective-permute-start | bytes 663560 | tf_op jit(solution)/shard_map/ppermute | solution.py:528
Sparse Core Ops, SparseCore 0:
  39.1 74.0 all-gather.2
  136.8 63.7 reduce-scatter.1
